TPU v7x, 32 devices: a whole 2x2x4 slice. The times are simulated.
32 devices in a mesh: batch: 16 (over z, y, x), fsdp: 2 (over core).
Axes of the slice: x: 2, y: 2, z: 4, core: 2. Of those that a mesh axis runs over, the one named last changes fastest.
Arguments:
- frames: bfloat16 [16, 1024, 1024], P('batch', 'fsdp'), may hold values from -6 to 6
- segment_ids: int32 [16, 1024], P('batch'), may hold values from 0 to 3, never falling along the last dimension, each value on 1 to 512 neighbouring positions
- valid_mask: int32 [16, 1024], P('batch'), may hold values 0 or 1
- first_norm: float32 [1024], replicated, may hold values from 0.5 to 1.5
- first_up: bfloat16 [4096, 1024], P('fsdp'), may hold values from -0.1875 to 0.1875
- first_down: bfloat16 [4096, 1024], P('fsdp'), may hold values from -0.1875 to 0.1875
- attention_norm: float32 [1024], replicated, may hold values from 0.5 to 1.5
- query_proj: bfloat16 [1024, 1024], P('fsdp'), may hold values from -0.1875 to 0.1875
- key_proj: bfloat16 [1024, 1024], P('fsdp'), may hold values from -0.1875 to 0.1875
- value_proj: bfloat16 [1024, 1024], P('fsdp'), may hold values from -0.1875 to 0.1875
- output_proj: bfloat16 [1024, 1024], P('fsdp'), may hold values from -3 to 3
- position_proj: bfloat16 [1024, 1024], P('fsdp'), may hold values from -0.1875 to 0.1875
- content_bias: float32 [1024], replicated, may hold values from -3 to 3
- position_bias: float32 [1024], replicated, may hold values from -3 to 3
- convolution_norm: float32 [1024], replicated, may hold values from 0.5 to 1.5
- pointwise_in: bfloat16 [1024, 2048], P('fsdp'), may hold values from -0.1875 to 0.1875
- depthwise: float32 [1024, 5], replicated, may hold values from -2.5 to 2.5
- batch_gain: float32 [1024], replicated, may hold values from 0.5 to 1.5
- batch_shift: float32 [1024], replicated, may hold values from -3 to 3
- pointwise_out: bfloat16 [1024, 1024], P('fsdp'), may hold values from -0.1875 to 0.1875
- second_norm: float32 [1024], replicated, may hold values from 0.5 to 1.5
- second_up: bfloat16 [4096, 1024], P('fsdp'), may hold values from -0.1875 to 0.1875
- second_down: bfloat16 [4096, 1024], P('fsdp'), may hold values from -0.1875 to 0.1875
- final_norm: float32 [1024], replicated, may hold values from 0.5 to 1.5
- cotangent: bfloat16 [16, 1024, 1024], P('batch', 'fsdp'), may hold values from -6 to 6
Outputs:
- layer_out: bfloat16 [16, 1024, 1024], P('batch', 'fsdp')
- frames_grad: bfloat16 [16, 1024, 1024], P('batch', 'fsdp')
- first_norm_grad: float32 [1024], P('fsdp')
- first_up_grad: float32 [4096, 1024], P('fsdp')
- first_down_grad: float32 [4096, 1024], P('fsdp')
- attention_norm_grad: float32 [1024], P('fsdp')
- query_proj_grad: float32 [1024, 1024], P('fsdp')
- key_proj_grad: float32 [1024, 1024], P('fsdp')
- value_proj_grad: float32 [1024, 1024], P('fsdp')
- output_proj_grad: float32 [1024, 1024], P('fsdp')
- position_proj_grad: float32 [1024, 1024], P('fsdp')
- content_bias_grad: float32 [1024], P('fsdp')
- position_bias_grad: float32 [1024], P('fsdp')
- convolution_norm_grad: float32 [1024], P('fsdp')
- pointwise_in_grad: float32 [1024, 2048], P('fsdp')
- depthwise_grad: float32 [1024, 5], P('fsdp')
- batch_gain_grad: float32 [1024], P('fsdp')
- batch_shift_grad: float32 [1024], P('fsdp')
- pointwise_out_grad: float32 [1024, 1024], P('fsdp')
- second_norm_grad: float32 [1024], P('fsdp')
- second_up_grad: float32 [4096, 1024], P('fsdp')
- second_down_grad: float32 [4096, 1024], P('fsdp')
- final_norm_grad: float32 [1024], P('fsdp')
Inputs may be any that keep to these rules, and one draw needn't show every extreme that they name: `segment_ids`: segment numbers never fall along a row; each utterance of a row has 1 to 512 frames.
All inputs are finite; a program needn't handle non-finite values. No bound on the sum of `valid_mask` on one device may be relied on, other than what follows from the above.
Results may differ from a plain program's by a relative error of at most 0.035.
Values may be sent and summed in bfloat16 or wider, within the bound.
No kernel may reach another device: no remote copies, remote signals or barrier semaphores. Data moves between devices by JAX's collectives and lax.ppermute only.
A program may use at most 384 MiB of HBM per device.

v0:
```python
import math

import jax
import jax.numpy as jnp
from jax import lax
from jax.sharding import PartitionSpec as P

D = 1024
H = 8
DH = 128
KER = 5


epsilon = 1e-05
neg_big = -1e30


def with_halo(block, sides, width):
    for axis, dim in sides:
        count = lax.axis_size(axis)
        forward = [(i, i + 1) for i in range(count - 1)]
        backward = [(target, source) for source, target in forward]
        low = lax.ppermute(
            lax.slice_in_dim(block, block.shape[dim] - width, None, axis=dim), axis, forward
        )
        high = lax.ppermute(lax.slice_in_dim(block, 0, width, axis=dim), axis, backward)
        block = jnp.concatenate([low, block, high], axis=dim)
    return block


def layer_norm(values, norm_gain):
    average = jnp.mean(values, axis=-1, keepdims=True)
    centred = values - average
    inverse_dev = lax.rsqrt(jnp.mean(centred * centred, axis=-1, keepdims=True) + epsilon)
    normed = centred * inverse_dev
    return (normed * norm_gain, normed, inverse_dev)


def norm_back(gradient, normed, inverse_dev, norm_gain):
    scaled = gradient * norm_gain
    first_mean = jnp.mean(scaled, axis=-1, keepdims=True)
    second_mean = jnp.mean(scaled * normed, axis=-1, keepdims=True)
    return (
        inverse_dev * (scaled - first_mean - normed * second_mean),
        jnp.sum(gradient * normed, axis=0),
    )


def silu_slope(values):
    opener = jax.nn.sigmoid(values)
    return opener * (1.0 + values * (1.0 - opener))


def encoding(distance, features):
    half_width = features // 2
    channel = jnp.arange(half_width).astype(jnp.float32)
    frequency = jnp.exp(channel * (-2.0 * math.log(10000.0) / features))
    angles = distance[:, None] * frequency[None, :]
    return jnp.concatenate([jnp.sin(angles), jnp.cos(angles)], axis=1)


def rel_shift(full_window, queries, keys_count):
    leading = full_window.shape[:-2]
    window = full_window.shape[-1]
    flattened = full_window.reshape(leading + (queries * window,))
    flattened = flattened[..., queries - 1 : queries - 1 + queries * (window - 1)]
    return flattened.reshape(leading + (queries, window - 1))[..., :keys_count]


def rel_unshift(gradient, queries, window):
    leading = gradient.shape[:-2]
    keys_count = gradient.shape[-1]
    widened = jnp.pad(gradient, [(0, 0)] * len(leading) + [(0, 0), (0, window - 1 - keys_count)])
    flattened = widened.reshape(leading + (queries * (window - 1),))
    flattened = jnp.pad(flattened, [(0, 0)] * len(leading) + [(queries - 1, 1)])
    return flattened.reshape(leading + (queries, window))


def on_device(
    frames,
    segment_ids,
    valid_mask,
    first_norm,
    first_up,
    first_down,
    attention_norm,
    query_proj,
    key_proj,
    value_proj,
    output_proj,
    position_proj,
    content_bias,
    position_bias,
    convolution_norm,
    pointwise_in,
    depthwise,
    batch_gain,
    batch_shift,
    pointwise_out,
    second_norm,
    second_up,
    second_down,
    final_norm,
    cotangent,
):
    groups = lax.axis_size("fsdp")
    member = lax.axis_index("fsdp")
    rows_here, shard_frames, features = frames.shape
    row_length = segment_ids.shape[1]
    tokens = rows_here * shard_frames
    window = row_length + shard_frames
    rim_width = (KER - 1) // 2
    scaling = 1.0 / math.sqrt(DH)
    frame_start = member * shard_frames
    seg_here = lax.dynamic_slice_in_dim(segment_ids, frame_start, shard_frames, 1)
    seg_padded = jnp.pad(segment_ids, ((0, 0), (rim_width, rim_width)), constant_values=-1)
    seg_rim = lax.dynamic_slice_in_dim(seg_padded, frame_start, shard_frames + 2 * rim_width, 1)
    valid_here = (
        lax.dynamic_slice_in_dim(valid_mask, frame_start, shard_frames, 1)
        .astype(jnp.float32)
        .reshape(tokens, 1)
    )
    same_utterance = (seg_here[:, :, None] == segment_ids[:, None, :])[:, None]
    distance = (frame_start + shard_frames - 1 - jnp.arange(window)).astype(jnp.float32)
    positions = encoding(distance, D).astype(jnp.bfloat16)

    def fetch_pair(first_matrix, second_matrix):
        return (
            lax.all_gather(first_matrix, "fsdp", axis=0, tiled=True),
            lax.all_gather(second_matrix, "fsdp", axis=0, tiled=True),
        )

    def fetch_attention():
        return (
            lax.all_gather(query_proj, "fsdp", axis=0, tiled=True),
            lax.all_gather(key_proj, "fsdp", axis=0, tiled=True),
            lax.all_gather(value_proj, "fsdp", axis=0, tiled=True),
            lax.all_gather(output_proj, "fsdp", axis=0, tiled=True),
            lax.all_gather(position_proj, "fsdp", axis=0, tiled=True),
        )

    def shard_rows(left_side, right_side, accuracy=None):
        return lax.psum_scatter(
            lax.dot_general(
                left_side,
                right_side,
                (((0,), (0,)), ((), ())),
                preferred_element_type=jnp.float32,
                precision=accuracy,
            ).astype(jnp.bfloat16),
            "fsdp",
            scatter_dimension=0,
            tiled=True,
        ).astype(jnp.float32)

    def add_rim(values):
        return with_halo(values.astype(jnp.bfloat16), (("fsdp", 1),), rim_width).astype(
            values.dtype
        )

    def feed_forward(source, norm_gain, up_shard, down_shard):
        normed_out, normed, inverse_dev = layer_norm(source, norm_gain)
        lowered = normed_out.astype(jnp.bfloat16)
        up_matrix, down_matrix = fetch_pair(up_shard, down_shard)
        hidden_pre = lax.dot_general(
            lowered, up_matrix, (((1,), (1,)), ((), ())), preferred_element_type=jnp.float32
        )
        hidden = jax.nn.silu(hidden_pre).astype(jnp.bfloat16)
        branch = jnp.dot(hidden, down_matrix, preferred_element_type=jnp.float32)
        return (source + 0.5 * branch, (lowered, hidden_pre, hidden, normed, inverse_dev))

    def feed_back(gradient, stored, norm_gain, up_shard, down_shard):
        inputs, hidden_pre, hidden, normed, inverse_dev = stored
        branch_grad = (0.5 * gradient).astype(jnp.bfloat16)
        up_matrix, down_matrix = fetch_pair(up_shard, down_shard)
        hidden_grad = lax.dot_general(
            branch_grad, down_matrix, (((1,), (1,)), ((), ())), preferred_element_type=jnp.float32
        )
        pre_grad = (hidden_grad * silu_slope(hidden_pre)).astype(jnp.bfloat16)
        down_grad = shard_rows(hidden, branch_grad)
        up_grad = shard_rows(pre_grad, inputs)
        normed_grad = jnp.dot(pre_grad, up_matrix, preferred_element_type=jnp.float32)
        source_grad, gain_grad = norm_back(normed_grad, normed, inverse_dev, norm_gain)
        return (gradient + source_grad, gain_grad, up_grad, down_grad)

    def score_rows(query_content, query_position, key_heads, pos_heads):
        content = jnp.einsum(
            "rihe,rjhe->rhij", query_content, key_heads, preferred_element_type=jnp.float32
        )
        full_window = jnp.einsum(
            "rihe,uhe->rhiu", query_position, pos_heads, preferred_element_type=jnp.float32
        )
        summed = content + rel_shift(full_window, shard_frames, row_length)
        return jnp.where(same_utterance, summed * scaling, neg_big)

    start_vals = frames.astype(jnp.float32).reshape(tokens, D)
    after_first, first_stored = feed_forward(start_vals, first_norm, first_up, first_down)
    normed_out, normed, inverse_dev = layer_norm(after_first, attention_norm)
    lowered = normed_out.astype(jnp.bfloat16)
    query_full, key_full, value_full, output_full, position_full = fetch_attention()
    queries = jnp.dot(lowered, query_full, preferred_element_type=jnp.float32)
    keys_here = (
        jnp.dot(lowered, key_full, preferred_element_type=jnp.float32)
        .astype(jnp.bfloat16)
        .reshape(rows_here, shard_frames, D)
    )
    values_here = (
        jnp.dot(lowered, value_full, preferred_element_type=jnp.float32)
        .astype(jnp.bfloat16)
        .reshape(rows_here, shard_frames, D)
    )
    keys_all = lax.all_gather(keys_here, "fsdp", axis=1, tiled=True)
    values_all = lax.all_gather(values_here, "fsdp", axis=1, tiled=True)
    key_heads = keys_all.reshape(rows_here, row_length, H, DH)
    value_heads = values_all.reshape(rows_here, row_length, H, DH)
    query_content = (
        (queries + content_bias).astype(jnp.bfloat16).reshape(rows_here, shard_frames, H, DH)
    )
    query_position = (
        (queries + position_bias).astype(jnp.bfloat16).reshape(rows_here, shard_frames, H, DH)
    )
    pos_heads = (
        jnp.dot(positions, position_full, preferred_element_type=jnp.float32)
        .astype(jnp.bfloat16)
        .reshape(window, H, DH)
    )
    masked = score_rows(query_content, query_position, key_heads, pos_heads)
    row_max = jnp.max(masked, axis=-1, keepdims=True)
    shifted_exp = jnp.exp(masked - row_max)
    row_total = jnp.sum(shifted_exp, axis=-1, keepdims=True)
    probabilities = (shifted_exp / row_total).astype(jnp.bfloat16)
    log_total = row_max + jnp.log(row_total)
    context = jnp.einsum(
        "rhij,rjhe->rihe", probabilities, value_heads, preferred_element_type=jnp.float32
    )
    context = context.astype(jnp.bfloat16).reshape(tokens, D)
    branch = jnp.dot(context, output_full, preferred_element_type=jnp.float32)
    stored = (
        lowered,
        normed,
        inverse_dev,
        query_content,
        query_position,
        key_heads,
        value_heads,
        pos_heads,
        log_total,
        context,
    )
    after_attention = after_first + branch
    normed_out, normed, inverse_dev = layer_norm(after_attention, convolution_norm)
    lowered = normed_out.astype(jnp.bfloat16)
    in_full, out_full = fetch_pair(pointwise_in, pointwise_out)
    gate_in = jnp.dot(lowered, in_full, preferred_element_type=jnp.float32)
    signal = gate_in[:, :D]
    opener = jax.nn.sigmoid(gate_in[:, D:])
    gated_vals = (signal * opener).reshape(rows_here, shard_frames, D)
    rimmed = add_rim(gated_vals)
    depth_out = jnp.zeros((rows_here, shard_frames, D), jnp.float32)
    for offset in range(KER):
        linked = (seg_rim[:, offset : offset + shard_frames] == seg_here).astype(jnp.float32)[
            :, :, None
        ]
        depth_out = (
            depth_out + rimmed[:, offset : offset + shard_frames] * linked * depthwise[:, offset]
        )
    depth_out = depth_out.reshape(tokens, D)
    weighted = valid_here * depth_out
    first_sum, second_sum, count_all = lax.psum(
        (jnp.sum(weighted, axis=0), jnp.sum(weighted * depth_out, axis=0), jnp.sum(valid_here)),
        ("batch", "fsdp"),
    )
    average = first_sum / count_all
    inverse_bn = lax.rsqrt(second_sum / count_all - average * average + epsilon)
    standard = (depth_out - average) * inverse_bn
    shifted = standard * batch_gain + batch_shift
    swished = jax.nn.silu(shifted).astype(jnp.bfloat16)
    branch = jnp.dot(swished, out_full, preferred_element_type=jnp.float32)
    after_conv = after_attention + branch
    after_second, second_stored = feed_forward(after_conv, second_norm, second_up, second_down)
    out_norm, final_normed, final_inverse = layer_norm(after_second, final_norm)
    layer_out = out_norm.astype(jnp.bfloat16).reshape(rows_here, shard_frames, D)
    gradient, final_gain_grad = norm_back(
        cotangent.astype(jnp.float32).reshape(tokens, D), final_normed, final_inverse, final_norm
    )
    gradient, second_gain_grad, second_up_grad, second_down_grad = feed_back(
        gradient, second_stored, second_norm, second_up, second_down
    )
    (
        lowered,
        normed,
        inverse_dev,
        signal,
        opener,
        rimmed,
        depth_out,
        average,
        inverse_bn,
        count_all,
        standard,
        shifted,
        swished,
    ) = (
        lowered,
        normed,
        inverse_dev,
        signal,
        opener,
        rimmed,
        depth_out,
        average,
        inverse_bn,
        count_all,
        standard,
        shifted,
        swished,
    )
    in_full, out_full = fetch_pair(pointwise_in, pointwise_out)
    out_grad = gradient.astype(jnp.bfloat16)
    out_w_grad = shard_rows(swished, out_grad)
    swish_grad = lax.dot_general(
        out_grad, out_full, (((1,), (1,)), ((), ())), preferred_element_type=jnp.float32
    )
    shifted_grad = swish_grad * silu_slope(shifted)
    plain_sum, cross_sum = lax.psum(
        (jnp.sum(shifted_grad, axis=0), jnp.sum(shifted_grad * standard, axis=0)), ("batch", "fsdp")
    )
    mean_grad = -inverse_bn * batch_gain * plain_sum
    var_grad = -0.5 * inverse_bn * inverse_bn * batch_gain * cross_sum
    depth_grad = (
        shifted_grad * batch_gain * inverse_bn
        + valid_here
        * (mean_grad - 2.0 * average * var_grad + 2.0 * depth_out * var_grad)
        / count_all
    )
    deep = depth_grad.reshape(rows_here, shard_frames, D)
    rim_grad = add_rim(deep)
    gated_grad = jnp.zeros((rows_here, shard_frames, D), jnp.float32)
    kernel_cols = []
    for offset in range(KER):
        linked = (seg_rim[:, offset : offset + shard_frames] == seg_here).astype(jnp.float32)[
            :, :, None
        ]
        kernel_cols.append(
            jnp.sum(deep * rimmed[:, offset : offset + shard_frames] * linked, axis=(0, 1))
        )
        mirror = KER - 1 - offset
        mirrored = (seg_rim[:, mirror : mirror + shard_frames] == seg_here).astype(jnp.float32)[
            :, :, None
        ]
        gated_grad = (
            gated_grad
            + rim_grad[:, mirror : mirror + shard_frames] * mirrored * depthwise[:, offset]
        )
    kernel_grad = jnp.stack(kernel_cols, axis=1)
    gated_grad = gated_grad.reshape(tokens, D)
    gate_grad = jnp.concatenate(
        [gated_grad * opener, gated_grad * signal * opener * (1.0 - opener)], axis=1
    ).astype(jnp.bfloat16)
    in_w_grad = shard_rows(lowered, gate_grad)
    normed_grad = lax.dot_general(
        gate_grad, in_full, (((1,), (1,)), ((), ())), preferred_element_type=jnp.float32
    )
    source_grad, gain_grad = norm_back(normed_grad, normed, inverse_dev, convolution_norm)
    gradient, conv_gain_grad, in_w_grad, out_w_grad, kernel_grad, bn_gain_sum, bn_shift_sum = (
        gradient + source_grad,
        gain_grad,
        in_w_grad,
        out_w_grad,
        kernel_grad,
        cross_sum,
        plain_sum,
    )
    (
        lowered,
        normed,
        inverse_dev,
        query_content,
        query_position,
        key_heads,
        value_heads,
        pos_heads,
        log_total,
        context,
    ) = stored
    query_full, key_full, value_full, output_full, position_full = fetch_attention()
    out_grad = gradient.astype(jnp.bfloat16)
    output_grad = shard_rows(context, out_grad)
    context_grad = lax.dot_general(
        out_grad, output_full, (((1,), (1,)), ((), ())), preferred_element_type=jnp.float32
    )
    context_grad = context_grad.astype(jnp.bfloat16).reshape(rows_here, shard_frames, H, DH)
    masked = score_rows(query_content, query_position, key_heads, pos_heads)
    probabilities = jnp.exp(masked - log_total)
    prob_grad = jnp.einsum(
        "rihe,rjhe->rhij", context_grad, value_heads, preferred_element_type=jnp.float32
    )
    value_part = jnp.einsum(
        "rhij,rihe->rjhe",
        probabilities.astype(jnp.bfloat16),
        context_grad,
        preferred_element_type=jnp.float32,
    )
    inner = jnp.sum(probabilities * prob_grad, axis=-1, keepdims=True)
    score_grad = jnp.where(
        same_utterance, probabilities * (prob_grad - inner) * scaling, 0.0
    ).astype(jnp.bfloat16)
    content_grad = jnp.einsum(
        "rhij,rjhe->rihe", score_grad, key_heads, preferred_element_type=jnp.float32
    )
    key_part = jnp.einsum(
        "rhij,rihe->rjhe", score_grad, query_content, preferred_element_type=jnp.float32
    )
    key_grad = lax.psum_scatter(
        key_part.reshape(rows_here, row_length, D).astype(jnp.bfloat16),
        "fsdp",
        scatter_dimension=1,
        tiled=True,
    ).astype(jnp.float32)
    value_grad = lax.psum_scatter(
        value_part.reshape(rows_here, row_length, D).astype(jnp.bfloat16),
        "fsdp",
        scatter_dimension=1,
        tiled=True,
    ).astype(jnp.float32)
    window_grad = rel_unshift(score_grad, shard_frames, window)
    position_part = jnp.einsum(
        "rhiu,uhe->rihe", window_grad, pos_heads, preferred_element_type=jnp.float32
    )
    pos_grad = jnp.einsum(
        "rhiu,rihe->uhe", window_grad, query_position, preferred_element_type=jnp.float32
    ).reshape(window, D)
    content_flat = content_grad.reshape(tokens, D)
    position_flat = position_part.reshape(tokens, D)
    query_grad = (content_flat + position_flat).astype(jnp.bfloat16)
    key_low = key_grad.reshape(tokens, D).astype(jnp.bfloat16)
    value_low = value_grad.reshape(tokens, D).astype(jnp.bfloat16)
    query_w_grad = shard_rows(lowered, query_grad)
    key_w_grad = shard_rows(lowered, key_low)
    value_w_grad = shard_rows(lowered, value_low)
    position_w_grad = shard_rows(positions.astype(jnp.float32), pos_grad, lax.Precision.HIGHEST)
    dims = (((1,), (1,)), ((), ()))
    normed_grad = lax.dot_general(query_grad, query_full, dims, preferred_element_type=jnp.float32)
    normed_grad = normed_grad + lax.dot_general(
        key_low, key_full, dims, preferred_element_type=jnp.float32
    )
    normed_grad = normed_grad + lax.dot_general(
        value_low, value_full, dims, preferred_element_type=jnp.float32
    )
    source_grad, gain_grad = norm_back(normed_grad, normed, inverse_dev, attention_norm)
    matrices = (query_w_grad, key_w_grad, value_w_grad, output_grad, position_w_grad)
    gradient, attention_gain_grad, content_grad, position_grad, matrices = (
        gradient + source_grad,
        gain_grad,
        jnp.sum(content_flat, axis=0),
        jnp.sum(position_flat, axis=0),
        matrices,
    )
    query_w_grad, key_w_grad, value_w_grad, output_grad, position_w_grad = matrices
    gradient, first_gain_grad, first_up_grad, first_down_grad = feed_back(
        gradient, first_stored, first_norm, first_up, first_down
    )
    (
        first_up_grad,
        first_down_grad,
        query_w_grad,
        key_w_grad,
        value_w_grad,
        output_grad,
        position_w_grad,
        in_w_grad,
        out_w_grad,
        second_up_grad,
        second_down_grad,
    ) = (
        lax.psum(first_up_grad.astype(jnp.bfloat16), "batch").astype(jnp.float32),
        lax.psum(first_down_grad.astype(jnp.bfloat16), "batch").astype(jnp.float32),
        lax.psum(query_w_grad.astype(jnp.bfloat16), "batch").astype(jnp.float32),
        lax.psum(key_w_grad.astype(jnp.bfloat16), "batch").astype(jnp.float32),
        lax.psum(value_w_grad.astype(jnp.bfloat16), "batch").astype(jnp.float32),
        lax.psum(output_grad.astype(jnp.bfloat16), "batch").astype(jnp.float32),
        lax.psum(position_w_grad.astype(jnp.bfloat16), "batch").astype(jnp.float32),
        lax.psum(in_w_grad.astype(jnp.bfloat16), "batch").astype(jnp.float32),
        lax.psum(out_w_grad.astype(jnp.bfloat16), "batch").astype(jnp.float32),
        lax.psum(second_up_grad.astype(jnp.bfloat16), "batch").astype(jnp.float32),
        lax.psum(second_down_grad.astype(jnp.bfloat16), "batch").astype(jnp.float32),
    )
    (
        first_gain_grad,
        attention_gain_grad,
        content_grad,
        position_grad,
        conv_gain_grad,
        kernel_grad,
        second_gain_grad,
        final_gain_grad,
    ) = lax.psum(
        (
            first_gain_grad,
            attention_gain_grad,
            content_grad,
            position_grad,
            conv_gain_grad,
            kernel_grad,
            second_gain_grad,
            final_gain_grad,
        ),
        ("batch", "fsdp"),
    )
    part_size = D // groups

    def own_part(values):
        return lax.dynamic_slice_in_dim(values, member * part_size, part_size, 0)

    frames_grad = gradient.astype(jnp.bfloat16).reshape(rows_here, shard_frames, D)
    return (
        layer_out,
        frames_grad,
        own_part(first_gain_grad),
        first_up_grad,
        first_down_grad,
        own_part(attention_gain_grad),
        query_w_grad,
        key_w_grad,
        value_w_grad,
        output_grad,
        position_w_grad,
        own_part(content_grad),
        own_part(position_grad),
        own_part(conv_gain_grad),
        in_w_grad,
        own_part(kernel_grad),
        own_part(bn_gain_sum),
        own_part(bn_shift_sum),
        out_w_grad,
        own_part(second_gain_grad),
        second_up_grad,
        second_down_grad,
        own_part(final_gain_grad),
    )


def solution(mesh):
    return jax.shard_map(
        on_device,
        mesh=mesh,
        in_specs=(
            P("batch", "fsdp", None),
            P("batch", None),
            P("batch", None),
            P(),
            P("fsdp", None),
            P("fsdp", None),
            P(),
            P("fsdp", None),
            P("fsdp", None),
            P("fsdp", None),
            P("fsdp", None),
            P("fsdp", None),
            P(),
            P(),
            P(),
            P("fsdp", None),
            P(),
            P(),
            P(),
            P("fsdp", None),
            P(),
            P("fsdp", None),
            P("fsdp", None),
            P(),
            P("batch", "fsdp", None),
        ),
        out_specs=(
            P("batch", "fsdp", None),
            P("batch", "fsdp", None),
            P("fsdp"),
            P("fsdp", None),
            P("fsdp", None),
            P("fsdp"),
            P("fsdp", None),
            P("fsdp", None),
            P("fsdp", None),
            P("fsdp", None),
            P("fsdp", None),
            P("fsdp"),
            P("fsdp"),
            P("fsdp"),
            P("fsdp", None),
            P("fsdp", None),
            P("fsdp"),
            P("fsdp"),
            P("fsdp", None),
            P("fsdp"),
            P("fsdp", None),
            P("fsdp", None),
            P("fsdp"),
        ),
        check_vma=False,
    )
```

profile of v0, /device:TPU:0, one launch (start us, length us, event | category | flops | bytes accessed | tf_op | source)
XLA Modules:
  0.0 1518.8 jit_solution(443370348629748152)
XLA Ops:
  11.9 20.3 %all-gather.16.cloned.1.call-done = bf16[4096,1024]{1,0:T(8,128)(2,1)} async-done(((bf16[2048,1024]{1,0:T(8,128)(2,1)}), bf16[4096,1024]{1,0:T(8,128)(2,1)}) %all-gather.16.cloned.1.call-update) | async-done | bytes 8388624 | tf_op jit(solution)/shard_map/all_gather | solution.py:129
  32.2 10.5 fusion.122
  42.6 12.1 all-gather.18.cloned.1.call-done
  54.8 9.6 fusion.135
  68.1 3.8 convolution_convert_fusion.12
  72.0 9.3 all-gather.20.cloned.1.call-done
  81.3 3.8 convolution_convert_fusion.13
  88.9 13.0 fusion.24
  103.3 8.2 convolution_convert_fusion.5
  111.5 4.2 add_convert_fusion.1
  117.2 12.8 convolution_bitcast_fusion
  130.0 25.7 %copy.63 = f32[1,8,512,1536]{3,2,1,0:T(8,128)} copy(f32[1,8,512,1536]{2,3,1,0:T(8,128)} %convolution_bitcast_fusion) | data formatting | bytes 50331648 | tf_op jit(solution)/shard_map/rihe,uhe->rhiu/transpose | solution.py:190
  155.7 24.1 %reshape.533 = f32[1,8,786432]{2,1,0:T(8,128)} reshape(f32[1,8,512,1536]{3,2,1,0:T(8,128)} %copy.63) | data formatting | bytes 50331648 | tf_op jit(solution)/shard_map/reshape | solution.py:65
  179.8 20.4 %slice.134 = f32[1,8,785920]{2,1,0:T(8,128)} slice(f32[1,8,786432]{2,1,0:T(8,128)} %reshape.533), slice={[0:1], [0:8], [511:786431]} | slice | bytes 50298880 | tf_op jit(solution)/shard_map/slice | solution.py:66
  200.1 21.7 %reshape.561 = f32[6287360]{0:T(1024)} reshape(f32[1,8,785920]{2,1,0:T(8,128)} %slice.134) | data formatting | bytes 50298880
  221.8 39.1 %reshape.534 = f32[1,8,512,1535]{3,2,1,0:T(8,128)} reshape(f32[6287360]{0:T(1024)} %reshape.561) | data formatting | bytes 50298880 | tf_op jit(solution)/shard_map/reshape | solution.py:67
  262.5 4.3 copy.73
  266.8 12.0 fusion.136
  278.8 7.7 fusion.6
  286.5 8.5 fusion.92
  300.0 5.3 fusion.124
  316.0 40.8 %all-reduce.5 = (f32[1024]{0:T(1024)S(1)}, f32[]{:T(128)}, f32[1024]{0:T(1024)S(1)}) all-reduce(f32[1024]{0:T(1024)S(1)} %get-tuple-element.43, f32[]{:T(128)} %get-tuple-element.74, f32[1024]{0:T(1024)S(1)} %get-tuple-element.42), channel_id=1, replica_groups=mesh['batch'=16,'fsdp'=2] {'batch','fsdp'}, use_global_device_ids=true, to_apply=%region_13.14 | all-reduce | flops 2049 | bytes 16392 | tf_op jit(solution)/shard_map/psum | solution.py:269
  357.6 4.4 fusion.138
  363.7 12.0 fusion.125
  375.8 11.0 fusion.139
  390.2 12.4 multiply_convert_fusion.1
  402.6 9.4 multiply_reduce_fusion.1
  414.5 3.4 fusion.128
  417.9 40.4 %all-reduce.4 = (f32[1024]{0:T(1024)S(1)}, f32[1024]{0:T(1024)S(1)}) all-reduce(f32[1024]{0:T(1024)S(1)} %get-tuple-element.45, f32[1024]{0:T(1024)S(1)} %get-tuple-element.44), channel_id=1, replica_groups=mesh['batch'=16,'fsdp'=2] {'batch','fsdp'}, use_global_device_ids=true, to_apply=%region_25.26 | all-reduce | flops 2048 | bytes 16384 | tf_op jit(solution)/shard_map/psum | solution.py:325
  458.9 5.8 fusion.75
  483.4 12.1 fusion.5
  495.5 12.1 fusion.4
  511.7 9.3 fusion.87
  522.8 4.4 convolution_convert_fusion.6
  527.3 9.5 pad.13
  536.8 22.7 %reshape.563 = bf16[6287360]{0:T(1024)(128)(2,1)} reshape(bf16[1,8,512,1535]{3,2,1,0:T(8,128)(2,1)} %pad.13) | data formatting | bytes 25149440
  559.5 22.7 %reshape.544 = bf16[1,8,785920]{2,1,0:T(8,128)(2,1)} reshape(bf16[6287360]{0:T(1024)(128)(2,1)} %reshape.563) | data formatting | bytes 25149440 | tf_op jit(solution)/shard_map/reshape | solution.py:74
  582.2 11.8 pad.14
  594.1 7.8 fusion.19
  601.8 13.5 bitcast_reduce_fusion
  615.3 4.2 convolution_convert_fusion.10
  621.1 3.9 convolution_convert_fusion.7
  626.4 12.4 fusion.8
  638.9 13.2 fusion.83
  653.3 3.8 convolution_convert_fusion.9
  657.4 3.9 convolution_convert_fusion.8
  663.0 6.1 convolution_convert_fusion.4
  670.7 9.8 convolution_convert_fusion.1
  682.2 12.1 convolution_convert_fusion
  694.5 3.4 fusion.140
  705.7 8.4 multiply_convert_fusion
  716.3 7.6 convolution_convert_fusion.3
  724.4 11.1 convolution_convert_fusion.2
  735.8 10.7 reduce-scatter.38.cloned.1.call-done
  746.5 21.1 %reduce-scatter.18.cloned.1.call-done = bf16[2048,1024]{1,0:T(8,128)(2,1)} async-done(((bf16[4096,1024]{1,0:T(8,128)(2,1)}), bf16[2048,1024]{1,0:T(8,128)(2,1)}) %reduce-scatter.18.cloned.1.call-update) | async-done | bytes 4194320 | tf_op jit(solution)/shard_map/reduce_scatter | solution.py:143
  767.6 20.8 %reduce-scatter.20.cloned.1.call-done = bf16[2048,1024]{1,0:T(8,128)(2,1)} async-done(((bf16[4096,1024]{1,0:T(8,128)(2,1)}), bf16[2048,1024]{1,0:T(8,128)(2,1)}) %reduce-scatter.20.cloned.1.call-update) | async-done | bytes 4194320 | tf_op jit(solution)/shard_map/reduce_scatter | solution.py:143
  790.5 10.8 fusion.43
  801.3 45.0 %all-reduce.3 = (f32[1024]{0:T(1024)S(1)}, f32[1024]{0:T(1024)S(1)}, f32[1024]{0:T(1024)S(1)}, f32[1024]{0:T(1024)S(1)}, f32[1024]{0:T(1024)S(1)}, /*index=5*/f3...) all-reduce(f32[1024]{0:T(1024)S(1)} %get-tuple-element.36, ...), channel_id=1, replica_groups=mesh['batch'=16,'fsdp'=2] {'batch','fsdp'}, use_global_device_ids=true, to_apply=%region_36.37 | all-reduce | flops 12288 | bytes 98304 | tf_op jit(solution)/shard_map/psum | solution.py:497
  851.5 3.3 fusion.100
  854.8 623.9 %all-reduce.9.cloned.1.call-done = (bf16[2048,1024]{1,0:T(8,128)(2,1)}, bf16[2048,1024]{1,0:T(8,128)(2,1)}, bf16[512,1024]{1,0:T(8,128)(2,1)}, bf16[512,1024]{1,...) async-done(((bf16[2048,1024]{1,0:T(8,128)(2,1)}, ...) | async-done | bytes 25165840 | tf_op jit(solution)/shard_map/psum | solution.py:476
  1478.7 6.8 convert_element_type.352
  1485.5 4.4 convert_element_type.354
  1502.9 4.4 convert_element_type.370
  1507.4 4.4 convert_element_type.372
  (342 shorter events, 105.5 us)
Async XLA Ops:
  7.2 25.0 %all-gather.16.cloned.1.call-start = ((), (), s32[]{:S(2)}) async-start(), calls=%async_computation.13 | async-start | bytes 12582912 | tf_op jit(solution)/shard_map/all_gather | solution.py:129
  7.9 46.8 %all-gather.18.cloned.1.call-start = ((), (), s32[]{:S(2)}) async-start(), calls=%async_computation.14 | async-start | bytes 12582912 | tf_op jit(solution)/shard_map/all_gather | solution.py:130
  8.7 59.4 %all-gather.24.cloned.1.call-start = ((), (), s32[]{:S(2)}) async-start(), calls=%async_computation.17 | async-start | bytes 3145728 | tf_op jit(solution)/shard_map/all_gather | solution.py:136
  9.4 71.8 %all-gather.20.cloned.1.call-start = ((), (), s32[]{:S(2)}) async-start(), calls=%async_computation.15 | async-start | bytes 3145728 | tf_op jit(solution)/shard_map/all_gather | solution.py:137
  10.0 22.2 %copy-start.77 = (f32[1024]{0:T(1024)S(1)}, f32[1024]{0:T(1024)}, u32[]{:S(2)}) copy-start(f32[1024]{0:T(1024)} %param.28) | copy-start | bytes 12292
  10.0 93.3 %all-gather.26.cloned.1.call-start = ((), (), s32[]{:S(2)}) async-start(), calls=%async_computation.18 | async-start | bytes 3145728 | tf_op jit(solution)/shard_map/all_gather | solution.py:139
  10.6 100.9 %all-gather.22.cloned.1.call-start = ((), (), s32[]{:S(2)}) async-start(), calls=%async_computation.16 | async-start | bytes 3145728 | tf_op jit(solution)/shard_map/all_gather | solution.py:135
  11.2 251.3 %all-gather.40.cloned.1.call-start = ((), (), s32[]{:S(2)}) async-start(), calls=%async_computation.38 | async-start | bytes 3145728 | tf_op jit(solution)/shard_map/all_gather | solution.py:212
  11.4 31.2 %copy-start.56 = (f32[512]{0:T(512)}, f32[512]{0:T(512)S(1)}, u32[]{:S(2)}) copy-start(f32[512]{0:T(512)S(1)} %broadcast_multiply_fusion.14) | copy-start | bytes 6148
  11.9 30.7 %copy-start.71 = (f32[512]{0:T(512)}, f32[512]{0:T(512)S(1)}, u32[]{:S(2)}) copy-start(f32[512]{0:T(512)S(1)} %add_rsqrt_fusion.5) | copy-start | bytes 6148
  64.4 230.6 %copy-start.1 = (f32[512,1024]{1,0:T(8,128)}, f32[512,1024]{1,0:T(8,128)S(1)}, u32[]{:S(2)}) copy-start(f32[512,1024]{1,0:T(8,128)S(1)} %get-tuple-element.106) | copy-start | bytes 6291460
  66.1 45.4 %copy-start.38 = (bf16[512,1024]{1,0:T(8,128)(2,1)}, bf16[512,1024]{1,0:T(8,128)(2,1)S(1)}, u32[]{:S(2)}) copy-start(bf16[512,1024]{1,0:T(8,128)(2,1)S(1)} %multiply_convert_fusion.13) | copy-start | bytes 3145732
  71.9 214.5 %all-gather.38.cloned.1.call-start = ((), (), s32[]{:S(2)}) async-start(), calls=%async_computation.37 | async-start | bytes 3145728 | tf_op jit(solution)/shard_map/all_gather | solution.py:213
  85.1 209.9 %all-gather.28.cloned.1.call-start = ((), (), s32[]{:S(2)}) async-start(), calls=%async_computation.19 | async-start | bytes 3145728 | tf_op jit(solution)/shard_map/all_gather | solution.py:138
  85.8 214.2 %all-gather.30.cloned.1.call-start = ((), (), s32[]{:S(2)}) async-start(), calls=%async_computation.20 | async-start | bytes 6291456 | tf_op jit(solution)/shard_map/all_gather | solution.py:129
  86.4 271.1 %all-gather.32.cloned.1.call-start = ((), (), s32[]{:S(2)}) async-start(), calls=%async_computation.21 | async-start | bytes 3145728 | tf_op jit(solution)/shard_map/all_gather | solution.py:130
  87.2 276.5 %all-gather.34.cloned.1.call-start = ((), (), s32[]{:S(2)}) async-start(), calls=%async_computation.22 | async-start | bytes 12582912 | tf_op jit(solution)/shard_map/all_gather | solution.py:129
  87.8 288.0 %all-gather.36.cloned.1.call-start = ((), (), s32[]{:S(2)}) async-start(), calls=%async_computation.23 | async-start | bytes 12582912 | tf_op jit(solution)/shard_map/all_gather | solution.py:130
  88.5 13.4 copy-start.51
  88.5 563.7 %reduce-scatter.14.cloned.1.call-start = ((), (), s32[]{:S(2)}) async-start(), calls=%async_computation.24 | async-start | bytes 3145728 | tf_op jit(solution)/shard_map/reduce_scatter | solution.py:414
  103.3 8.2 copy-start.85
  103.3 8.2 copy-start.86
  117.2 12.8 copy-start.8
  305.3 6.4 copy-start.79
  307.3 5.0 collective-permute-start.1
  308.6 3.8 collective-permute-start
  312.8 44.8 %copy-start.60 = (f32[1024]{0:T(1024)S(1)}, f32[1024]{0:T(1024)}, u32[]{:S(2)}) copy-start(f32[1024]{0:T(1024)} %param.42) | copy-start | bytes 12292
  312.8 44.8 %copy-start.87 = (f32[1024]{0:T(1024)S(1)}, f32[1024]{0:T(1024)}, u32[]{:S(2)}) copy-start(f32[1024]{0:T(1024)} %param.43) | copy-start | bytes 12292
  386.7 25.3 %copy-start.6 = (f32[512,1024]{1,0:T(8,128)}, f32[512,1024]{1,0:T(8,128)S(1)}, u32[]{:S(2)}) copy-start(f32[512,1024]{1,0:T(8,128)S(1)} %get-tuple-element.114) | copy-start | bytes 6291460
  390.2 12.4 copy-start.26
  402.6 9.4 copy-start.27
  458.3 6.5 copy-start.67
  458.3 6.5 copy-start.69
  458.9 11.3 copy-start.4
  464.8 4.4 collective-permute-start.3
  466.1 3.8 collective-permute-start.2
  483.4 12.1 copy-start.29
  495.5 12.1 copy-start.11
  511.7 145.7 %reduce-scatter.16.cloned.1.call-start = ((), (), s32[]{:S(2)}) async-start(), calls=%async_computation.25 | async-start | bytes 3145728 | tf_op jit(solution)/shard_map/reduce_scatter | solution.py:420
  521.1 214.4 %reduce-scatter.34.cloned.1.call-start = ((), (), s32[]{:S(2)}) async-start(), calls=%async_computation.34 | async-start | bytes 3145728 | tf_op jit(solution)/shard_map/reduce_scatter | solution.py:143
  527.2 208.4 %reduce-scatter.22.cloned.1.call-start = ((), (), s32[]{:S(2)}) async-start(), calls=%async_computation.28 | async-start | bytes 3145728 | tf_op jit(solution)/shard_map/reduce_scatter | solution.py:143
  582.2 11.8 copy-start.5
  594.1 7.8 copy-start.12
  619.5 116.1 %reduce-scatter.28.cloned.1.call-start = ((), (), s32[]{:S(2)}) async-start(), calls=%async_computation.31 | async-start | bytes 3145728 | tf_op jit(solution)/shard_map/reduce_scatter | solution.py:143
  625.0 110.7 %reduce-scatter.30.cloned.1.call-start = ((), (), s32[]{:S(2)}) async-start(), calls=%async_computation.32 | async-start | bytes 3145728 | tf_op jit(solution)/shard_map/reduce_scatter | solution.py:143
  626.4 12.5 copy-start.36
  626.4 12.5 copy-start.37
  652.1 83.6 %reduce-scatter.24.cloned.1.call-start = ((), (), s32[]{:S(2)}) async-start(), calls=%async_computation.29 | async-start | bytes 3145728 | tf_op jit(solution)/shard_map/reduce_scatter | solution.py:143
  657.2 78.5 %reduce-scatter.26.cloned.1.call-start = ((), (), s32[]{:S(2)}) async-start(), calls=%async_computation.30 | async-start | bytes 3145728 | tf_op jit(solution)/shard_map/reduce_scatter | solution.py:143
  661.4 74.4 %reduce-scatter.32.cloned.1.call-start = ((), (), s32[]{:S(2)}) async-start(), calls=%async_computation.33 | async-start | bytes 6291456 | tf_op jit(solution)/shard_map/reduce_scatter | solution.py:143
  669.2 66.6 %reduce-scatter.36.cloned.1.call-start = ((), (), s32[]{:S(2)}) async-start(), calls=%async_computation.35 | async-start | bytes 12582912 | tf_op jit(solution)/shard_map/reduce_scatter | solution.py:143
  680.6 65.9 %reduce-scatter.38.cloned.1.call-start = ((), (), s32[]{:S(2)}) async-start(), calls=%async_computation.36 | async-start | bytes 12582912 | tf_op jit(solution)/shard_map/reduce_scatter | solution.py:143
  694.3 73.3 %reduce-scatter.18.cloned.1.call-start = ((), (), s32[]{:S(2)}) async-start(), calls=%async_computation.26 | async-start | bytes 12582912 | tf_op jit(solution)/shard_map/reduce_scatter | solution.py:143
  698.0 6.9 slice-start
  705.7 10.6 copy-start.14
  705.7 10.6 copy-start.57
  705.7 10.6 copy-start.72
  705.7 10.6 copy-start.78
  723.9 64.5 %reduce-scatter.20.cloned.1.call-start = ((), (), s32[]{:S(2)}) async-start(), calls=%async_computation.27 | async-start | bytes 12582912 | tf_op jit(solution)/shard_map/reduce_scatter | solution.py:143
  735.5 743.2 %all-reduce.9.cloned.1.call-start = ((), (), s32[]{:S(2)}) async-start(), calls=%async_computation.39 | async-start | bytes 50331648 | tf_op jit(solution)/shard_map/psum | solution.py:476
  790.5 10.8 copy-start.59
  790.5 10.8 copy-start.75
  790.5 10.8 copy-start.76
  1478.7 6.8 copy-start.32
  (59 other events, 139.8 us)
Sparse Core Ops, SparseCore 0:
  9.6 22.5 all-gather.15
  33.7 21.0 all-gather.17
  56.3 11.7 all-gather.23
  69.5 11.7 all-gather.19
  82.7 11.7 all-gather.25
  95.8 11.7 all-gather.21
  109.8 11.7 all-gather.39
  123.7 11.7 all-gather.37
  137.0 11.7 all-gather.27
  150.2 14.8 all-gather.29
  166.6 11.7 all-gather.31
  179.8 21.0 all-gather.33
  202.4 21.0 all-gather.35
  511.8 10.2 reduce-scatter.13
  524.3 10.7 reduce-scatter.15
  537.2 10.7 reduce-scatter.33
  619.6 9.9 reduce-scatter.21
  631.8 10.7 reduce-scatter.27
  652.2 10.1 reduce-scatter.29
  665.1 10.7 reduce-scatter.23
  678.8 10.7 reduce-scatter.25
  691.9 13.2 reduce-scatter.31
  708.2 18.0 reduce-scatter.35
  728.4 18.0 reduce-scatter.37
  749.5 18.0 reduce-scatter.17
  770.3 18.0 reduce-scatter.19
  795.8 682.8 all-reduce.8
where the time goes:
time: 1530 us; the launch traced here: 1520 us
  waiting for transfers between devices  728 us (48%)
  matrix products  304 us (20%)
  local copies, waits for them, and re-layouts  241 us (16%)
  blocking collectives  126 us (8%)
  other arithmetic  92.5 us (6%)
  between operations  15.8 us (1%)
    psum x1, waiting for transfers between devices, on_device(): lax.psum(first_up_grad.astype(jnp.bfloat16), 'batch').astype(jnp.float32)  624 us
    dot_general x11, matrix products, shard_rows(): lax.dot_general(left_side, right_side, (((0,), (0,)), ((), ())), preferre...  80.1 us
    unnamed x186, local copies, waits for them, and re-layouts  73.8 us
    reduce_scatter x11, waiting for transfers between devices, shard_rows(): lax.psum_scatter(lax.dot_general(left_side, right_side, (((0,), (0,)), ((...  52.8 us
    psum x1, blocking collectives, on_device(): lax.psum((first_gain_grad, attention_gain_grad, content_grad, position_gr...  45 us
    psum x1, blocking collectives, on_device(): lax.psum((jnp.sum(weighted, axis=0), jnp.sum(weighted * depth_out, axis=0...  40.8 us
    psum x1, blocking collectives, on_device(): lax.psum((jnp.sum(shifted_grad, axis=0), jnp.sum(shifted_grad * standard,...  40.4 us
    reshape x1, local copies, waits for them, and re-layouts, rel_shift(): return flattened.reshape(leading + (queries, window - 1))[..., :keys_count]  39.1 us
  transfers between devices with their start and end apart: 31, of which 10 were waited for; matrix products, arithmetic and copies ran while one was open for 32% of the time, Pallas kernels for 0%

commit v1 on v0

v1 whole, which is shorter than its diff:
```python
import functools
import math

import jax
import jax.numpy as jnp
from jax import lax
from jax.experimental import pallas as pl
from jax.experimental.pallas import tpu as pltpu
from jax.sharding import PartitionSpec as P

H = 8
DH = 128
KER = 5
RIM = (KER - 1) // 2
EPS = 1e-05
NEG = -1e30
BF = jnp.bfloat16
F32 = jnp.float32
VMEM = 56 * 1024 * 1024


def dot(a, b, da=1, db=0):
    return lax.dot_general(a, b, (((da,), (db,)), ((), ())), preferred_element_type=F32)


def norm_parts(v):
    centred = v - jnp.mean(v, axis=-1, keepdims=True)
    rstd = lax.rsqrt(jnp.mean(centred * centred, axis=-1, keepdims=True) + EPS)
    return centred * rstd, rstd


def norm_back(grad, hat, rstd, gain):
    scaled = grad * gain
    first = jnp.mean(scaled, axis=-1, keepdims=True)
    second = jnp.mean(scaled * hat, axis=-1, keepdims=True)
    return rstd * (scaled - first - hat * second)


def slope(v):
    s = jax.nn.sigmoid(v)
    return s * (1.0 + v * (1.0 - s))


def shifted(v, s):
    g = lax.axis_size("fsdp")
    return lax.ppermute(v, "fsdp", [(i, (i + s) % g) for i in range(g)])


def natural(blocks):
    g = len(blocks)
    me = lax.axis_index("fsdp")
    if g == 1:
        return blocks[0][None]
    if g == 2:
        a, b = blocks
        return jnp.where(me == 0, jnp.stack([a, b]), jnp.stack([b, a]))
    stacked = jnp.stack(blocks[::-1])
    return jnp.roll(stacked, me + 1, axis=0)


def gather_rows(v):
    g = lax.axis_size("fsdp")
    out = natural([v] + [shifted(v, s) for s in range(1, g)])
    return out.reshape((g * v.shape[0],) + v.shape[1:])


def pair_sum(v):
    g = lax.axis_size("fsdp")
    total = v.astype(F32)
    for s in range(1, g):
        total = total + shifted(v, s).astype(F32)
    return total


def pair_scatter(v):
    g = lax.axis_size("fsdp")
    me = lax.axis_index("fsdp")
    n = v.shape[0] // g
    total = lax.dynamic_slice_in_dim(v, me * n, n, 0).astype(F32)
    for s in range(1, g):
        other = lax.dynamic_slice_in_dim(v, lax.rem(me + s, g) * n, n, 0)
        total = total + shifted(other, s).astype(F32)
    return total


def row_blocks_swap(v):
    g = lax.axis_size("fsdp")
    me = lax.axis_index("fsdp")
    n = v.shape[0] // g
    blocks = [lax.dynamic_slice_in_dim(v, me * n, n, 0)]
    for s in range(1, g):
        blocks.append(shifted(lax.dynamic_slice_in_dim(v, lax.rem(me + s, g) * n, n, 0), s))
    return natural(blocks)


def own_columns(matrices):
    g = lax.axis_size("fsdp")
    me = lax.axis_index("fsdp")

    def columns(member):
        parts = []
        for m, width in matrices:
            parts.append(lax.dynamic_slice_in_dim(m, member * width, width, 1))
        return jnp.concatenate(parts, axis=1)

    blocks = [columns(me)]
    for s in range(1, g):
        blocks.append(shifted(columns(lax.rem(me + s, g)), s))
    out = natural(blocks)
    return out.reshape((-1, out.shape[-1]))


def bit_of(b):
    return (lax.axis_index("batch") >> b) & 1


def exchange(v, b):
    n = lax.axis_size("batch")
    return lax.ppermute(v, "batch", [(i, i ^ (1 << b)) for i in range(n)])


def is_power(n):
    return n & (n - 1) == 0


def row_sum(v):
    n = lax.axis_size("batch")
    if not is_power(n):
        return lax.psum(v, "batch")
    for b in range(n.bit_length() - 1):
        v = v + exchange(v, b)
    return v


def orders():
    bits = lax.axis_size("batch").bit_length() - 1
    if bits == 4:
        return ([0, 2, 1, 3], [1, 2, 0, 3])
    rest = list(range(bits))
    return (rest, rest[1:] + rest[:1])


def add16(a, b):
    return (a.astype(F32) + b.astype(F32)).astype(BF)


def all_sum(v, order):
    for b in order[:-1]:
        half = v.shape[0] // 2
        mine = bit_of(b)
        send = lax.dynamic_slice_in_dim(v, (1 - mine) * half, half, 0)
        keep = lax.dynamic_slice_in_dim(v, mine * half, half, 0)
        v = add16(keep, exchange(send, b))
    for b in order[-1:]:
        v = add16(v, exchange(v, b))
    for b in order[:-1][::-1]:
        other = exchange(v, b)
        v = jnp.where(
            bit_of(b) == 1,
            jnp.concatenate([other, v], 0),
            jnp.concatenate([v, other], 0),
        )
    return v


def group_sum(arrays):
    n = lax.axis_size("batch")
    if not is_power(n) or n == 1:
        return [lax.psum(a, "batch").astype(F32) for a in arrays]
    whole = jnp.concatenate(arrays, 0) if len(arrays) > 1 else arrays[0]
    half = whole.shape[0] // 2
    first, second = orders()
    whole = jnp.concatenate([all_sum(whole[:half], first), all_sum(whole[half:], second)], 0)
    out, at = [], 0
    for a in arrays:
        out.append(whole[at : at + a.shape[0]].astype(F32))
        at += a.shape[0]
    return out


def ffn_forward_kernel(x_ref, gain_ref, up_ref, down_ref, part_ref, pre_ref, u_ref, acc_ref):
    i = pl.program_id(0)
    rows = 256
    steps = x_ref.shape[0] // rows

    @pl.when(i == 0)
    def _():
        for t in range(steps):
            at = pl.ds(t * rows, rows)
            hat, _ = norm_parts(x_ref[at, :])
            u_ref[at, :] = (hat * gain_ref[...]).astype(BF)

    for t in range(steps):
        at = pl.ds(t * rows, rows)
        a = dot(u_ref[at, :], up_ref[...], 1, 1)
        pre_ref[at, :] = a.astype(BF)
        h = (a * jax.nn.sigmoid(a)).astype(BF)
        f = dot(h, down_ref[...])

        @pl.when(i == 0)
        def _():
            acc_ref[at, :] = f

        @pl.when(i > 0)
        def _():
            acc_ref[at, :] += f

    @pl.when(i == pl.num_programs(0) - 1)
    def _():
        part_ref[...] = acc_ref[...].astype(BF)


def whole_spec(shape):
    return pl.BlockSpec(shape, lambda *_: (0,) * len(shape))


def ffn_forward(x, gain, up, down):
    t, d = x.shape
    hid = up.shape[0]
    blk = min(512, hid)
    return pl.pallas_call(
        ffn_forward_kernel,
        grid=(hid // blk,),
        in_specs=[
            whole_spec((t, d)),
            whole_spec((1, d)),
            pl.BlockSpec((blk, d), lambda i: (i, 0)),
            pl.BlockSpec((blk, d), lambda i: (i, 0)),
        ],
        out_specs=[
            whole_spec((t, d)),
            pl.BlockSpec((t, blk), lambda i: (0, i)),
            whole_spec((t, d)),
        ],
        out_shape=[
            jax.ShapeDtypeStruct((t, d), BF),
            jax.ShapeDtypeStruct((t, hid), BF),
            jax.ShapeDtypeStruct((t, d), BF),
        ],
        scratch_shapes=[pltpu.VMEM((t, d), F32)],
        compiler_params=pltpu.CompilerParams(vmem_limit_bytes=VMEM),
        cost_estimate=pl.CostEstimate(
            flops=4 * t * d * hid, bytes_accessed=8 * t * d + 4 * hid * d, transcendentals=t * hid
        ),
        name="ffn_forward",
    )(x, gain[None], up, down)


def ffn_down_kernel(g_ref, pre_ref, out_ref, gf_ref):
    @pl.when(pl.program_id(0) == 0)
    def _():
        gf_ref[...] = (0.5 * g_ref[...]).astype(BF)

    a = pre_ref[...].astype(F32)
    h = (a * jax.nn.sigmoid(a)).astype(BF)
    out_ref[...] = dot(h, gf_ref[...], 0, 0).astype(BF)


def ffn_down_grad(g, pre):
    t, d = g.shape
    hid = pre.shape[1]
    blk = min(512, hid)
    return pl.pallas_call(
        ffn_down_kernel,
        grid=(hid // blk,),
        in_specs=[whole_spec((t, d)), pl.BlockSpec((t, blk), lambda i: (0, i))],
        out_specs=pl.BlockSpec((blk, d), lambda i: (i, 0)),
        out_shape=jax.ShapeDtypeStruct((hid, d), BF),
        scratch_shapes=[pltpu.VMEM((t, d), BF)],
        compiler_params=pltpu.CompilerParams(vmem_limit_bytes=VMEM),
        cost_estimate=pl.CostEstimate(
            flops=2 * t * d * hid, bytes_accessed=4 * t * d + 4 * hid * d, transcendentals=t * hid
        ),
        name="ffn_down_grad",
    )(g, pre)


def ffn_back_kernel(g_ref, pre_ref, u_ref, up_ref, down_ref, up_grad_ref, part_ref, gf_ref, acc_ref):
    i = pl.program_id(0)
    rows = 256
    steps = g_ref.shape[0] // rows

    @pl.when(i == 0)
    def _():
        gf_ref[...] = (0.5 * g_ref[...]).astype(BF)

    parts = []
    for t in range(steps):
        at = pl.ds(t * rows, rows)
        gh = dot(gf_ref[at, :], down_ref[...], 1, 1)
        ga = (gh * slope(pre_ref[at, :].astype(F32))).astype(BF)
        f = dot(ga, up_ref[...])

        @pl.when(i == 0)
        def _():
            acc_ref[at, :] = f

        @pl.when(i > 0)
        def _():
            acc_ref[at, :] += f

        parts.append(ga)
    ga = jnp.concatenate(parts, 0)
    up_grad_ref[...] = dot(ga, u_ref[...], 0, 0).astype(BF)

    @pl.when(i == pl.num_programs(0) - 1)
    def _():
        part_ref[...] = acc_ref[...].astype(BF)


def ffn_back(g, pre, u, up, down):
    t, d = g.shape
    hid = up.shape[0]
    blk = min(512, hid)
    return pl.pallas_call(
        ffn_back_kernel,
        grid=(hid // blk,),
        in_specs=[
            whole_spec((t, d)),
            pl.BlockSpec((t, blk), lambda i: (0, i)),
            whole_spec((t, d)),
            pl.BlockSpec((blk, d), lambda i: (i, 0)),
            pl.BlockSpec((blk, d), lambda i: (i, 0)),
        ],
        out_specs=[pl.BlockSpec((blk, d), lambda i: (i, 0)), whole_spec((t, d))],
        out_shape=[jax.ShapeDtypeStruct((hid, d), BF), jax.ShapeDtypeStruct((t, d), BF)],
        scratch_shapes=[pltpu.VMEM((t, d), BF), pltpu.VMEM((t, d), F32)],
        compiler_params=pltpu.CompilerParams(vmem_limit_bytes=VMEM),
        cost_estimate=pl.CostEstimate(
            flops=6 * t * d * hid, bytes_accessed=8 * t * d + 8 * hid * d, transcendentals=t * hid
        ),
        name="ffn_back",
    )(g, pre, u, up, down)


def turned(rows, length):
    return pl.ds(pl.multiple_of(lax.rem(length - pl.program_id(1) * rows, length), rows), length)


def fill_twice(twice_ref, pos_ref):
    length = pos_ref.shape[0]

    @pl.when(pl.program_id(1) == 0)
    def _():
        twice_ref[:length, :] = pos_ref[...]
        twice_ref[length:, :] = pos_ref[...]


def masked_scores(segq_ref, segk_ref, qc_ref, qp_ref, k_ref, pos):
    far = pltpu.roll(dot(qp_ref[...], pos, 1, 1), 0, 1, stride=1, stride_axis=0)
    z = dot(qc_ref[...], k_ref[...], 1, 1) + far
    z = jnp.where(segq_ref[...] == segk_ref[...], z, NEG)
    e = jnp.exp2((z - jnp.max(z, axis=1, keepdims=True)) * (math.log2(math.e) / math.sqrt(DH)))
    return e, 1.0 / jnp.sum(e, axis=1, keepdims=True)


def attention_kernel(segq_ref, segk_ref, qc_ref, qp_ref, k_ref, v_ref, pos_ref, out_ref, twice_ref):
    fill_twice(twice_ref, pos_ref)
    pos = twice_ref[turned(qc_ref.shape[0], k_ref.shape[0]), :]
    e, inverse = masked_scores(segq_ref, segk_ref, qc_ref, qp_ref, k_ref, pos)
    out_ref[...] = (dot(e.astype(BF), v_ref[...]) * inverse).astype(BF)


def attention_specs(t, rows):
    by_query = pl.BlockSpec((rows, DH), lambda h, i: (i, h))
    by_head = pl.BlockSpec((t, DH), lambda h, i: (0, h))
    return by_query, by_head, [
        pl.BlockSpec((rows, 1), lambda h, i: (i, 0)),
        pl.BlockSpec((1, t), lambda h, i: (0, 0)),
    ]


def attention(seg, qc, qp, k, v, pos):
    t, width = qc.shape
    heads = width // DH
    rows = min(256, t)
    by_query, by_head, seg_specs = attention_specs(t, rows)
    return pl.pallas_call(
        attention_kernel,
        grid=(heads, t // rows),
        in_specs=seg_specs + [by_query, by_query, by_head, by_head, by_head],
        out_specs=by_query,
        out_shape=jax.ShapeDtypeStruct((t, width), BF),
        scratch_shapes=[pltpu.VMEM((2 * t, DH), BF)],
        compiler_params=pltpu.CompilerParams(vmem_limit_bytes=VMEM),
        cost_estimate=pl.CostEstimate(
            flops=12 * t * t * width, bytes_accessed=12 * t * width, transcendentals=heads * t * t
        ),
        name="attention_forward",
    )(seg[:, None], seg[None, :], qc, qp, k, v, pos)


def attention_back_kernel(
    segq_ref, segk_ref, qc_ref, qp_ref, k_ref, v_ref, pos_ref, gctx_ref,
    gq_ref, gk_ref, gv_ref, gpos_ref, content_ref, position_ref, gk_acc, gv_acc, twice_ref, gpos_acc,
):
    i = pl.program_id(1)
    rows = qc_ref.shape[0]
    length = k_ref.shape[0]

    @pl.when(i == 0)
    def _():
        gk_acc[...] = jnp.zeros_like(gk_acc)
        gv_acc[...] = jnp.zeros_like(gv_acc)
        gpos_acc[...] = jnp.zeros_like(gpos_acc)
        content_ref[...] = jnp.zeros_like(content_ref)
        position_ref[...] = jnp.zeros_like(position_ref)

    fill_twice(twice_ref, pos_ref)
    place = turned(rows, length)
    pos = twice_ref[place, :]
    e, inverse = masked_scores(segq_ref, segk_ref, qc_ref, qp_ref, k_ref, pos)
    prob = e * inverse
    gctx = gctx_ref[...]
    gprob = dot(gctx, v_ref[...], 1, 1)
    gv_acc[...] += dot(prob.astype(BF), gctx, 0, 0)
    inner = jnp.sum(prob * gprob, axis=1, keepdims=True)
    gz = (prob * (gprob - inner) * (1.0 / math.sqrt(DH))).astype(BF)
    gqc = dot(gz, k_ref[...])
    gk_acc[...] += dot(gz, qc_ref[...], 0, 0)
    at_row = lax.broadcasted_iota(jnp.int32, (rows, rows), 0)
    at_col = lax.broadcasted_iota(jnp.int32, (rows, rows), 1)
    flip = jnp.where(at_row + at_col == rows - 1, 1.0, 0.0).astype(BF)
    wide = pltpu.roll(dot(flip, gz), length - rows + 1, 1, stride=1, stride_axis=0).astype(BF)
    qp_flip = dot(flip, qp_ref[...]).astype(BF)
    gqp = dot(wide, pos)
    gpos_acc[place, :] += dot(wide, qp_flip, 0, 0)
    gq_ref[...] = (gqc + dot(flip, gqp.astype(BF))).astype(BF)
    content_ref[0] += jnp.sum(gqc, axis=0, keepdims=True)
    position_ref[0] += jnp.sum(gqp, axis=0, keepdims=True)

    @pl.when(i == pl.num_programs(1) - 1)
    def _():
        gk_ref[...] = gk_acc[...].astype(BF)
        gv_ref[...] = gv_acc[...].astype(BF)
        gpos_ref[...] = gpos_acc[:length, :] + gpos_acc[length:, :]


def attention_back(seg, qc, qp, k, v, pos, gctx):
    t, width = qc.shape
    heads = width // DH
    rows = min(256, t)
    by_query, by_head, seg_specs = attention_specs(t, rows)
    bias = pl.BlockSpec((1, 1, DH), lambda h, i: (h, 0, 0))
    return pl.pallas_call(
        attention_back_kernel,
        grid=(heads, t // rows),
        in_specs=seg_specs + [by_query, by_query, by_head, by_head, by_head, by_query],
        out_specs=[by_query, by_head, by_head, by_head, bias, bias],
        out_shape=[
            jax.ShapeDtypeStruct((t, width), BF),
            jax.ShapeDtypeStruct((t, width), BF),
            jax.ShapeDtypeStruct((t, width), BF),
            jax.ShapeDtypeStruct((t, width), F32),
            jax.ShapeDtypeStruct((heads, 1, DH), F32),
            jax.ShapeDtypeStruct((heads, 1, DH), F32),
        ],
        scratch_shapes=[
            pltpu.VMEM((t, DH), F32),
            pltpu.VMEM((t, DH), F32),
            pltpu.VMEM((2 * t, DH), BF),
            pltpu.VMEM((2 * t, DH), F32),
        ],
        compiler_params=pltpu.CompilerParams(vmem_limit_bytes=VMEM),
        cost_estimate=pl.CostEstimate(
            flops=36 * t * t * width, bytes_accessed=24 * t * width, transcendentals=heads * t * t
        ),
        name="attention_back",
    )(seg[:, None], seg[None, :], qc, qp, k, v, pos, gctx)


def encoding(length, features):
    half = features // 2
    frequency = jnp.exp(jnp.arange(half).astype(F32) * (-2.0 * math.log(10000.0) / features))
    fine = 32
    steps = jnp.arange(length // fine) * fine
    a = jnp.where(steps < length // 2, -steps, length - steps).astype(F32)[:, None] * frequency[None]
    b = jnp.arange(fine).astype(F32)[:, None] * frequency[None]
    sa, ca = jnp.sin(a)[:, None], jnp.cos(a)[:, None]
    sb, cb = jnp.sin(b)[None], jnp.cos(b)[None]
    sine = sa * cb - ca * sb
    cosine = ca * cb + sa * sb
    return jnp.concatenate([sine, cosine], axis=-1).reshape(length, features).astype(BF)


def on_device(
    frames,
    segment_ids,
    valid_mask,
    first_norm,
    first_up,
    first_down,
    attention_norm,
    query_proj,
    key_proj,
    value_proj,
    output_proj,
    position_proj,
    content_bias,
    position_bias,
    convolution_norm,
    pointwise_in,
    depthwise,
    batch_gain,
    batch_shift,
    pointwise_out,
    second_norm,
    second_up,
    second_down,
    final_norm,
    cotangent,
):
    groups = lax.axis_size("fsdp")
    member = lax.axis_index("fsdp")
    shard_frames, d = frames.shape[1:]
    t = segment_ids.shape[1]
    part = d // groups
    seg = segment_ids[0]
    valid = valid_mask[0].astype(F32)[:, None]

    def own(v, axis=0):
        return lax.dynamic_slice_in_dim(v, member * part, part, axis)

    x0 = gather_rows(frames[0]).astype(F32)
    cot = gather_rows(cotangent[0]).astype(F32)
    value_in, gate_in = pointwise_in[:, :d], pointwise_in[:, d:]
    columns = own_columns(
        [(m, part) for m in (query_proj, key_proj, value_proj, value_in, gate_in, position_proj)]
    )
    qkv_own = columns[:, : 3 * part]
    in_own = columns[:, 3 * part : 5 * part]
    pos_own = columns[:, 5 * part :]
    encoded = encoding(t, d)
    pos = dot(encoded, pos_own).astype(BF)

    part_sum, pre1, u1 = ffn_forward(x0, first_norm, first_up, first_down)
    x1 = x0 + 0.5 * pair_sum(part_sum)
    hat, _ = norm_parts(x1)
    ua = (hat * attention_norm).astype(BF)
    qkv = dot(ua, qkv_own)
    queries = qkv[:, :part]
    keys = qkv[:, part : 2 * part].astype(BF)
    values = qkv[:, 2 * part :].astype(BF)
    qc = (queries + own(content_bias)).astype(BF)
    qp = (queries + own(position_bias)).astype(BF)
    ctx = attention(seg, qc, qp, keys, values, pos)
    x2 = x1 + pair_sum(dot(ctx, output_proj).astype(BF))
    hat, _ = norm_parts(x2)
    uc = (hat * convolution_norm).astype(BF)
    gp = dot(uc, in_own)
    signal, opener = gp[:, :part], jax.nn.sigmoid(gp[:, part:])
    glu = signal * opener
    taps = own(depthwise)
    seg_rim = jnp.pad(seg, (RIM, RIM), constant_values=-1)
    linked = [(seg_rim[o : o + t] == seg).astype(F32)[:, None] for o in range(KER)]

    def rims(v):
        return jnp.pad(v, ((RIM, RIM), (0, 0)))

    glu_rim = rims(glu)
    dc = sum(glu_rim[o : o + t] * linked[o] * taps[:, o] for o in range(KER))
    weighted = valid * dc
    sums = jnp.stack(
        [
            jnp.sum(weighted, axis=0),
            jnp.sum(weighted * dc, axis=0),
            jnp.full((part,), jnp.sum(valid)),
        ]
    )
    sums = row_sum(sums)
    count = sums[2]
    mu = sums[0] / count
    brstd = lax.rsqrt(sums[1] / count - mu * mu + EPS)
    gain_own, shift_own = own(batch_gain), own(batch_shift)

    def standard():
        return (dc - mu) * brstd

    bo = standard() * gain_own + shift_own
    sw = jax.nn.silu(bo).astype(BF)
    x3 = x2 + pair_sum(dot(sw, pointwise_out).astype(BF))
    part_sum, pre2, u2 = ffn_forward(x3, second_norm, second_up, second_down)
    x4 = x3 + 0.5 * pair_sum(part_sum)
    hat, rstd = norm_parts(x4)
    layer_out = lax.dynamic_slice_in_dim(hat, member * shard_frames, shard_frames, 0)
    layer_out = (layer_out * final_norm).astype(BF)[None]

    final_gain = jnp.sum(cot * hat, axis=0)
    g = norm_back(cot, hat, rstd, final_norm)
    second_down_grad = ffn_down_grad(g, pre2)
    second_up_grad, part_sum = ffn_back(g, pre2, u2, second_up, second_down)
    second_sum = group_sum([second_down_grad, second_up_grad])
    gu = pair_sum(part_sum)
    hat, rstd = norm_parts(x3)
    second_gain = jnp.sum(gu * hat, axis=0)
    g = g + norm_back(gu, hat, rstd, second_norm)

    gco = g.astype(BF)
    out_w_grad = dot(sw, gco, 0, 0).astype(BF)
    gbo = dot(gco, pointwise_out, 1, 1) * slope(bo)
    ab = row_sum(jnp.stack([jnp.sum(gbo, axis=0), jnp.sum(gbo * standard(), axis=0)]))
    gmu = -brstd * gain_own * ab[0]
    gvar = -0.5 * brstd * brstd * gain_own * ab[1]
    gdc = gbo * (gain_own * brstd) + valid * ((gmu - 2.0 * mu * gvar + 2.0 * dc * gvar) / count)
    gdc_rim = rims(gdc)
    gglu = sum(
        gdc_rim[KER - 1 - o : KER - 1 - o + t] * linked[KER - 1 - o] * taps[:, o]
        for o in range(KER)
    )
    taps_grad = [jnp.sum(gdc * glu_rim[o : o + t] * linked[o], axis=0) for o in range(KER)]
    ggp = jnp.concatenate([gglu * opener, gglu * signal * opener * (1.0 - opener)], axis=1)
    ggp = ggp.astype(BF)
    in_w_grad = dot(uc, ggp, 0, 0).astype(BF)
    gu = pair_sum(dot(ggp, in_own, 1, 1).astype(BF))
    hat, rstd = norm_parts(x2)
    conv_gain = jnp.sum(gu * hat, axis=0)
    g = g + norm_back(gu, hat, rstd, convolution_norm)

    gao = g.astype(BF)
    output_grad = dot(ctx, gao, 0, 0).astype(BF)
    gctx = dot(gao, output_proj, 1, 1).astype(BF)
    gq, gk, gv, gpos, content_grad, position_grad = attention_back(
        seg, qc, qp, keys, values, pos, gctx
    )
    gqkv = jnp.concatenate([gq, gk, gv], axis=1)
    qkv_grad = dot(ua, gqkv, 0, 0).astype(BF)
    gpos_high = gpos.astype(BF)
    gpos_low = (gpos - gpos_high.astype(F32)).astype(BF)
    pos_grad = (dot(encoded, gpos_high, 0, 0) + dot(encoded, gpos_low, 0, 0)).astype(BF)
    gu = pair_sum(dot(gqkv, qkv_own, 1, 1).astype(BF))
    hat, rstd = norm_parts(x1)
    attention_gain = jnp.sum(gu * hat, axis=0)
    g = g + norm_back(gu, hat, rstd, attention_norm)

    swapped = row_blocks_swap(jnp.concatenate([qkv_grad, in_w_grad, pos_grad], axis=1))

    def unfold(at):
        block = swapped[:, :, at * part : (at + 1) * part]
        return jnp.swapaxes(block, 0, 1).reshape(part, d)

    middle_sum = group_sum([out_w_grad, output_grad] + [unfold(at) for at in range(6)])

    first_down_grad = ffn_down_grad(g, pre1)
    first_up_grad, part_sum = ffn_back(g, pre1, u1, first_up, first_down)
    first_sum = group_sum([first_down_grad, first_up_grad])
    gu = pair_sum(part_sum)
    hat, rstd = norm_parts(x0)
    first_gain = jnp.sum(gu * hat, axis=0)
    g = g + norm_back(gu, hat, rstd, first_norm)
    frames_grad = lax.dynamic_slice_in_dim(g, member * shard_frames, shard_frames, 0)
    frames_grad = frames_grad.astype(BF)[None]

    gains = [own(v) for v in (first_gain, attention_gain, conv_gain, second_gain, final_gain)]
    small = jnp.stack(
        gains + [content_grad.reshape(part), position_grad.reshape(part)] + taps_grad
    )
    small = row_sum(small)
    out_w_grad, output_grad, q_grad, k_grad, v_grad, value_grad, gate_grad, pos_grad = middle_sum
    return (
        layer_out,
        frames_grad,
        small[0],
        first_sum[1],
        first_sum[0],
        small[1],
        q_grad,
        k_grad,
        v_grad,
        output_grad,
        pos_grad,
        small[5],
        small[6],
        small[2],
        jnp.concatenate([value_grad, gate_grad], axis=1),
        small[7:].T,
        ab[1],
        ab[0],
        out_w_grad,
        small[3],
        second_sum[1],
        second_sum[0],
        small[4],
    )


def solution(mesh):
    rows, shard, whole = P("batch", "fsdp", None), P("fsdp", None), P()
    return jax.shard_map(
        on_device,
        mesh=mesh,
        in_specs=(
            rows,
            P("batch", None),
            P("batch", None),
            whole,
            shard,
            shard,
            whole,
            shard,
            shard,
            shard,
            shard,
            shard,
            whole,
            whole,
            whole,
            shard,
            whole,
            whole,
            whole,
            shard,
            whole,
            shard,
            shard,
            whole,
            rows,
        ),
        out_specs=(
            rows,
            rows,
            P("fsdp"),
            shard,
            shard,
            P("fsdp"),
            shard,
            shard,
            shard,
            shard,
            shard,
            P("fsdp"),
            P("fsdp"),
            P("fsdp"),
            shard,
            shard,
            P("fsdp"),
            P("fsdp"),
            shard,
            P("fsdp"),
            shard,
            shard,
            P("fsdp"),
        ),
        check_vma=False,
    )
```

time: 1530 us -> 915 us (0.60)
  waiting for transfers between devices: 728 us -> 410 us
  matrix products: 304 us -> 42.7 us
  local copies, waits for them, and re-layouts: 241 us -> 38.7 us
  Pallas kernels: 0 us -> 175 us
  blocking collectives: 126 us -> 0 us
  other arithmetic: 92.5 us -> 164 us
  starting transfers between devices: 10.8 us -> 72 us
    psum x1 -> x0, waiting for transfers between devices: 624 us -> none  [on_device(): lax.psum(first_up_grad.astype(jnp.bfloat16), 'batch').astype(jnp.float32)]
    ppermute x4 -> x66, waiting for transfers between devices: 0.96 us -> 410 us  [the longest x54 399 us: exchange(): return lax.ppermute(v, 'batch', [(i, i ^ 1 << b) for i in range(n)])]
    dot_general x41 -> x15, matrix products: 304 us -> 42.7 us  [dot(): lax.dot_general(a, b, (((da,), (db,)), ((), ())), preferred_element_type=...]
    pallas_call x0 -> x8, Pallas kernels: none -> 175 us  [the longest x2 53.4 us: ffn_back(): pl.pallas_call(ffn_back_kernel, grid=(hid // blk,), in_specs=[whole_spec(...]
    psum x3 -> x0, blocking collectives: 126 us -> none  [the longest x1 45 us: on_device(): lax.psum((first_gain_grad, attention_gain_grad, content_grad, position_gr...]
    reshape x3 -> x6, local copies, waits for them, and re-layouts: 85.9 us -> 0.71 us  [unfold(): return jnp.swapaxes(block, 0, 1).reshape(part, d)]
    ppermute x4 -> x66, starting transfers between devices: 8.64 us -> 72 us  [the longest x54 69.7 us: exchange(): return lax.ppermute(v, 'batch', [(i, i ^ 1 << b) for i in range(n)])]
    unnamed x186 -> x166, local copies, waits for them, and re-layouts: 73.8 us -> 13.9 us
  transfers between devices with their start and end apart: 31 -> 66, of which waited for: 10 -> 34; matrix products, arithmetic and copies ran while one was open for 32% -> 20% of each run, Pallas kernels for 0% -> 9%
where the time goes in v1:
time: 915 us; the launch traced here: 906 us
  waiting for transfers between devices  410 us (45%)
  Pallas kernels  175 us (19%)
  other arithmetic  164 us (18%)
  starting transfers between devices  72 us (8%)
  matrix products  42.7 us (5%)
  local copies, waits for them, and re-layouts  38.7 us (4%)
    ppermute x54, waiting for transfers between devices, exchange(): return lax.ppermute(v, 'batch', [(i, i ^ 1 << b) for i in range(n)])  399 us
    ppermute x54, starting transfers between devices, exchange(): return lax.ppermute(v, 'batch', [(i, i ^ 1 << b) for i in range(n)])  69.7 us
    pallas_call x2, Pallas kernels, ffn_back(): pl.pallas_call(ffn_back_kernel, grid=(hid // blk,), in_specs=[whole_spec(...  53.4 us
    pallas_call x2, Pallas kernels, ffn_forward(): pl.pallas_call(ffn_forward_kernel, grid=(hid // blk,), in_specs=[whole_sp...  42.9 us
    dot_general x15, matrix products, dot(): lax.dot_general(a, b, (((da,), (db,)), ((), ())), preferred_element_type=...  42.7 us
    pallas_call x1, Pallas kernels, attention_back(): pl.pallas_call(attention_back_kernel, grid=(heads, t // rows), in_specs=s...  39.6 us
    select_n x14, other arithmetic, all_sum(): jnp.where(bit_of(b) == 1, jnp.concatenate([other, v], 0), jnp.concatenate...  29.4 us
    convert_element_type x5, other arithmetic, group_sum(): out.append(whole[at:at + a.shape[0]].astype(F32))  25.7 us
  transfers between devices with their start and end apart: 66, of which 34 were waited for; matrix products, arithmetic and copies ran while one was open for 20% of the time, Pallas kernels for 9%

profile of v1, /device:TPU:0, one launch (start us, length us, event | category | flops | bytes accessed | tf_op | source)
XLA Modules:
  0.0 905.5 jit_solution(14181736354649715410)
XLA Ops:
  10.6 21.3 %ffn_forward.2 = (bf16[1024,1024]{1,0:T(8,128)(2,1)}, bf16[1024,2048]{1,0:T(8,128)(2,1)}, bf16[1024,1024]{1,0:T(8,128)(2,1)}) custom-call(f32[1024,1024]{1,0:T(8,128)} %bitcast.120, f32[1,1024]{1,0:T(1,128)} %bitcast.193, bf16[2048,1024]{1,0:T(8,128)(2,1)} %up_ref.7, bf16[2048,1024]{1,0:T(8,128)(2,1)} %down_ref.7), custom_call_target="tpu_custom_call" | custom-call | flops 8589934592 | bytes 16777216 | tf_op jit(solution)/shard_map/ffn_forward/pallas_call | solution.py:221
  37.1 4.4 fusion.75
  42.2 6.3 maximum_select_fusion
  48.5 3.6 fusion.81
  57.6 19.8 %attention_forward.1 = bf16[1024,512]{1,0:T(8,128)(2,1)} custom-call(s32[1024,1]{1,0:T(8,128)} %copy.61.segq_ref, s32[1,1024]{1,0:T(1,128)} %segk_ref.3, bf16[1024,512]{1,0:T(8,128)(2,1)} %get-tuple-element.107.qc_ref, bf16[1024,512]{1,0:T(8,128)(2,1)} %get-tuple-element.106.qp_ref, bf16[1024,512]{1,0:T(8,128)(2,1)} %get-tuple-element.117.k_ref, ...), custom_call_target="tpu_custom_call" | custom-call | flops 6442450944 | bytes 6291456 | tf_op jit(solution)/shard_map/attention_forward/pallas_call | solution.py:378
  84.3 3.6 fusion.74
  88.7 4.8 fusion.36
  109.5 3.1 collective-permute-start.7
  115.9 4.1 collective-permute-done.8
  120.1 3.1 add_add_fusion.x_ref
  123.1 21.6 %ffn_forward.3 = (bf16[1024,1024]{1,0:T(8,128)(2,1)}, bf16[1024,2048]{1,0:T(8,128)(2,1)}, bf16[1024,1024]{1,0:T(8,128)(2,1)}) custom-call(f32[1024,1024]{1,0:T(8,128)} %add_add_fusion.x_ref, f32[1,1024]{1,0:T(1,128)} %bitcast.177, bf16[2048,1024]{1,0:T(8,128)(2,1)} %up_ref.6, bf16[2048,1024]{1,0:T(8,128)(2,1)} %down_ref.6), custom_call_target="tpu_custom_call" | custom-call | flops 8589934592 | bytes 16777216 | tf_op jit(solution)/shard_map/ffn_forward/pallas_call | solution.py:221
  145.3 5.5 collective-permute-done.10
  150.8 3.1 fusion.9
  153.9 4.2 fusion.70
  158.1 3.4 multiply_reduce_fusion.9
  161.5 5.6 fusion.10
  167.2 6.9 fusion.7.g_ref
  174.1 26.8 %ffn_back.2 = (bf16[2048,1024]{1,0:T(8,128)(2,1)}, bf16[1024,1024]{1,0:T(8,128)(2,1)}) custom-call(f32[1024,1024]{1,0:T(8,128)} %fusion.7.g_ref, bf16[1024,2048]{1,0:T(8,128)(2,1)} %get-tuple-element.41.pre_ref, bf16[1024,1024]{1,0:T(8,128)(2,1)} %get-tuple-element.42.u_ref, bf16[2048,1024]{1,0:T(8,128)(2,1)} %up_ref.6, bf16[2048,1024]{1,0:T(8,128)(2,1)} %down_ref.6), custom_call_target="tpu_custom_call" | custom-call | flops 12884901888 | bytes 25165824 | tf_op jit(solution)/shard_map/ffn_back/pallas_call | solution.py:315
  204.5 3.2 multiply_reduce_fusion.5
  209.1 9.5 %ffn_down_grad.3 = bf16[2048,1024]{1,0:T(8,128)(2,1)} custom-call(f32[1024,1024]{1,0:T(8,128)} %fusion.7.g_ref, bf16[1024,2048]{1,0:T(8,128)(2,1)} %get-tuple-element.41.pre_ref), custom_call_target="tpu_custom_call" | custom-call | flops 4294967296 | bytes 12582912 | tf_op jit(solution)/shard_map/ffn_down_grad/pallas_call | solution.py:263
  225.5 3.6 multiply_reduce_fusion
  229.1 3.2 multiply_add_fusion.2
  235.3 33.3 %collective-permute-done.59 = bf16[1024,1024]{1,0:T(8,128)(2,1)S(1)} collective-permute-done((bf16[1024,1024]{1,0:T(8,128)(2,1)S(1)}, bf16[1024,1024]{1,0:T(8,128)(2,1)S(1)}, u32[]{:S(2)}, u32[]{:S(2)}) %collective-permute-start.59) | collective-permute-done | bytes 2097184 | tf_op jit(solution)/shard_map/ppermute | solution.py:119
  276.2 19.8 %collective-permute-done.14 = f32[2,512]{1,0:T(2,128)S(1)} collective-permute-done((f32[2,512]{1,0:T(2,128)S(1)}, f32[2,512]{1,0:T(2,128)S(1)}, u32[]{:S(2)}, u32[]{:S(2)}) %collective-permute-start.14) | collective-permute-done | bytes 4128 | tf_op jit(solution)/shard_map/ppermute | solution.py:119
  300.6 3.0 multiply_reduce_fusion.14
  307.3 4.0 convolution_convert_fusion.2
  312.3 9.6 %collective-permute-done.53 = bf16[512,1024]{1,0:T(8,128)(2,1)S(1)} collective-permute-done((bf16[512,1024]{1,0:T(8,128)(2,1)S(1)}, bf16[512,1024]{1,0:T(8,128)(2,1)S(1)}, u32[]{:S(2)}, u32[]{:S(2)}) %collective-permute-start.53) | collective-permute-done | bytes 1048608 | tf_op jit(solution)/shard_map/ppermute | solution.py:119
  329.0 4.3 collective-permute-done.54
  336.6 27.9 %collective-permute-done.62 = bf16[256,1024]{1,0:T(8,128)(2,1)S(1)} collective-permute-done((bf16[256,1024]{1,0:T(8,128)(2,1)S(1)}, bf16[256,1024]{1,0:T(8,128)(2,1)S(1)}, u32[]{:S(2)}, u32[]{:S(2)}) %collective-permute-start.62) | collective-permute-done | bytes 524320 | tf_op jit(solution)/shard_map/ppermute | solution.py:119
  365.3 9.3 %collective-permute-done.55 = bf16[256,1024]{1,0:T(8,128)(2,1)S(1)} collective-permute-done((bf16[256,1024]{1,0:T(8,128)(2,1)S(1)}, bf16[256,1024]{1,0:T(8,128)(2,1)S(1)}, u32[]{:S(2)}, u32[]{:S(2)}) %collective-permute-start.55) | collective-permute-done | bytes 524320 | tf_op jit(solution)/shard_map/ppermute | solution.py:119
  382.8 39.6 %attention_back.1 = (bf16[1024,512]{1,0:T(8,128)(2,1)}, bf16[1024,512]{1,0:T(8,128)(2,1)}, bf16[1024,512]{1,0:T(8,128)(2,1)}, f32[1024,512]{1,0:T(8,128)}, f32[4,1,128]{2,1,0:T(1,128)}, /*index=5*/f32[4,1,128]{2,1,0:T(1,128)}) custom-call(s32[1024,1]{1,0:T(8,128)} %copy.61.segq_ref, s32[1,1024]{1,0:T(1,128)} %segk_ref.3, ...), custom_call_target="tpu_custom_call" | custom-call | flops 19327352832 | bytes 12582912 | tf_op jit(solution)/shard_map/attention_back/pallas_call | solution.py:445
  425.3 5.8 fusion.32
  431.1 4.1 convolution_convert_fusion
  439.8 3.1 dynamic-slice_bitcast_fusion
  448.5 15.8 %collective-permute-done.57 = bf16[512,1024]{1,0:T(8,128)(2,1)S(1)} collective-permute-done((bf16[512,1024]{1,0:T(8,128)(2,1)S(1)}, bf16[512,1024]{1,0:T(8,128)(2,1)S(1)}, u32[]{:S(2)}, u32[]{:S(2)}) %collective-permute-start.57) | collective-permute-done | bytes 1048608 | tf_op jit(solution)/shard_map/ppermute | solution.py:119
  469.7 3.1 multiply_add_fusion.g_ref
  472.8 9.4 %ffn_down_grad.2 = bf16[2048,1024]{1,0:T(8,128)(2,1)} custom-call(f32[1024,1024]{1,0:T(8,128)} %multiply_add_fusion.g_ref, bf16[1024,2048]{1,0:T(8,128)(2,1)} %get-tuple-element.47.pre_ref), custom_call_target="tpu_custom_call" | custom-call | flops 4294967296 | bytes 12582912 | tf_op jit(solution)/shard_map/ffn_down_grad/pallas_call | solution.py:263
  482.3 3.1 constant_dynamic-slice_fusion.16
  485.8 26.6 %ffn_back.3 = (bf16[2048,1024]{1,0:T(8,128)(2,1)}, bf16[1024,1024]{1,0:T(8,128)(2,1)}) custom-call(f32[1024,1024]{1,0:T(8,128)} %multiply_add_fusion.g_ref, bf16[1024,2048]{1,0:T(8,128)(2,1)} %get-tuple-element.47.pre_ref, bf16[1024,1024]{1,0:T(8,128)(2,1)} %get-tuple-element.48.u_ref, bf16[2048,1024]{1,0:T(8,128)(2,1)} %up_ref.7, bf16[2048,1024]{1,0:T(8,128)(2,1)} %down_ref.7), custom_call_target="tpu_custom_call" | custom-call | flops 12884901888 | bytes 25165824 | tf_op jit(solution)/shard_map/ffn_back/pallas_call | solution.py:315
  512.4 3.2 constant_dynamic-slice_fusion.19
  517.2 4.0 maximum_select_fusion.1
  536.5 6.6 fusion.2
  543.0 21.4 %collective-permute-done.23 = bf16[1024,1024]{1,0:T(8,128)(2,1)S(1)} collective-permute-done((bf16[1024,1024]{1,0:T(8,128)(2,1)}, bf16[1024,1024]{1,0:T(8,128)(2,1)S(1)}, u32[]{:S(2)}, u32[]{:S(2)}) %collective-permute-start.23) | collective-permute-done | bytes 2097184 | tf_op jit(solution)/shard_map/ppermute | solution.py:119
  565.5 41.6 %collective-permute-done.45 = bf16[1024,1024]{1,0:T(8,128)(2,1)S(1)} collective-permute-done((bf16[1024,1024]{1,0:T(8,128)(2,1)}, bf16[1024,1024]{1,0:T(8,128)(2,1)S(1)}, u32[]{:S(2)}, u32[]{:S(2)}) %collective-permute-start.45) | collective-permute-done | bytes 2097184 | tf_op jit(solution)/shard_map/ppermute | solution.py:119
  610.7 11.3 %collective-permute-done.38 = bf16[1024,1024]{1,0:T(8,128)(2,1)S(1)} collective-permute-done((bf16[1024,1024]{1,0:T(8,128)(2,1)}, bf16[1024,1024]{1,0:T(8,128)(2,1)S(1)}, u32[]{:S(2)}, u32[]{:S(2)}) %collective-permute-start.38) | collective-permute-done | bytes 2097184 | tf_op jit(solution)/shard_map/ppermute | solution.py:119
  624.6 8.6 collective-permute-done.24
  636.2 25.1 %collective-permute-done.46 = bf16[512,1024]{1,0:T(8,128)(2,1)S(1)} collective-permute-done((bf16[512,1024]{1,0:T(8,128)(2,1)S(1)}, bf16[512,1024]{1,0:T(8,128)(2,1)S(1)}, u32[]{:S(2)}, u32[]{:S(2)}) %collective-permute-start.46) | collective-permute-done | bytes 1048608 | tf_op jit(solution)/shard_map/ppermute | solution.py:119
  665.1 21.0 %collective-permute-done.39 = bf16[512,1024]{1,0:T(8,128)(2,1)S(1)} collective-permute-done((bf16[512,1024]{1,0:T(8,128)(2,1)S(1)}, bf16[512,1024]{1,0:T(8,128)(2,1)S(1)}, u32[]{:S(2)}, u32[]{:S(2)}) %collective-permute-start.39) | collective-permute-done | bytes 1048608 | tf_op jit(solution)/shard_map/ppermute | solution.py:119
  691.7 30.7 %collective-permute-done.26 = bf16[256,1024]{1,0:T(8,128)(2,1)S(1)} collective-permute-done((bf16[256,1024]{1,0:T(8,128)(2,1)S(1)}, bf16[256,1024]{1,0:T(8,128)(2,1)S(1)}, u32[]{:S(2)}, u32[]{:S(2)}) %collective-permute-start.26) | collective-permute-done | bytes 524320 | tf_op jit(solution)/shard_map/ppermute | solution.py:119
  725.8 7.7 collective-permute-done.48
  740.7 16.8 %collective-permute-done.41 = bf16[256,1024]{1,0:T(8,128)(2,1)S(1)} collective-permute-done((bf16[256,1024]{1,0:T(8,128)(2,1)S(1)}, bf16[256,1024]{1,0:T(8,128)(2,1)S(1)}, u32[]{:S(2)}, u32[]{:S(2)}) %collective-permute-start.41) | collective-permute-done | bytes 524320 | tf_op jit(solution)/shard_map/ppermute | solution.py:119
  762.9 5.0 multiply_reduce_fusion.3
  768.1 3.5 collective-permute-done.42
  775.1 24.1 %collective-permute-done.28 = bf16[512,1024]{1,0:T(8,128)(2,1)} collective-permute-done((bf16[512,1024]{1,0:T(8,128)(2,1)}, bf16[512,1024]{1,0:T(8,128)(2,1)}, u32[]{:S(2)}, u32[]{:S(2)}) %collective-permute-start.28) | collective-permute-done | bytes 1048608 | tf_op jit(solution)/shard_map/ppermute | solution.py:119
  799.2 3.4 maximum_select_fusion.10
  804.2 3.3 maximum_select_fusion.11
  808.1 6.6 fusion.3
  815.4 6.3 collective-permute-done.50
  821.7 3.3 maximum_select_fusion.13
  826.5 25.4 %collective-permute-done.20 = f32[12,512]{1,0:T(8,128)S(1)} collective-permute-done((f32[12,512]{1,0:T(8,128)S(1)}, f32[12,512]{1,0:T(8,128)S(1)}, u32[]{:S(2)}, u32[]{:S(2)}) %collective-permute-start.20) | collective-permute-done | bytes 24608 | tf_op jit(solution)/shard_map/ppermute | solution.py:119
  863.5 4.4 fusion
  868.0 4.4 fusion.1
  872.4 19.1 %collective-permute-done.51 = bf16[1024,1024]{1,0:T(8,128)(2,1)S(1)} collective-permute-done((bf16[1024,1024]{1,0:T(8,128)(2,1)S(1)}, bf16[1024,1024]{1,0:T(8,128)(2,1)S(1)}, u32[]{:S(2)}, u32[]{:S(2)}) %collective-permute-start.51) | collective-permute-done | bytes 2097184 | tf_op jit(solution)/shard_map/ppermute | solution.py:119
  899.1 3.6 slice_convert_fusion
  (426 shorter events, 199.8 us)
Async XLA Ops:
  0.7 7.5 collective-permute-start
  31.9 5.2 collective-permute-start.1
  34.2 8.0 collective-permute-start.2
  80.0 4.4 collective-permute-start.3
  97.7 4.3 collective-permute-start.4
  105.8 3.7 collective-permute-start.6
  109.5 4.7 collective-permute-start.7
  115.8 4.2 collective-permute-start.8
  144.8 9.1 %collective-permute-start.9 = (bf16[1024,1024]{1,0:T(8,128)(2,1)}, bf16[1024,1024]{1,0:T(8,128)(2,1)}, u32[]{:S(2)}, u32[]{:S(2)}) collective-permute-start(bf16[1024,1024]{1,0:T(8,128)(2,1)} %get-tuple-element.40), channel_id=1, source_target_pairs={{0,1},{1,0},{2,3},{3,2},{4,5},{5,4},{6,7},{7,6},{8,9},{9,8},{10,11... | collective-permute-start | bytes 6291464 | tf_op jit(solution)/shard_map/ppermute | solution.py:46
  144.9 5.9 collective-permute-start.10
  200.9 24.6 %collective-permute-start.11 = (bf16[1024,1024]{1,0:T(8,128)(2,1)}, bf16[1024,1024]{1,0:T(8,128)(2,1)}, u32[]{:S(2)}, u32[]{:S(2)}) collective-permute-start(bf16[1024,1024]{1,0:T(8,128)(2,1)} %get-tuple-element.43), channel_id=1, source_target_pairs={{0,1},{1,0},{2,3},{3,2},{4,5},{5,4},{6,7},{7,6},{8,9},{9,8},{10,11... | collective-permute-start | bytes 6291464 | tf_op jit(solution)/shard_map/ppermute | solution.py:46
  220.6 48.1 %collective-permute-start.59 = (bf16[1024,1024]{1,0:T(8,128)(2,1)S(1)}, bf16[1024,1024]{1,0:T(8,128)(2,1)S(1)}, u32[]{:S(2)}, u32[]{:S(2)}) collective-permute-start(bf16[1024,1024]{1,0:T(8,128)(2,1)S(1)} %constant_dynamic-slice_fusion.3), channel_id=1, source_target_pairs={{0,2},{2,0},{4,6},{6,4},{8,10},{10,8},{12,14},{14,12},{16,18},{18,... | collective-permute-start | bytes 6291464 | tf_op jit(solution)/shard_map/ppermute | solution.py:119
  222.6 52.6 %collective-permute-start.52 = (bf16[1024,1024]{1,0:T(8,128)(2,1)S(1)}, bf16[1024,1024]{1,0:T(8,128)(2,1)S(1)}, u32[]{:S(2)}, u32[]{:S(2)}) collective-permute-start(bf16[1024,1024]{1,0:T(8,128)(2,1)S(1)} %constant_dynamic-slice_fusion.6), channel_id=1, source_target_pairs={{0,4},{2,6},{4,0},{6,2},{8,12},{10,14},{12,8},{14,10},{16,20},{18,... | collective-permute-start | bytes 6291464 | tf_op jit(solution)/shard_map/ppermute | solution.py:119
  234.4 35.2 %collective-permute-start.12 = (f32[2,512]{1,0:T(2,128)S(1)}, f32[2,512]{1,0:T(2,128)S(1)}, u32[]{:S(2)}, u32[]{:S(2)}) collective-permute-start(f32[2,512]{1,0:T(2,128)S(1)} %pad_maximum_fusion.9), channel_id=1, source_target_pairs={{0,2},{2,0},{4,6},{6,4},{8,10},{10,8},{12,14},{14,12},{16,18},{18,... | collective-permute-start | bytes 12296 | tf_op jit(solution)/shard_map/ppermute | solution.py:119
  271.5 39.8 %collective-permute-start.60 = (bf16[512,1024]{1,0:T(8,128)(2,1)S(1)}, bf16[512,1024]{1,0:T(8,128)(2,1)S(1)}, u32[]{:S(2)}, u32[]{:S(2)}) collective-permute-start(bf16[512,1024]{1,0:T(8,128)(2,1)S(1)} %constant_dynamic-slice_fusion.2), channel_id=1, source_target_pairs={{0,8},{2,10},{4,12},{6,14},{8,0},{10,2},{12,4},{14,6},{16,24},{18,... | collective-permute-start | bytes 3145736 | tf_op jit(solution)/shard_map/ppermute | solution.py:119
  273.3 22.6 %collective-permute-start.14 = (f32[2,512]{1,0:T(2,128)S(1)}, f32[2,512]{1,0:T(2,128)S(1)}, u32[]{:S(2)}, u32[]{:S(2)}) collective-permute-start(f32[2,512]{1,0:T(2,128)S(1)} %fusion.90), channel_id=1, source_target_pairs={{0,8},{2,10},{4,12},{6,14},{8,0},{10,2},{12,4},{14,6},{16,24},{18,... | collective-permute-start | bytes 12296 | tf_op jit(solution)/shard_map/ppermute | solution.py:119
  296.0 4.6 collective-permute-start.15
  298.6 23.2 %collective-permute-start.53 = (bf16[512,1024]{1,0:T(8,128)(2,1)S(1)}, bf16[512,1024]{1,0:T(8,128)(2,1)S(1)}, u32[]{:S(2)}, u32[]{:S(2)}) collective-permute-start(bf16[512,1024]{1,0:T(8,128)(2,1)S(1)} %constant_dynamic-slice_fusion.5), channel_id=1, source_target_pairs={{0,8},{2,10},{4,12},{6,14},{8,0},{10,2},{12,4},{14,6},{16,24},{18,... | collective-permute-start | bytes 3145736 | tf_op jit(solution)/shard_map/ppermute | solution.py:119
  311.3 65.1 %collective-permute-start.16 = (bf16[1024,1024]{1,0:T(8,128)(2,1)S(1)}, bf16[1024,1024]{1,0:T(8,128)(2,1)S(1)}, u32[]{:S(2)}, u32[]{:S(2)}) collective-permute-start(bf16[1024,1024]{1,0:T(8,128)(2,1)S(1)} %convolution_convert_fusion.2), channel_id=1, source_target_pairs={{0,1},{1,0},{2,3},{3,2},{4,5},{5,4},{6,7},{7,6},{8,9},{9,8},{10,11... | collective-permute-start | bytes 6291464 | tf_op jit(solution)/shard_map/ppermute | solution.py:46
  311.8 14.5 %collective-permute-start.61 = (bf16[256,1024]{1,0:T(8,128)(2,1)S(1)}, bf16[256,1024]{1,0:T(8,128)(2,1)S(1)}, u32[]{:S(2)}, u32[]{:S(2)}) collective-permute-start(bf16[256,1024]{1,0:T(8,128)(2,1)S(1)} %constant_dynamic-slice_fusion.1), channel_id=1, source_target_pairs={{0,4},{2,6},{4,0},{6,2},{8,12},{10,14},{12,8},{14,10},{16,20},{18,... | collective-permute-start | bytes 1572872 | tf_op jit(solution)/shard_map/ppermute | solution.py:119
  322.3 11.0 %collective-permute-start.54 = (bf16[256,1024]{1,0:T(8,128)(2,1)S(1)}, bf16[256,1024]{1,0:T(8,128)(2,1)S(1)}, u32[]{:S(2)}, u32[]{:S(2)}) collective-permute-start(bf16[256,1024]{1,0:T(8,128)(2,1)S(1)} %constant_dynamic-slice_fusion.4), channel_id=1, source_target_pairs={{0,2},{2,0},{4,6},{6,4},{8,10},{10,8},{12,14},{14,12},{16,18},{18,... | collective-permute-start | bytes 1572872 | tf_op jit(solution)/shard_map/ppermute | solution.py:119
  326.6 38.0 %collective-permute-start.62 = (bf16[256,1024]{1,0:T(8,128)(2,1)S(1)}, bf16[256,1024]{1,0:T(8,128)(2,1)S(1)}, u32[]{:S(2)}, u32[]{:S(2)}) collective-permute-start(bf16[256,1024]{1,0:T(8,128)(2,1)S(1)} %add_convert_fusion.17), channel_id=1, source_target_pairs={{0,16},{2,18},{4,20},{6,22},{8,24},{10,26},{12,28},{14,30},{16,0},... | collective-permute-start | bytes 1572872 | tf_op jit(solution)/shard_map/ppermute | solution.py:119
  333.5 41.1 %collective-permute-start.55 = (bf16[256,1024]{1,0:T(8,128)(2,1)S(1)}, bf16[256,1024]{1,0:T(8,128)(2,1)S(1)}, u32[]{:S(2)}, u32[]{:S(2)}) collective-permute-start(bf16[256,1024]{1,0:T(8,128)(2,1)S(1)} %add_convert_fusion.19), channel_id=1, source_target_pairs={{0,16},{2,18},{4,20},{6,22},{8,24},{10,26},{12,28},{14,30},{16,0},... | collective-permute-start | bytes 1572872 | tf_op jit(solution)/shard_map/ppermute | solution.py:119
  364.8 80.6 %collective-permute-start.63 = (bf16[256,1024]{1,0:T(8,128)(2,1)S(1)}, bf16[256,1024]{1,0:T(8,128)(2,1)}, u32[]{:S(2)}, u32[]{:S(2)}) collective-permute-start(bf16[256,1024]{1,0:T(8,128)(2,1)S(1)} %add_convert_fusion.16), channel_id=1, source_target_pairs={{0,4},{2,6},{4,0},{6,2},{8,12},{10,14},{12,8},{14,10},{16,20},{18,... | collective-permute-start | bytes 1572872 | tf_op jit(solution)/shard_map/ppermute | solution.py:119
  374.8 63.1 %collective-permute-start.56 = (bf16[256,1024]{1,0:T(8,128)(2,1)S(1)}, bf16[256,1024]{1,0:T(8,128)(2,1)S(1)}, u32[]{:S(2)}, u32[]{:S(2)}) collective-permute-start(bf16[256,1024]{1,0:T(8,128)(2,1)S(1)} %add_convert_fusion.18), channel_id=1, source_target_pairs={{0,2},{2,0},{4,6},{6,4},{8,10},{10,8},{12,14},{14,12},{16,18},{18,... | collective-permute-start | bytes 1572872 | tf_op jit(solution)/shard_map/ppermute | solution.py:119
  436.5 30.7 %collective-permute-start.17 = (bf16[1024,1024]{1,0:T(8,128)(2,1)S(1)}, bf16[1024,1024]{1,0:T(8,128)(2,1)S(1)}, u32[]{:S(2)}, u32[]{:S(2)}) collective-permute-start(bf16[1024,1024]{1,0:T(8,128)(2,1)S(1)} %fusion.32), channel_id=1, source_target_pairs={{0,1},{1,0},{2,3},{3,2},{4,5},{5,4},{6,7},{7,6},{8,9},{9,8},{10,11... | collective-permute-start | bytes 6291464 | tf_op jit(solution)/shard_map/ppermute | solution.py:46
  438.4 26.0 %collective-permute-start.57 = (bf16[512,1024]{1,0:T(8,128)(2,1)S(1)}, bf16[512,1024]{1,0:T(8,128)(2,1)S(1)}, u32[]{:S(2)}, u32[]{:S(2)}) collective-permute-start(bf16[512,1024]{1,0:T(8,128)(2,1)S(1)} %maximum_select_fusion.20), channel_id=1, source_target_pairs={{0,8},{2,10},{4,12},{6,14},{8,0},{10,2},{12,4},{14,6},{16,24},{18,... | collective-permute-start | bytes 3145736 | tf_op jit(solution)/shard_map/ppermute | solution.py:119
  442.9 74.3 %collective-permute-start.37 = (bf16[512,3072]{1,0:T(8,128)(2,1)}, bf16[512,3072]{1,0:T(8,128)(2,1)}, u32[]{:S(2)}, u32[]{:S(2)}) collective-permute-start(bf16[512,3072]{1,0:T(8,128)(2,1)} %get-tuple-element.105), channel_id=1, source_target_pairs={{0,1},{1,0},{2,3},{3,2},{4,5},{5,4},{6,7},{7,6},{8,9},{9,8},{10,11... | collective-permute-start | bytes 9437192 | tf_op jit(solution)/shard_map/ppermute | solution.py:46
  447.1 77.6 %collective-permute-start.64 = (bf16[512,1024]{1,0:T(8,128)(2,1)S(1)}, bf16[512,1024]{1,0:T(8,128)(2,1)}, u32[]{:S(2)}, u32[]{:S(2)}) collective-permute-start(bf16[512,1024]{1,0:T(8,128)(2,1)S(1)} %maximum_select_fusion.21), channel_id=1, source_target_pairs={{0,8},{2,10},{4,12},{6,14},{8,0},{10,2},{12,4},{14,6},{16,24},{18,... | collective-permute-start | bytes 3145736 | tf_op jit(solution)/shard_map/ppermute | solution.py:119
  466.7 68.9 %collective-permute-start.58 = (bf16[1024,1024]{1,0:T(8,128)(2,1)}, bf16[1024,1024]{1,0:T(8,128)(2,1)}, u32[]{:S(2)}, u32[]{:S(2)}) collective-permute-start(bf16[1024,1024]{1,0:T(8,128)(2,1)} %maximum_select_fusion.14), channel_id=1, source_target_pairs={{0,4},{2,6},{4,0},{6,2},{8,12},{10,14},{12,8},{14,10},{16,20},{18,... | collective-permute-start | bytes 6291464 | tf_op jit(solution)/shard_map/ppermute | solution.py:119
  485.4 48.8 %collective-permute-start.30 = (bf16[1024,1024]{1,0:T(8,128)(2,1)}, bf16[1024,1024]{1,0:T(8,128)(2,1)S(1)}, u32[]{:S(2)}, u32[]{:S(2)}) collective-permute-start(bf16[1024,1024]{1,0:T(8,128)(2,1)} %constant_dynamic-slice_fusion.16), channel_id=1, source_target_pairs={{0,2},{2,0},{4,6},{6,4},{8,10},{10,8},{12,14},{14,12},{16,18},{18,... | collective-permute-start | bytes 6291464 | tf_op jit(solution)/shard_map/ppermute | solution.py:119
  515.7 48.8 %collective-permute-start.23 = (bf16[1024,1024]{1,0:T(8,128)(2,1)}, bf16[1024,1024]{1,0:T(8,128)(2,1)S(1)}, u32[]{:S(2)}, u32[]{:S(2)}) collective-permute-start(bf16[1024,1024]{1,0:T(8,128)(2,1)} %constant_dynamic-slice_fusion.19), channel_id=1, source_target_pairs={{0,4},{2,6},{4,0},{6,2},{8,12},{10,14},{12,8},{14,10},{16,20},{18,... | collective-permute-start | bytes 6291464 | tf_op jit(solution)/shard_map/ppermute | solution.py:119
  524.2 82.9 %collective-permute-start.45 = (bf16[1024,1024]{1,0:T(8,128)(2,1)}, bf16[1024,1024]{1,0:T(8,128)(2,1)S(1)}, u32[]{:S(2)}, u32[]{:S(2)}) collective-permute-start(bf16[1024,1024]{1,0:T(8,128)(2,1)} %constant_dynamic-slice_fusion.9), channel_id=1, source_target_pairs={{0,4},{2,6},{4,0},{6,2},{8,12},{10,14},{12,8},{14,10},{16,20},{18,... | collective-permute-start | bytes 6291464 | tf_op jit(solution)/shard_map/ppermute | solution.py:119
  527.4 280.1 %collective-permute-start.65 = (bf16[1024,1024]{1,0:T(8,128)(2,1)S(1)}, bf16[1024,1024]{1,0:T(8,128)(2,1)}, u32[]{:S(2)}, u32[]{:S(2)}) collective-permute-start(bf16[1024,1024]{1,0:T(8,128)(2,1)S(1)} %maximum_select_fusion.15), channel_id=1, source_target_pairs={{0,2},{2,0},{4,6},{6,4},{8,10},{10,8},{12,14},{14,12},{16,18},{18,... | collective-permute-start | bytes 6291464 | tf_op jit(solution)/shard_map/ppermute | solution.py:119
  534.1 87.9 %collective-permute-start.38 = (bf16[1024,1024]{1,0:T(8,128)(2,1)}, bf16[1024,1024]{1,0:T(8,128)(2,1)S(1)}, u32[]{:S(2)}, u32[]{:S(2)}) collective-permute-start(bf16[1024,1024]{1,0:T(8,128)(2,1)} %constant_dynamic-slice_fusion.12), channel_id=1, source_target_pairs={{0,2},{2,0},{4,6},{6,4},{8,10},{10,8},{12,14},{14,12},{16,18},{18,... | collective-permute-start | bytes 6291464 | tf_op jit(solution)/shard_map/ppermute | solution.py:119
  535.7 73.2 %collective-permute-start.31 = (bf16[512,1024]{1,0:T(8,128)(2,1)S(1)}, bf16[512,1024]{1,0:T(8,128)(2,1)S(1)}, u32[]{:S(2)}, u32[]{:S(2)}) collective-permute-start(bf16[512,1024]{1,0:T(8,128)(2,1)S(1)} %constant_dynamic-slice_fusion.15), channel_id=1, source_target_pairs={{0,8},{2,10},{4,12},{6,14},{8,0},{10,2},{12,4},{14,6},{16,24},{18,... | collective-permute-start | bytes 3145736 | tf_op jit(solution)/shard_map/ppermute | solution.py:119
  564.4 196.3 %collective-permute-start.18 = (bf16[1024,1024]{1,0:T(8,128)(2,1)S(1)}, bf16[1024,1024]{1,0:T(8,128)(2,1)S(1)}, u32[]{:S(2)}, u32[]{:S(2)}) collective-permute-start(bf16[1024,1024]{1,0:T(8,128)(2,1)S(1)} %copy-done.28), channel_id=1, source_target_pairs={{0,1},{1,0},{2,3},{3,2},{4,5},{5,4},{6,7},{7,6},{8,9},{9,8},{10,11... | collective-permute-start | bytes 6291464 | tf_op jit(solution)/shard_map/ppermute | solution.py:46
  607.1 26.1 %collective-permute-start.24 = (bf16[512,1024]{1,0:T(8,128)(2,1)S(1)}, bf16[512,1024]{1,0:T(8,128)(2,1)S(1)}, u32[]{:S(2)}, u32[]{:S(2)}) collective-permute-start(bf16[512,1024]{1,0:T(8,128)(2,1)S(1)} %constant_dynamic-slice_fusion.18), channel_id=1, source_target_pairs={{0,8},{2,10},{4,12},{6,14},{8,0},{10,2},{12,4},{14,6},{16,24},{18,... | collective-permute-start | bytes 3145736 | tf_op jit(solution)/shard_map/ppermute | solution.py:119
  608.9 52.4 %collective-permute-start.46 = (bf16[512,1024]{1,0:T(8,128)(2,1)S(1)}, bf16[512,1024]{1,0:T(8,128)(2,1)S(1)}, u32[]{:S(2)}, u32[]{:S(2)}) collective-permute-start(bf16[512,1024]{1,0:T(8,128)(2,1)S(1)} %constant_dynamic-slice_fusion.8), channel_id=1, source_target_pairs={{0,8},{2,10},{4,12},{6,14},{8,0},{10,2},{12,4},{14,6},{16,24},{18,... | collective-permute-start | bytes 3145736 | tf_op jit(solution)/shard_map/ppermute | solution.py:119
  622.0 12.4 %collective-permute-start.32 = (bf16[256,1024]{1,0:T(8,128)(2,1)S(1)}, bf16[256,1024]{1,0:T(8,128)(2,1)S(1)}, u32[]{:S(2)}, u32[]{:S(2)}) collective-permute-start(bf16[256,1024]{1,0:T(8,128)(2,1)S(1)} %constant_dynamic-slice_fusion.14), channel_id=1, source_target_pairs={{0,4},{2,6},{4,0},{6,2},{8,12},{10,14},{12,8},{14,10},{16,20},{18,... | collective-permute-start | bytes 1572872 | tf_op jit(solution)/shard_map/ppermute | solution.py:119
  633.2 53.0 %collective-permute-start.39 = (bf16[512,1024]{1,0:T(8,128)(2,1)S(1)}, bf16[512,1024]{1,0:T(8,128)(2,1)S(1)}, u32[]{:S(2)}, u32[]{:S(2)}) collective-permute-start(bf16[512,1024]{1,0:T(8,128)(2,1)S(1)} %constant_dynamic-slice_fusion.11), channel_id=1, source_target_pairs={{0,8},{2,10},{4,12},{6,14},{8,0},{10,2},{12,4},{14,6},{16,24},{18,... | collective-permute-start | bytes 3145736 | tf_op jit(solution)/shard_map/ppermute | solution.py:119
  634.4 29.0 %collective-permute-start.25 = (bf16[256,1024]{1,0:T(8,128)(2,1)S(1)}, bf16[256,1024]{1,0:T(8,128)(2,1)S(1)}, u32[]{:S(2)}, u32[]{:S(2)}) collective-permute-start(bf16[256,1024]{1,0:T(8,128)(2,1)S(1)} %constant_dynamic-slice_fusion.17), channel_id=1, source_target_pairs={{0,2},{2,0},{4,6},{6,4},{8,10},{10,8},{12,14},{14,12},{16,18},{18,... | collective-permute-start | bytes 1572872 | tf_op jit(solution)/shard_map/ppermute | solution.py:119
  661.3 28.8 %collective-permute-start.33 = (bf16[256,1024]{1,0:T(8,128)(2,1)S(1)}, bf16[256,1024]{1,0:T(8,128)(2,1)S(1)}, u32[]{:S(2)}, u32[]{:S(2)}) collective-permute-start(bf16[256,1024]{1,0:T(8,128)(2,1)S(1)} %add_convert_fusion.25), channel_id=1, source_target_pairs={{0,16},{2,18},{4,20},{6,22},{8,24},{10,26},{12,28},{14,30},{16,0},... | collective-permute-start | bytes 1572872 | tf_op jit(solution)/shard_map/ppermute | solution.py:119
  663.4 24.9 %collective-permute-start.47 = (bf16[256,1024]{1,0:T(8,128)(2,1)S(1)}, bf16[256,1024]{1,0:T(8,128)(2,1)S(1)}, u32[]{:S(2)}, u32[]{:S(2)}) collective-permute-start(bf16[256,1024]{1,0:T(8,128)(2,1)S(1)} %constant_dynamic-slice_fusion.7), channel_id=1, source_target_pairs={{0,2},{2,0},{4,6},{6,4},{8,10},{10,8},{12,14},{14,12},{16,18},{18,... | collective-permute-start | bytes 1572872 | tf_op jit(solution)/shard_map/ppermute | solution.py:119
  686.2 36.2 %collective-permute-start.26 = (bf16[256,1024]{1,0:T(8,128)(2,1)S(1)}, bf16[256,1024]{1,0:T(8,128)(2,1)S(1)}, u32[]{:S(2)}, u32[]{:S(2)}) collective-permute-start(bf16[256,1024]{1,0:T(8,128)(2,1)S(1)} %add_convert_fusion.27), channel_id=1, source_target_pairs={{0,16},{2,18},{4,20},{6,22},{8,24},{10,26},{12,28},{14,30},{16,0},... | collective-permute-start | bytes 1572872 | tf_op jit(solution)/shard_map/ppermute | solution.py:119
  688.3 35.8 %collective-permute-start.40 = (bf16[256,1024]{1,0:T(8,128)(2,1)S(1)}, bf16[256,1024]{1,0:T(8,128)(2,1)S(1)}, u32[]{:S(2)}, u32[]{:S(2)}) collective-permute-start(bf16[256,1024]{1,0:T(8,128)(2,1)S(1)} %constant_dynamic-slice_fusion.10), channel_id=1, source_target_pairs={{0,4},{2,6},{4,0},{6,2},{8,12},{10,14},{12,8},{14,10},{16,20},{18,... | collective-permute-start | bytes 1572872 | tf_op jit(solution)/shard_map/ppermute | solution.py:119
  690.1 43.5 %collective-permute-start.48 = (bf16[256,1024]{1,0:T(8,128)(2,1)S(1)}, bf16[256,1024]{1,0:T(8,128)(2,1)S(1)}, u32[]{:S(2)}, u32[]{:S(2)}) collective-permute-start(bf16[256,1024]{1,0:T(8,128)(2,1)S(1)} %add_convert_fusion.21), channel_id=1, source_target_pairs={{0,16},{2,18},{4,20},{6,22},{8,24},{10,26},{12,28},{14,30},{16,0},... | collective-permute-start | bytes 1572872 | tf_op jit(solution)/shard_map/ppermute | solution.py:119
  722.4 13.8 %collective-permute-start.34 = (bf16[256,1024]{1,0:T(8,128)(2,1)S(1)}, bf16[256,1024]{1,0:T(8,128)(2,1)S(1)}, u32[]{:S(2)}, u32[]{:S(2)}) collective-permute-start(bf16[256,1024]{1,0:T(8,128)(2,1)S(1)} %add_convert_fusion.24), channel_id=1, source_target_pairs={{0,4},{2,6},{4,0},{6,2},{8,12},{10,14},{12,8},{14,10},{16,20},{18,... | collective-permute-start | bytes 1572872 | tf_op jit(solution)/shard_map/ppermute | solution.py:119
  724.1 15.0 %collective-permute-start.27 = (bf16[256,1024]{1,0:T(8,128)(2,1)S(1)}, bf16[256,1024]{1,0:T(8,128)(2,1)S(1)}, u32[]{:S(2)}, u32[]{:S(2)}) collective-permute-start(bf16[256,1024]{1,0:T(8,128)(2,1)S(1)} %add_convert_fusion.26), channel_id=1, source_target_pairs={{0,2},{2,0},{4,6},{6,4},{8,10},{10,8},{12,14},{14,12},{16,18},{18,... | collective-permute-start | bytes 1572872 | tf_op jit(solution)/shard_map/ppermute | solution.py:119
  733.5 24.0 %collective-permute-start.41 = (bf16[256,1024]{1,0:T(8,128)(2,1)S(1)}, bf16[256,1024]{1,0:T(8,128)(2,1)S(1)}, u32[]{:S(2)}, u32[]{:S(2)}) collective-permute-start(bf16[256,1024]{1,0:T(8,128)(2,1)S(1)} %add_convert_fusion.23), channel_id=1, source_target_pairs={{0,16},{2,18},{4,20},{6,22},{8,24},{10,26},{12,28},{14,30},{16,0},... | collective-permute-start | bytes 1572872 | tf_op jit(solution)/shard_map/ppermute | solution.py:119
  736.1 21.6 %collective-permute-start.49 = (bf16[256,1024]{1,0:T(8,128)(2,1)S(1)}, bf16[256,1024]{1,0:T(8,128)(2,1)S(1)}, u32[]{:S(2)}, u32[]{:S(2)}) collective-permute-start(bf16[256,1024]{1,0:T(8,128)(2,1)S(1)} %add_convert_fusion.20), channel_id=1, source_target_pairs={{0,2},{2,0},{4,6},{6,4},{8,10},{10,8},{12,14},{14,12},{16,18},{18,... | collective-permute-start | bytes 1572872 | tf_op jit(solution)/shard_map/ppermute | solution.py:119
  739.1 63.5 %collective-permute-start.35 = (bf16[512,1024]{1,0:T(8,128)(2,1)}, bf16[512,1024]{1,0:T(8,128)(2,1)}, u32[]{:S(2)}, u32[]{:S(2)}) collective-permute-start(bf16[512,1024]{1,0:T(8,128)(2,1)} %maximum_select_fusion.17), channel_id=1, source_target_pairs={{0,8},{2,10},{4,12},{6,14},{8,0},{10,2},{12,4},{14,6},{16,24},{18,... | collective-permute-start | bytes 3145736 | tf_op jit(solution)/shard_map/ppermute | solution.py:119
  757.5 41.7 %collective-permute-start.28 = (bf16[512,1024]{1,0:T(8,128)(2,1)}, bf16[512,1024]{1,0:T(8,128)(2,1)}, u32[]{:S(2)}, u32[]{:S(2)}) collective-permute-start(bf16[512,1024]{1,0:T(8,128)(2,1)} %maximum_select_fusion.16), channel_id=1, source_target_pairs={{0,8},{2,10},{4,12},{6,14},{8,0},{10,2},{12,4},{14,6},{16,24},{18,... | collective-permute-start | bytes 3145736 | tf_op jit(solution)/shard_map/ppermute | solution.py:119
  757.7 14.0 %collective-permute-start.42 = (bf16[256,1024]{1,0:T(8,128)(2,1)S(1)}, bf16[256,1024]{1,0:T(8,128)(2,1)}, u32[]{:S(2)}, u32[]{:S(2)}) collective-permute-start(bf16[256,1024]{1,0:T(8,128)(2,1)S(1)} %add_convert_fusion.22), channel_id=1, source_target_pairs={{0,4},{2,6},{4,0},{6,2},{8,12},{10,14},{12,8},{14,10},{16,20},{18,... | collective-permute-start | bytes 1572872 | tf_op jit(solution)/shard_map/ppermute | solution.py:119
  760.8 60.9 %collective-permute-start.50 = (bf16[512,1024]{1,0:T(8,128)(2,1)}, bf16[512,1024]{1,0:T(8,128)(2,1)}, u32[]{:S(2)}, u32[]{:S(2)}) collective-permute-start(bf16[512,1024]{1,0:T(8,128)(2,1)} %maximum_select_fusion.19), channel_id=1, source_target_pairs={{0,8},{2,10},{4,12},{6,14},{8,0},{10,2},{12,4},{14,6},{16,24},{18,... | collective-permute-start | bytes 3145736 | tf_op jit(solution)/shard_map/ppermute | solution.py:119
  771.7 43.1 %collective-permute-start.19 = (f32[12,512]{1,0:T(8,128)S(1)}, f32[12,512]{1,0:T(8,128)S(1)}, u32[]{:S(2)}, u32[]{:S(2)}) collective-permute-start(f32[12,512]{1,0:T(8,128)S(1)} %stack.125), channel_id=1, source_target_pairs={{0,2},{2,0},{4,6},{6,4},{8,10},{10,8},{12,14},{14,12},{16,18},{18,... | collective-permute-start | bytes 73736 | tf_op jit(solution)/shard_map/ppermute | solution.py:119
  799.2 61.5 %collective-permute-start.43 = (bf16[512,1024]{1,0:T(8,128)(2,1)S(1)}, bf16[512,1024]{1,0:T(8,128)(2,1)S(1)}, u32[]{:S(2)}, u32[]{:S(2)}) collective-permute-start(bf16[512,1024]{1,0:T(8,128)(2,1)S(1)} %maximum_select_fusion.18), channel_id=1, source_target_pairs={{0,8},{2,10},{4,12},{6,14},{8,0},{10,2},{12,4},{14,6},{16,24},{18,... | collective-permute-start | bytes 3145736 | tf_op jit(solution)/shard_map/ppermute | solution.py:119
  802.6 60.9 %collective-permute-start.29 = (bf16[1024,1024]{1,0:T(8,128)(2,1)S(1)}, bf16[1024,1024]{1,0:T(8,128)(2,1)S(1)}, u32[]{:S(2)}, u32[]{:S(2)}) collective-permute-start(bf16[1024,1024]{1,0:T(8,128)(2,1)S(1)} %maximum_select_fusion.10), channel_id=1, source_target_pairs={{0,4},{2,6},{4,0},{6,2},{8,12},{10,14},{12,8},{14,10},{16,20},{18,... | collective-permute-start | bytes 6291464 | tf_op jit(solution)/shard_map/ppermute | solution.py:119
  807.5 60.5 %collective-permute-start.36 = (bf16[1024,1024]{1,0:T(8,128)(2,1)S(1)}, bf16[1024,1024]{1,0:T(8,128)(2,1)S(1)}, u32[]{:S(2)}, u32[]{:S(2)}) collective-permute-start(bf16[1024,1024]{1,0:T(8,128)(2,1)S(1)} %maximum_select_fusion.11), channel_id=1, source_target_pairs={{0,2},{2,0},{4,6},{6,4},{8,10},{10,8},{12,14},{14,12},{16,18},{18,... | collective-permute-start | bytes 6291464 | tf_op jit(solution)/shard_map/ppermute | solution.py:119
  814.8 37.2 %collective-permute-start.20 = (f32[12,512]{1,0:T(8,128)S(1)}, f32[12,512]{1,0:T(8,128)S(1)}, u32[]{:S(2)}, u32[]{:S(2)}) collective-permute-start(f32[12,512]{1,0:T(8,128)S(1)} %add.444), channel_id=1, source_target_pairs={{0,4},{2,6},{4,0},{6,2},{8,12},{10,14},{12,8},{14,10},{16,20},{18,... | collective-permute-start | bytes 73736 | tf_op jit(solution)/shard_map/ppermute | solution.py:119
  825.0 66.5 %collective-permute-start.51 = (bf16[1024,1024]{1,0:T(8,128)(2,1)S(1)}, bf16[1024,1024]{1,0:T(8,128)(2,1)S(1)}, u32[]{:S(2)}, u32[]{:S(2)}) collective-permute-start(bf16[1024,1024]{1,0:T(8,128)(2,1)S(1)} %maximum_select_fusion.13), channel_id=1, source_target_pairs={{0,4},{2,6},{4,0},{6,2},{8,12},{10,14},{12,8},{14,10},{16,20},{18,... | collective-permute-start | bytes 6291464 | tf_op jit(solution)/shard_map/ppermute | solution.py:119
  852.0 3.9 collective-permute-start.21
  855.9 4.8 collective-permute-start.22
  861.7 35.1 %collective-permute-start.44 = (bf16[1024,1024]{1,0:T(8,128)(2,1)S(1)}, bf16[1024,1024]{1,0:T(8,128)(2,1)S(1)}, u32[]{:S(2)}, u32[]{:S(2)}) collective-permute-start(bf16[1024,1024]{1,0:T(8,128)(2,1)S(1)} %maximum_select_fusion.12), channel_id=1, source_target_pairs={{0,2},{2,0},{4,6},{6,4},{8,10},{10,8},{12,14},{14,12},{16,18},{18,... | collective-permute-start | bytes 6291464 | tf_op jit(solution)/shard_map/ppermute | solution.py:119
  (78 other events, 928.9 us)

commit v2 on v1

v2 whole, which is shorter than its diff:
```python
import functools
import math

import jax
import jax.numpy as jnp
from jax import lax
from jax.experimental import pallas as pl
from jax.experimental.pallas import tpu as pltpu
from jax.sharding import PartitionSpec as P

H = 8
DH = 128
KER = 5
RIM = (KER - 1) // 2
EPS = 1e-05
NEG = -1e30
BF = jnp.bfloat16
F32 = jnp.float32
VMEM = 56 * 1024 * 1024
PLAN = ("", "a", "", "a", "a", "", "ba", "a", "bcab", "c", "b", "cdbac", "dc", "bedc", "eedb", "feescfdscfesdfesfdfsdf")


def dot(a, b, da=1, db=0):
    return lax.dot_general(a, b, (((da,), (db,)), ((), ())), preferred_element_type=F32)


def norm_parts(v):
    centred = v - jnp.mean(v, axis=-1, keepdims=True)
    rstd = lax.rsqrt(jnp.mean(centred * centred, axis=-1, keepdims=True) + EPS)
    return centred * rstd, rstd


def norm_back(grad, hat, rstd, gain):
    scaled = grad * gain
    first = jnp.mean(scaled, axis=-1, keepdims=True)
    second = jnp.mean(scaled * hat, axis=-1, keepdims=True)
    return rstd * (scaled - first - hat * second)


def slope(v):
    s = jax.nn.sigmoid(v)
    return s * (1.0 + v * (1.0 - s))


def shifted(v, s):
    g = lax.axis_size("fsdp")
    return lax.ppermute(v, "fsdp", [(i, (i + s) % g) for i in range(g)])


def natural(blocks):
    g = len(blocks)
    me = lax.axis_index("fsdp")
    if g == 1:
        return blocks[0][None]
    if g == 2:
        a, b = blocks
        return jnp.where(me == 0, jnp.stack([a, b]), jnp.stack([b, a]))
    stacked = jnp.stack(blocks[::-1])
    return jnp.roll(stacked, me + 1, axis=0)


def gather_rows(v, place):
    g = lax.axis_size("fsdp")
    if g == 2:
        return placed(place, v, shifted(v, 1))
    out = natural([v] + [shifted(v, s) for s in range(1, g)])
    return out.reshape((g * v.shape[0],) + v.shape[1:])


def pair_swap(v):
    g = lax.axis_size("fsdp")
    if g == 2:
        return lax.all_to_all(v, "fsdp", 0, 0)
    other = pair_other(v[0])
    return jnp.stack([other, other])


def pair_other(v):
    g = lax.axis_size("fsdp")
    if g == 2:
        return shifted(v, 1)
    return sum(shifted(v, s).astype(F32) for s in range(1, g))


def row_blocks_swap(v):
    g = lax.axis_size("fsdp")
    n = v.shape[0] // g
    return lax.all_to_all(v.reshape(g, n, v.shape[1]), "fsdp", 0, 0)


def own_columns(matrices):
    g = lax.axis_size("fsdp")
    me = lax.axis_index("fsdp")

    def columns(member):
        parts = []
        for m, width in matrices:
            parts.append(lax.dynamic_slice_in_dim(m, member * width, width, 1))
        return jnp.concatenate(parts, axis=1)

    blocks = [columns(me)]
    for s in range(1, g):
        blocks.append(shifted(columns(lax.rem(me + s, g)), s))
    return blocks


def bit_of(b):
    return (lax.axis_index("batch") >> b) & 1


def exchange(v, b):
    n = lax.axis_size("batch")
    return lax.ppermute(v, "batch", [(i, i ^ (1 << b)) for i in range(n)])


def is_power(n):
    return n & (n - 1) == 0


def row_sum(v):
    n = lax.axis_size("batch")
    if not is_power(n):
        return lax.psum(v, "batch")
    for b in range(n.bit_length() - 1):
        v = v + exchange(v, b)
    return v


def add16(a, b):
    return (a.astype(F32) + b.astype(F32)).astype(BF)


def halves(v, b):
    half = v.shape[0] // 2
    mine = bit_of(b)
    keep = lax.dynamic_slice_in_dim(v, mine * half, half, 0)
    return keep, lax.dynamic_slice_in_dim(v, (1 - mine) * half, half, 0)


def joined(v, other, b):
    low, high = jnp.concatenate([v, other], 0), jnp.concatenate([other, v], 0)
    return jnp.where(bit_of(b) == 1, high, low)


class Sequence:
    def __init__(self):
        self.last = None

    def run(self, step, *inputs):
        if self.last is not None:
            *inputs, _ = lax.optimization_barrier((*inputs, self.last))
        outputs = step(*inputs)
        leaves = jax.tree.leaves(outputs)
        self.last = leaves[0] if leaves else self.last
        return outputs


    def tie(self, *values):
        if self.last is None:
            return values
        return lax.optimization_barrier((*values, self.last))[:-1]


class BatchSum:
    def __init__(self, sequence, arrays, parts=None):
        self.sequence = sequence
        self.parts = parts
        self.sizes = arrays if parts is not None else [a.shape[0] for a in arrays]
        self.arrays = arrays
        bits = lax.axis_size("batch").bit_length() - 1
        rest = list(range(3, bits))
        self.bits = list(zip([0, 2, 1] + rest, [1, 2, 0] + rest, strict=True))
        self.event = 0
        self.out = None

    def send(self, k, pair):
        a, b = self.bits[k]
        if a == b:
            got = exchange(pair, a)
            return got[0], got[1]
        return exchange(pair[0], a), exchange(pair[1], b)

    def launch(self, k, now):
        a, b = self.bits[k]
        parts = [halves(now[0], a), halves(now[1], b)]
        keep, away = tuple(p[0] for p in parts), tuple(p[1] for p in parts)
        return keep, (jnp.stack(away) if a == b else away)

    def step(self):
        e, n = self.event, len(self.bits)
        self.event += 1
        if e == 0 and self.parts is not None:
            self.keep, away = self.parts
            self.got = self.send(0, away)
        elif e == 0:

            def first(*arrays):
                whole = jnp.concatenate(arrays, 0) if len(arrays) > 1 else arrays[0]
                half = whole.shape[0] // 2
                return self.launch(0, (whole[:half], whole[half:]))

            self.keep, away = self.sequence.run(first, *self.arrays)
            self.got = self.send(0, away)
        elif e < n:

            def add(k0, k1, g0, g1):
                now = (add16(k0, g0), add16(k1, g1))
                if e < n - 1:
                    return self.launch(e, now)
                return (jnp.stack(now),)

            out = self.sequence.run(add, *self.keep, *self.got)
            if e < n - 1:
                self.keep, away = out
                self.got = self.send(e, away)
            else:
                self.keep = out[0]
                self.got = exchange(self.keep, self.bits[e][0])
        elif e == n:

            def last(k, g):
                now = add16(k, g)
                return self.spread(n - 2, (now[0], now[1]))

            now = self.sequence.run(last, self.keep, self.got)
            self.forward(n - 2, now)
        elif e < 2 * n - 1:
            k = 2 * n - 2 - e

            def more(c0, c1, g0, g1):
                a, b = self.bits[k + 1]
                return self.spread(k, (joined(c0, g0, a), joined(c1, g1, b)))

            now = self.sequence.run(more, *self.now, *self.got)
            self.forward(k, now)
        else:

            def final(c0, c1, g0, g1):
                a, b = self.bits[0]
                whole = jnp.concatenate([joined(c0, g0, a), joined(c1, g1, b)], 0)
                out, at = [], 0
                for size in self.sizes:
                    out.append(whole[at : at + size].astype(F32))
                    at += size
                return out

            self.out = self.sequence.run(final, *self.now, *self.got)

    def spread(self, k, now):
        a, b = self.bits[k]
        return jnp.stack(now) if a == b else now

    def forward(self, k, now):
        self.now = (now[0], now[1])
        self.got = self.send(k, now)

    def finish(self):
        while self.out is None:
            self.step()
        return self.out


class SmallSum:
    def __init__(self, sequence, v):
        self.sequence = sequence
        self.v = v
        self.bit = 0
        self.got = exchange(v, 0)
        self.bits = lax.axis_size("batch").bit_length() - 1

    def step(self):
        if self.bit == self.bits:
            return
        self.v = self.sequence.run(lambda a, b: a + b, self.v, self.got)
        self.bit += 1
        if self.bit < self.bits:
            self.got = exchange(self.v, self.bit)

    def finish(self):
        while self.bit < self.bits:
            self.step()
        return self.v


ROWS = 256
CHEAP = pl.CostEstimate(flops=1, bytes_accessed=1, transcendentals=0)


def launch(kernel, name, steps, place, ins, outs, scratch=()):
    return pl.pallas_call(
        kernel,
        grid_spec=pltpu.PrefetchScalarGridSpec(
            num_scalar_prefetch=1,
            grid=(steps,),
            in_specs=[spec for _, spec in ins],
            out_specs=[spec for _, _, spec in outs],
            scratch_shapes=list(scratch),
        ),
        out_shape=[jax.ShapeDtypeStruct(shape, kind) for shape, kind, _ in outs],
        compiler_params=pltpu.CompilerParams(vmem_limit_bytes=VMEM),
        cost_estimate=CHEAP,
        name=name,
    )(place, *[a for a, _ in ins])


def whole(shape):
    return pl.BlockSpec(tuple(shape), lambda i, place: (0,) * len(shape))


def all_of(a):
    return a, whole(a.shape)


def blocks_of(shape, lag=0):
    last = shape[0] // ROWS - 1
    return pl.BlockSpec((ROWS, shape[1]), lambda i, place: (jnp.clip(i - lag, 0, last), 0))


def by_rows(a, lag=0):
    return a, blocks_of(a.shape, lag)


def out_rows(shape, kind, lag=0):
    return shape, kind, blocks_of(shape, lag)


def out_twice(shape, kind, lag=0):
    last = shape[0] // ROWS - 1
    spec = pl.BlockSpec((2, ROWS, shape[1]), lambda i, place: (0, jnp.clip(i - lag, 0, last), 0))
    return (2, *shape), kind, spec


def two_parts(part, other):
    last = part.shape[1] // ROWS - 1
    block = (None, ROWS, part.shape[2])
    return [
        (part, pl.BlockSpec(block, lambda i, place: (0, jnp.minimum(i, last), 0))),
        (other, pl.BlockSpec(block, lambda i, place: (place[0], jnp.minimum(i, last), 0))),
    ]


def out_all(shape, kind):
    return shape, kind, whole(shape)


def columns_of(place, s, width):
    return pl.ds(pl.multiple_of(place[8 + s] * width, width), width)


def first_step(*refs):
    @pl.when(pl.program_id(0) == 0)
    def _():
        for ref in refs:
            ref[...] = jnp.zeros_like(ref)


def last_step():
    return pl.program_id(0) == pl.num_programs(0) - 1


def wide(*refs):
    return [ref[...].astype(F32) for ref in refs]


def placed_kernel(place, own, other, out):
    @pl.when(pl.program_id(0) == 0)
    def _():
        out[...] = own[...]

    @pl.when(pl.program_id(0) == 1)
    def _():
        out[...] = other[...]


def placed(place, own, other):
    n, d = own.shape
    spec = pl.BlockSpec((n, d), lambda i, place: ((place[0] + 1 + i) % 2, 0))
    ins, outs = [all_of(own), all_of(other)], [((2 * n, d), own.dtype, spec)]
    return launch(placed_kernel, "placed", 2, place, ins, outs)[0]


def pack_kernel(place, *refs):
    half = len(refs) // 2 - 1
    own, away = refs[-2:]
    width = refs[0].shape[1]
    for j in range(half):
        columns = slice(j * width, (j + 1) * width)
        own[:, columns] = refs[j][...]
        away[:, columns] = refs[half + j][...]


def packed(place, matrices):
    n = matrices[0][0].shape[0]
    width = matrices[0][2]

    def part(m, first, mine):
        def at(i, place):
            member = (place[0] + 1) % 2 if mine else place[0]
            return (0, first + member)

        return m, pl.BlockSpec((n, width), at)

    ins = [part(m, first, mine) for mine in (True, False) for m, first, _ in matrices]
    outs = [((n, len(matrices) * width), BF, whole((n, len(matrices) * width)))] * 2
    return launch(pack_kernel, "packed", 1, place, ins, outs)


def ffn_forward_kernel(place, *refs, joined):
    if joined:
        base, p, r, gain, up, down, x_ref, part, pre, u_ref = refs
        a, b, c = wide(base, p, r)
        x = a + (b + c)
        x_ref[...] = x
    else:
        base, gain, up, down, part, pre, u_ref = refs
        (x,) = wide(base)
    u = (norm_parts(x)[0] * gain[...]).astype(BF)
    u_ref[...] = u
    chunk = min(1024, up.shape[0])
    total = None
    for c in range(0, up.shape[0], chunk):
        a = dot(u, up[c : c + chunk, :], 1, 1)
        pre[:, c : c + chunk] = a.astype(BF)
        h = (a * jax.nn.sigmoid(a)).astype(BF)
        f = dot(h, down[c : c + chunk, :])
        total = f if total is None else total + f
    part[...] = total.astype(BF)


def ffn_forward(place, base, pair, gain, up, down):
    t, d = base.shape
    hid = up.shape[0]
    ins = [by_rows(base)] + [by_rows(v) for v in pair] + [all_of(gain[None]), all_of(up), all_of(down)]
    outs = [out_rows((t, d), BF), out_rows((t, hid), BF), out_rows((t, d), BF)]
    if pair:
        outs = [out_rows((t, d), F32)] + outs
    kernel = functools.partial(ffn_forward_kernel, joined=bool(pair))
    return launch(kernel, "ffn_forward", t // ROWS, place, ins, outs)


def qkv_kernel(place, base, p, r, gain, content, position, *refs, groups):
    blocks, (x_ref, ua, qc, qp, k, v) = refs[:groups], refs[groups:]
    a, b, c = wide(base, p, r)
    x = a + 0.5 * (b + c)
    x_ref[...] = x
    ua[...] = (norm_parts(x)[0] * gain[...]).astype(BF)
    n = blocks[0].shape[0]
    all3 = sum(dot(ua[:, columns_of(place, s, n)], w[...]) for s, w in enumerate(blocks))
    part = qc.shape[1]
    q = all3[:, :part]
    qc[...] = (q + content[...]).astype(BF)
    qp[...] = (q + position[...]).astype(BF)
    k[...] = all3[:, part : 2 * part].astype(BF)
    v[...] = all3[:, 2 * part :].astype(BF)


def weight_blocks(blocks, width, at):
    return [(w, pl.BlockSpec((w.shape[0], width), lambda i, place: (0, at))) for w in blocks]


def qkv_forward(place, base, p, r, gain, content, position, blocks):
    t, d = base.shape
    part = content.shape[0]
    ins = [by_rows(base), by_rows(p), by_rows(r)]
    ins += [all_of(v[None]) for v in (gain, content, position)] + weight_blocks(blocks, 3 * part, 1)
    outs = [out_rows((t, d), F32), out_rows((t, d), BF)] + [out_rows((t, part), BF)] * 4
    kernel = functools.partial(qkv_kernel, groups=len(blocks))
    return launch(kernel, "qkv", t // ROWS, place, ins, outs)


def turned(rows, length):
    return pl.ds(pl.multiple_of(lax.rem(length - pl.program_id(0) * rows, length), rows), length)


def fill_twice(twice_ref, pos_ref):
    length = pos_ref.shape[0]

    @pl.when(pl.program_id(0) == 0)
    def _():
        twice_ref[:length, :] = pos_ref[...]
        twice_ref[length:, :] = pos_ref[...]


def exponentials(same, qc, qp, k, pos):
    far = pltpu.roll(dot(qp, pos, 1, 1), 0, 1, stride=1, stride_axis=0)
    z = jnp.where(same, dot(qc, k, 1, 1) + far, NEG)
    e = jnp.exp2((z - jnp.max(z, axis=1, keepdims=True)) * (math.log2(math.e) / math.sqrt(DH)))
    return e, 1.0 / jnp.sum(e, axis=1, keepdims=True)


def attention_kernel(place, segq, segk, qc, qp, k, v, pos, out_w, ctx, part, twice):
    fill_twice(twice, pos)
    at = turned(qc.shape[0], k.shape[0])
    same = segq[...] == segk[...]
    for h in range(qc.shape[1] // DH):
        c = slice(h * DH, (h + 1) * DH)
        e, inverse = exponentials(same, qc[:, c], qp[:, c], k[:, c], twice[at, c])
        ctx[:, c] = (dot(e.astype(BF), v[:, c]) * inverse).astype(BF)
    part[...] = dot(ctx[...], out_w[...]).astype(BF)


def attention(place, seg, qc, qp, k, v, pos, out_w):
    t, width = qc.shape
    d = out_w.shape[1]
    ins = [by_rows(seg[:, None]), all_of(seg[None]), by_rows(qc), by_rows(qp)]
    ins += [all_of(a) for a in (k, v, pos, out_w)]
    outs = [out_rows((t, width), BF), out_rows((t, d), BF)]
    scratch = [pltpu.VMEM((2 * t, width), BF)]
    return launch(attention_kernel, "attention_forward", t // ROWS, place, ins, outs, scratch)


def attention_back_kernel(
    place, segq, segk, qc, qp, k, v, pos, gctx,
    gq, gk, gv, gpos, content, position, gk_acc, gv_acc, twice, gpos_acc,
):
    rows, length = qc.shape[0], k.shape[0]
    first_step(gk_acc, gv_acc, gpos_acc, content, position)
    fill_twice(twice, pos)
    at = turned(rows, length)
    same = segq[...] == segk[...]
    at_row = lax.broadcasted_iota(jnp.int32, (rows, rows), 0)
    at_col = lax.broadcasted_iota(jnp.int32, (rows, rows), 1)
    flip = jnp.where(at_row + at_col == rows - 1, 1.0, 0.0).astype(BF)
    for h in range(qc.shape[1] // DH):
        c = slice(h * DH, (h + 1) * DH)
        near = twice[at, c]
        e, inverse = exponentials(same, qc[:, c], qp[:, c], k[:, c], near)
        prob = e * inverse
        gout = gctx[:, c]
        gprob = dot(gout, v[:, c], 1, 1)
        gv_acc[:, c] += dot(prob.astype(BF), gout, 0, 0)
        inner = jnp.sum(prob * gprob, axis=1, keepdims=True)
        gz = (prob * (gprob - inner) * (1.0 / math.sqrt(DH))).astype(BF)
        gqc = dot(gz, k[:, c])
        gk_acc[:, c] += dot(gz, qc[:, c], 0, 0)
        skew = pltpu.roll(dot(flip, gz), length - rows + 1, 1, stride=1, stride_axis=0).astype(BF)
        gqp = dot(skew, near)
        gpos_acc[at, c] += dot(skew, dot(flip, qp[:, c]).astype(BF), 0, 0)
        gq[:, c] = (gqc + dot(flip, gqp.astype(BF))).astype(BF)
        content[:, c] += jnp.sum(gqc, axis=0, keepdims=True)
        position[:, c] += jnp.sum(gqp, axis=0, keepdims=True)

    @pl.when(last_step())
    def _():
        gk[...] = gk_acc[...].astype(BF)
        gv[...] = gv_acc[...].astype(BF)
        gpos[...] = gpos_acc[:length, :] + gpos_acc[length:, :]


def attention_back(place, seg, qc, qp, k, v, pos, gctx, first):
    t, width = qc.shape
    if (width // DH) % 2 == 0:
        width //= 2
    elif not first:
        return None
    at = 0 if first else 1

    def columns(a, rows):
        return a, pl.BlockSpec((rows, width), lambda i, place: (i if rows < t else 0, at))

    ins = [by_rows(seg[:, None]), all_of(seg[None]), columns(qc, ROWS), columns(qp, ROWS)]
    ins += [columns(a, t) for a in (k, v, pos)] + [columns(gctx, ROWS)]
    outs = [out_rows((t, width), BF), out_all((t, width), BF), out_all((t, width), BF)]
    outs += [out_all((t, width), F32), out_all((1, width), F32), out_all((1, width), F32)]
    scratch = [pltpu.VMEM((t, width), F32)] * 2
    scratch += [pltpu.VMEM((2 * t, width), BF), pltpu.VMEM((2 * t, width), F32)]
    return launch(attention_back_kernel, "attention_back", t // ROWS, place, ins, outs, scratch)


EDGE = 8


def window(ref, block):
    return ref[pl.ds(pl.multiple_of(block * ROWS, ROWS), ROWS + 2 * EDGE), :]


def taken(rows, o):
    return rows[EDGE - RIM + o : EDGE - RIM + o + ROWS, :]


def keep_block(ref, block, rows):
    ref[pl.ds(pl.multiple_of(block * ROWS + EDGE, EDGE), ROWS), :] = rows


def clear_edges(*refs):
    @pl.when(pl.program_id(0) == 0)
    def _():
        for ref in refs:
            zero = jnp.zeros((EDGE, ref.shape[1]), ref.dtype)
            ref[:EDGE, :] = zero
            ref[ref.shape[0] - EDGE :, :] = zero


def conv_forward_kernel(place, base, p, r, gain, link, valid, taps, *refs, groups):
    blocks, (x_ref, uc, gp, dc, sums, glu) = refs[:groups], refs[groups:]
    i = pl.program_id(0)
    clear_edges(glu)
    first_step(sums)

    @pl.when(i < pl.num_programs(0) - 1)
    def _():
        a, b, c = wide(base, p, r)
        x = a + (b + c)
        x_ref[...] = x
        uc[...] = (norm_parts(x)[0] * gain[...]).astype(BF)
        n = blocks[0].shape[0]
        both = sum(dot(uc[:, columns_of(place, s, n)], w[...]) for s, w in enumerate(blocks))
        gp[...] = both.astype(BF)
        part = both.shape[1] // 2
        keep_block(glu, i, both[:, :part] * jax.nn.sigmoid(both[:, part:]))

    @pl.when(i > 0)
    def _():
        rows = window(glu, i - 1)
        out = sum(
            taken(rows, o) * (link[:, o : o + 1] * taps[o : o + 1, :]) for o in range(KER)
        )
        dc[...] = out
        counted = valid[...] * out
        sums[0:1, :] += jnp.sum(counted, axis=0, keepdims=True)
        sums[1:2, :] += jnp.sum(counted * out, axis=0, keepdims=True)
        sums[2:3, :] += jnp.sum(valid[...])


def conv_forward(place, base, p, r, gain, link, valid, taps, blocks):
    t, d = base.shape
    part = taps.shape[1]
    ins = [by_rows(base), by_rows(p), by_rows(r), all_of(gain[None])]
    ins += [by_rows(link, 1), by_rows(valid, 1), all_of(taps)] + weight_blocks(blocks, 2 * part, 0)
    outs = [out_rows((t, d), F32), out_rows((t, d), BF), out_rows((t, 2 * part), BF)]
    outs += [out_rows((t, part), F32, 1), out_all((3, part), F32)]
    kernel = functools.partial(conv_forward_kernel, groups=len(blocks))
    scratch = [pltpu.VMEM((t + 2 * EDGE, part), F32)]
    return launch(kernel, "conv_forward", t // ROWS + 1, place, ins, outs, scratch)


def batch_moments(sums):
    count = sums[2:3, :]
    mu = sums[0:1, :] / count
    return mu, lax.rsqrt(sums[1:2, :] / count - mu * mu + EPS), count


def batch_forward_kernel(place, dc, sums, gain, shift, out_w, sw, part):
    mu, rstd, _ = batch_moments(sums)
    bo = (dc[...] - mu) * rstd * gain[...] + shift[...]
    sw[...] = (bo * jax.nn.sigmoid(bo)).astype(BF)
    part[...] = dot(sw[...], out_w[...]).astype(BF)


def batch_forward(place, dc, sums, gain, shift, out_w):
    t, part = dc.shape
    d = out_w.shape[1]
    ins = [by_rows(dc), all_of(sums), all_of(gain[None]), all_of(shift[None]), all_of(out_w)]
    outs = [out_rows((t, part), BF), out_rows((t, d), BF)]
    return launch(batch_forward_kernel, "batch_forward", t // ROWS, place, ins, outs)


def back_step(g, p, r, x, gain, gg):
    gu, other = wide(p, r)
    gu = gu + other
    hat, rstd = norm_parts(x[...].astype(F32))
    gg[...] += jnp.sum(gu * hat, axis=0, keepdims=True)
    return g[...] + norm_back(gu, hat, rstd, gain[...])


def hidden_grad(pre, gf):
    a = pre[...].astype(F32)
    return dot((a * jax.nn.sigmoid(a)).astype(BF), gf[...], 0, 0).astype(BF)


def store_at(steps, refs, make):
    for j, ref in enumerate(refs):

        @pl.when(pl.program_id(0) == steps + j)
        def _(ref=ref):
            ref[...] = make()


def final_kernel(place, x, p, r, cot, gain, pre, layer, g, gf, gg, *sends):
    steps = gf.shape[0] // ROWS
    first_step(gg)
    i = pl.program_id(0)

    @pl.when(i < steps)
    def _():
        a, b, c, y = wide(x, p, r, cot)
        hat, rstd = norm_parts(a + 0.5 * (b + c))
        layer[...] = (hat * gain[...]).astype(BF)
        gg[...] += jnp.sum(y * hat, axis=0, keepdims=True)
        new = norm_back(y, hat, rstd, gain[...])
        g[...] = new
        gf[pl.ds(pl.multiple_of(i * ROWS, ROWS), ROWS), :] = (0.5 * new).astype(BF)

    store_at(steps, sends, lambda: hidden_grad(pre, gf))


def hidden_blocks(pre, steps):
    quarter = pre.shape[1] // 4
    return pre, pl.BlockSpec(
        (pre.shape[0], quarter), lambda i, place: (0, place[4 + jnp.clip(i - steps, 0, 3)])
    )


def final_down(place, x, p, r, cot, gain, pre):
    t, d = x.shape
    n = t // ROWS
    ins = [by_rows(x), by_rows(p), by_rows(r), by_rows(cot), all_of(gain[None])]
    ins += [hidden_blocks(pre, n)]
    outs = [out_rows((t, d), BF), out_rows((t, d), F32), out_all((t, d), BF), out_all((1, d), F32)]
    outs += [out_all((pre.shape[1] // 4, d), BF)] * 2
    return launch(final_kernel, "final_down", n + 2, place, ins, outs)


def keep_kernel(place, gf, pre, *keeps):
    store_at(0, keeps, lambda: hidden_grad(pre, gf))


def down_keep(place, gf, pre):
    d = gf.shape[1]
    ins = [all_of(gf), hidden_blocks(pre, -2)]
    outs = [out_all((pre.shape[1] // 4, d), BF)] * 2
    return launch(keep_kernel, "down_keep", 2, place, ins, outs)


def back_down_kernel(place, p, r, g, x, gain, pre, g_ref, gf, gg, *sends):
    steps = gf.shape[0] // ROWS
    first_step(gg)
    i = pl.program_id(0)

    @pl.when(i < steps)
    def _():
        new = back_step(g, p, r, x, gain, gg)
        g_ref[...] = new
        gf[pl.ds(pl.multiple_of(i * ROWS, ROWS), ROWS), :] = (0.5 * new).astype(BF)

    store_at(steps, sends, lambda: hidden_grad(pre, gf))


def back_down(place, p, r, g, x, gain, pre):
    t, d = x.shape
    n = t // ROWS
    ins = two_parts(p, r) + [by_rows(g), by_rows(x), all_of(gain[None]), hidden_blocks(pre, n)]
    outs = [out_rows((t, d), F32), out_all((t, d), BF), out_all((1, d), F32)]
    outs += [out_all((pre.shape[1] // 4, d), BF)] * 4
    return launch(back_down_kernel, "back_down", n + 4, place, ins, outs)


def ffn_back_kernel(place, gf, pre, up, down, part, ga):
    chunk = min(1024, up.shape[0])
    total = None
    for c in range(0, up.shape[0], chunk):
        gh = dot(gf[...], down[c : c + chunk, :], 1, 1)
        now = (gh * slope(pre[:, c : c + chunk].astype(F32))).astype(BF)
        ga[:, c : c + chunk] = now
        f = dot(now, up[c : c + chunk, :])
        total = f if total is None else total + f
    part[0] = part[1] = total.astype(BF)


def ffn_back(place, gf, pre, up, down):
    t, d = gf.shape
    hid = up.shape[0]
    ins = [by_rows(gf), by_rows(pre), all_of(up), all_of(down)]
    outs = [out_twice((t, d), BF), out_rows((t, hid), BF)]
    return launch(ffn_back_kernel, "ffn_back", t // ROWS, place, ins, outs)


def up_grad_kernel(place, ga, u, *refs):
    store_at(0, refs, lambda: dot(ga[...], u[...], 0, 0).astype(BF))


def up_grad(place, ga, u):
    d = u.shape[1]
    ins = [hidden_blocks(ga, 0), all_of(u)]
    outs = [out_all((ga.shape[1] // 4, d), BF)] * 4
    return launch(up_grad_kernel, "up_grad", 4, place, ins, outs)


def conv_back_one_kernel(
    place, p, r, g, x, gain, dc, sw, sums, bgain, bshift, out_w, g_ref, gg, gbo, ab, grad, acc
):
    first_step(gg, ab, acc)
    new = back_step(g, p, r, x, gain, gg)
    g_ref[...] = new
    low = new.astype(BF)
    mu, rstd, _ = batch_moments(sums)
    hat = (dc[...] - mu) * rstd
    back = dot(low, out_w[...], 1, 1) * slope(hat * bgain[...] + bshift[...])
    gbo[...] = back
    ab[0:1, :] += jnp.sum(back, axis=0, keepdims=True)
    ab[1:2, :] += jnp.sum(back * hat, axis=0, keepdims=True)
    acc[...] += dot(sw[...], low, 0, 0)

    @pl.when(last_step())
    def _():
        grad[...] = acc[...].astype(BF)


def conv_back_one(place, p, r, g, x, gain, dc, sw, sums, bgain, bshift, out_w):
    t, d = x.shape
    part = dc.shape[1]
    ins = two_parts(p, r) + [by_rows(g), by_rows(x), all_of(gain[None]), by_rows(dc)]
    ins += [by_rows(sw), all_of(sums), all_of(bgain[None]), all_of(bshift[None]), all_of(out_w)]
    outs = [out_rows((t, d), F32), out_all((1, d), F32), out_rows((t, part), F32)]
    outs += [out_all((2, part), F32), out_all((part, d), BF)]
    scratch = [pltpu.VMEM((part, d), F32)]
    return launch(conv_back_one_kernel, "conv_back_one", t // ROWS, place, ins, outs, scratch)


def conv_back_two_kernel(
    place, gbo, dc, gp, gp_lag, uc, link, valid, sums, ab, bgain, taps, *refs, groups
):
    blocks, (part, grad, taps_grad, gdc_s, glu_s, acc) = refs[:groups], refs[groups:]
    i = pl.program_id(0)
    width = dc.shape[1]
    clear_edges(gdc_s, glu_s)
    first_step(taps_grad, acc)

    @pl.when(i < pl.num_programs(0) - 1)
    def _():
        mu, rstd, count = batch_moments(sums)
        scaled = rstd * bgain[...]
        gvar = -0.5 * rstd * scaled * ab[1:2, :]
        mean_part = (-scaled * ab[0:1, :] - 2.0 * mu * gvar) / count
        slope_part = 2.0 * gvar / count
        gdc = gbo[...] * scaled + valid[...] * (mean_part + dc[...] * slope_part)
        keep_block(gdc_s, i, gdc)
        both = gp[...].astype(F32)
        keep_block(glu_s, i, both[:, :width] * jax.nn.sigmoid(both[:, width:]))

    @pl.when(i > 0)
    def _():
        gdc_rows, glu_rows = window(gdc_s, i - 1), window(glu_s, i - 1)
        middle = taken(gdc_rows, RIM)
        gglu = None
        for o in range(KER):
            linked = link[:, o : o + 1]
            mirror = KER - 1 - o
            term = taken(gdc_rows, o) * (linked * taps[mirror : mirror + 1, :])
            gglu = term if gglu is None else gglu + term
            taps_grad[o : o + 1, :] += jnp.sum(
                middle * (taken(glu_rows, o) * linked), axis=0, keepdims=True
            )
        both = gp_lag[...].astype(F32)
        opener = jax.nn.sigmoid(both[:, width:])
        first = gglu * opener
        second = first * both[:, :width] * (1.0 - opener)
        ggp = jnp.concatenate([first.astype(BF), second.astype(BF)], axis=1)
        n = blocks[0].shape[0]
        for s, w in enumerate(blocks):
            columns = columns_of(place, s, n)
            part[0, :, columns] = part[1, :, columns] = dot(ggp, w[...], 1, 1).astype(BF)
        acc[...] += dot(uc[...], ggp, 0, 0)

    @pl.when(last_step())
    def _():
        grad[...] = acc[...].astype(BF)


def conv_back_two(place, gbo, dc, gp, uc, link, valid, sums, ab, bgain, taps, blocks):
    t, d = uc.shape
    part = dc.shape[1]
    ins = [by_rows(gbo), by_rows(dc), by_rows(gp), by_rows(gp, 1), by_rows(uc, 1), by_rows(link, 1)]
    ins += [by_rows(valid), all_of(sums), all_of(ab), all_of(bgain[None]), all_of(taps)]
    ins += weight_blocks(blocks, 2 * part, 0)
    outs = [out_twice((t, d), BF, 1), out_all((d, 2 * part), BF), out_all((KER, part), F32)]
    scratch = [pltpu.VMEM((t + 2 * EDGE, part), F32)] * 2 + [pltpu.VMEM((d, 2 * part), F32)]
    kernel = functools.partial(conv_back_two_kernel, groups=len(blocks))
    return launch(kernel, "conv_back_two", t // ROWS + 1, place, ins, outs, scratch)


def context_back_kernel(place, p, r, g, x, gain, ctx, out_w, g_ref, gg, gctx, grad, acc):
    first_step(gg, acc)
    new = back_step(g, p, r, x, gain, gg)
    g_ref[...] = new
    low = new.astype(BF)
    gctx[...] = dot(low, out_w[...], 1, 1).astype(BF)
    acc[...] += dot(ctx[...], low, 0, 0)

    @pl.when(last_step())
    def _():
        grad[...] = acc[...].astype(BF)


def context_back(place, p, r, g, x, gain, ctx, out_w):
    t, d = x.shape
    part = ctx.shape[1]
    ins = two_parts(p, r) + [by_rows(g), by_rows(x), all_of(gain[None])]
    ins += [by_rows(ctx), all_of(out_w)]
    outs = [out_rows((t, d), F32), out_all((1, d), F32), out_rows((t, part), BF)]
    outs += [out_all((part, d), BF)]
    scratch = [pltpu.VMEM((part, d), F32)]
    return launch(context_back_kernel, "context_back", t // ROWS, place, ins, outs, scratch)


def projections_back_kernel(place, *refs, pieces, groups):
    parts, ua, refs = refs[:pieces], refs[pieces], refs[pieces + 1 :]
    blocks, (part, grad, acc) = refs[:groups], refs[groups:]
    first_step(acc)
    all3 = jnp.concatenate([p[...] for p in parts], axis=1)
    n = blocks[0].shape[0]
    for s, w in enumerate(blocks):
        columns = columns_of(place, s, n)
        part[0, :, columns] = part[1, :, columns] = dot(all3, w[...], 1, 1).astype(BF)
    acc[...] += dot(ua[...], all3, 0, 0)

    @pl.when(last_step())
    def _():
        grad[...] = acc[...].astype(BF)


def projections_back(place, *arrays):
    *parts, ua, blocks = arrays
    t, d = ua.shape
    part = sum(p.shape[1] for p in parts) // 3
    ins = [by_rows(p) for p in parts] + [by_rows(ua)] + weight_blocks(blocks, 3 * part, 1)
    outs = [out_twice((t, d), BF), out_all((d, 3 * part), BF)]
    scratch = [pltpu.VMEM((d, 3 * part), F32)]
    kernel = functools.partial(projections_back_kernel, pieces=len(parts), groups=len(blocks))
    return launch(kernel, "projections_back", t // ROWS, place, ins, outs, scratch)


def first_back_kernel(place, p, r, g, x, gain, out, gg):
    first_step(gg)
    out[...] = back_step(g, p, r, x, gain, gg).astype(BF)


def first_back(place, p, r, g, x, gain):
    t, d = x.shape
    ins = two_parts(p, r) + [by_rows(g), by_rows(x), all_of(gain[None])]
    outs = [out_rows((t, d), BF), out_all((1, d), F32)]
    return launch(first_back_kernel, "first_back", t // ROWS, place, ins, outs)


def encoding(length, features):
    half = features // 2
    frequency = jnp.exp(jnp.arange(half).astype(F32) * (-2.0 * math.log(10000.0) / features))
    fine = 32
    steps = jnp.arange(length // fine) * fine
    a = jnp.where(steps < length // 2, -steps, length - steps).astype(F32)[:, None] * frequency[None]
    b = jnp.arange(fine).astype(F32)[:, None] * frequency[None]
    sa, ca = jnp.sin(a)[:, None], jnp.cos(a)[:, None]
    sb, cb = jnp.sin(b)[None], jnp.cos(b)[None]
    sine = sa * cb - ca * sb
    cosine = ca * cb + sa * sb
    return jnp.concatenate([sine, cosine], axis=-1).reshape(length, features).astype(BF)


def on_device(
    frames,
    segment_ids,
    valid_mask,
    first_norm,
    first_up,
    first_down,
    attention_norm,
    query_proj,
    key_proj,
    value_proj,
    output_proj,
    position_proj,
    content_bias,
    position_bias,
    convolution_norm,
    pointwise_in,
    depthwise,
    batch_gain,
    batch_shift,
    pointwise_out,
    second_norm,
    second_up,
    second_down,
    final_norm,
    cotangent,
):
    groups = lax.axis_size("fsdp")
    member = lax.axis_index("fsdp")
    shard_frames, d = frames.shape[1:]
    t = segment_ids.shape[1]
    part = d // groups
    seg = segment_ids[0]
    valid = valid_mask[0].astype(F32)[:, None]
    bits = [bit_of(0), bit_of(1)]
    quarters = [1 - bits[0], 3 - bits[1], bits[0], 2 + bits[1]]
    owners = [lax.rem(member + groups - s, groups) for s in range(groups)]
    place = jnp.stack([(member + 1) % 2] + [jnp.int32(0)] * 3 + quarters + owners).astype(jnp.int32)

    def own(v, axis=0):
        return lax.dynamic_slice_in_dim(v, member * part, part, axis)

    def own_rows(v):
        return lax.dynamic_slice_in_dim(v, member * shard_frames, shard_frames, 0)[None]

    x0 = gather_rows(frames[0], place)
    seg_rim = jnp.pad(seg, (RIM, RIM), constant_values=-1)
    link = jnp.stack([(seg_rim[o : o + t] == seg).astype(F32) for o in range(KER)], axis=1)
    taps = own(depthwise).T
    gain_own, shift_own = own(batch_gain), own(batch_shift)

    if groups == 2:
        kept, away = packed(
            place,
            [(pointwise_in, 0, part), (pointwise_in, 2, part)]
            + [(m, 0, part) for m in (position_proj, query_proj, key_proj, value_proj)],
        )
        away, x0 = lax.optimization_barrier((away, x0))
        blocks = [kept, shifted(away, 1)]
    else:
        value_in, gate_in = pointwise_in[:, :d], pointwise_in[:, d:]
        blocks = own_columns(
            [(m, part) for m in (value_in, gate_in, position_proj, query_proj, key_proj, value_proj)]
        )
    part_sum, pre1, u1 = ffn_forward(place, x0, (), first_norm, first_up, first_down)
    other = pair_other(part_sum)
    encoded = encoding(t, d)
    pos = sum(
        dot(
            lax.dynamic_slice_in_dim(encoded, owner * part, part, 1),
            block[:, 2 * part : 3 * part],
        )
        for owner, block in zip(owners, blocks, strict=True)
    ).astype(BF)
    x1, ua, qc, qp, keys, values = qkv_forward(
        place, x0, part_sum, other, attention_norm, own(content_bias), own(position_bias), blocks
    )
    cotangent, _ = lax.optimization_barrier((cotangent, x1))
    cot = gather_rows(cotangent[0], place)
    ctx, part_sum = attention(place, seg, qc, qp, keys, values, pos, output_proj)
    other = pair_other(part_sum)
    x2, uc, gp, dc, sums = conv_forward(
        place, x1, part_sum, other, convolution_norm, link, valid, taps, blocks
    )
    sums = row_sum(sums)
    sw, part_sum = batch_forward(place, dc, sums, gain_own, shift_own, pointwise_out)
    other = pair_other(part_sum)
    x3, part_sum, pre2, u2 = ffn_forward(
        place, x2, (part_sum, other), second_norm, second_up, second_down
    )
    other = pair_other(part_sum)

    sequence = Sequence()
    run = sequence.run
    sums_of = {}
    plan = list(PLAN)

    def ready(name, arrays, parts=None):
        sums_of[name] = BatchSum(sequence, arrays, parts)
        if parts is not None:
            sums_of[name].step()

    def comm():
        for name in plan.pop(0):
            sums_of[name].step()

    hid = second_up.shape[0]
    layer_out, g, gf, final_gain, send0, send1 = final_down(
        place, x3, part_sum, other, cot, final_norm, pre2
    )
    keep = run(lambda *v: down_keep(place, *v), gf, pre2)
    ready("a", [hid], (tuple(keep), (send0, send1)))
    comm()
    part_sum, ga = run(lambda *v: ffn_back(place, *v), gf, pre2, second_up, second_down)
    comm()
    (part_sum,) = sequence.tie(part_sum)
    other = pair_swap(part_sum)
    quads = run(lambda *v: up_grad(place, *v), ga, u2)
    comm()
    g, second_gain, gbo, ab, out_w_grad = run(
        lambda *v: conv_back_one(place, *v),
        part_sum, other, g, x3, second_norm, dc, sw, sums, gain_own, shift_own, pointwise_out,
    )
    comm()
    (ab,) = sequence.tie(ab)
    ab = row_sum(ab)
    sequence.last = ab
    comm()
    quads = sequence.tie(*quads)
    ready("b", [hid], ((quads[2], quads[3]), (quads[0], quads[1])))
    part_sum, in_w_grad, taps_grad = run(
        lambda ab, gbo: conv_back_two(
            place, gbo, dc, gp, uc, link, valid, sums, ab, gain_own, taps, blocks
        ),
        ab,
        gbo,
    )
    comm()
    part_sum, in_w_grad = sequence.tie(part_sum, in_w_grad)
    other = pair_swap(part_sum)
    swapped = row_blocks_swap(in_w_grad)

    def unfold(swapped, at):
        columns = slice(at * part, (at + 1) * part)
        return jnp.concatenate([swapped[j][:, columns] for j in range(groups)], axis=1)

    ready("c", [out_w_grad, unfold(swapped, 0), unfold(swapped, 1)])
    comm()
    g, conv_gain, gctx, output_grad = run(
        lambda *v: context_back(place, *v),
        part_sum, other, g, x2, convolution_norm, ctx, output_proj,
    )
    comm()
    halves_of = []
    for first in (True, False):
        half = run(
            lambda *v, first=first: attention_back(place, seg, *v, first),
            qc, qp, keys, values, pos, gctx,
        )
        if half is not None:
            halves_of.append(half)
        comm()
    gqkv = [h[at] for at in range(3) for h in halves_of]
    gpos, content_grad, position_grad = (
        jnp.concatenate([h[at] for h in halves_of], axis=1) for at in range(3, 6)
    )
    part_sum, qkv_grad = run(lambda *v: projections_back(place, *v, blocks), *gqkv, ua)
    comm()
    part_sum, qkv_grad = sequence.tie(part_sum, qkv_grad)
    other = pair_swap(part_sum)
    high = gpos.astype(BF)
    low = (gpos - high.astype(F32)).astype(BF)
    pos_grad = (dot(encoded, high, 0, 0) + dot(encoded, low, 0, 0)).astype(BF)
    swapped = row_blocks_swap(jnp.concatenate([qkv_grad, pos_grad], axis=1))
    ready("d", [output_grad] + [unfold(swapped, at) for at in range(4)])
    comm()
    g, gf, attention_gain, *quads = run(
        lambda *v: back_down(place, *v), part_sum, other, g, x1, attention_norm, pre1
    )
    ready("e", [hid], ((quads[2], quads[3]), (quads[0], quads[1])))
    comm()
    part_sum, ga = run(lambda *v: ffn_back(place, *v), gf, pre1, first_up, first_down)
    comm()
    (part_sum,) = sequence.tie(part_sum)
    other = pair_swap(part_sum)
    quads = run(lambda *v: up_grad(place, *v), ga, u1)
    ready("f", [hid], ((quads[2], quads[3]), (quads[0], quads[1])))
    comm()
    frames_grad, first_gain = run(
        lambda *v: first_back(place, *v), part_sum, other, g, x0, first_norm
    )
    gains = [own(v[0]) for v in (first_gain, attention_gain, conv_gain, second_gain, final_gain)]
    small = jnp.concatenate(
        [jnp.stack(gains), content_grad, position_grad, taps_grad], axis=0
    )
    sums_of["s"] = SmallSum(sequence, small)
    comm()
    for job in sums_of.values():
        job.finish()
    small = sums_of["s"].v
    out_w_grad, value_grad, gate_grad = sums_of["c"].out
    output_grad, q_grad, k_grad, v_grad, pos_grad = sums_of["d"].out
    return (
        own_rows(layer_out),
        own_rows(frames_grad),
        small[0],
        sums_of["f"].out[0],
        sums_of["e"].out[0],
        small[1],
        q_grad,
        k_grad,
        v_grad,
        output_grad,
        pos_grad,
        small[5],
        small[6],
        small[2],
        jnp.concatenate([value_grad, gate_grad], axis=1),
        small[7:].T,
        ab[1],
        ab[0],
        out_w_grad,
        small[3],
        sums_of["b"].out[0],
        sums_of["a"].out[0],
        small[4],
    )


def solution(mesh):
    rows, shard, whole = P("batch", "fsdp", None), P("fsdp", None), P()
    return jax.shard_map(
        on_device,
        mesh=mesh,
        in_specs=(
            rows,
            P("batch", None),
            P("batch", None),
            whole,
            shard,
            shard,
            whole,
            shard,
            shard,
            shard,
            shard,
            shard,
            whole,
            whole,
            whole,
            shard,
            whole,
            whole,
            whole,
            shard,
            whole,
            shard,
            shard,
            whole,
            rows,
        ),
        out_specs=(
            rows,
            rows,
            P("fsdp"),
            shard,
            shard,
            P("fsdp"),
            shard,
            shard,
            shard,
            shard,
            shard,
            P("fsdp"),
            P("fsdp"),
            P("fsdp"),
            shard,
            shard,
            P("fsdp"),
            P("fsdp"),
            shard,
            P("fsdp"),
            shard,
            shard,
            P("fsdp"),
        ),
        check_vma=False,
    )
```

time: 915 us -> 792 us (0.87)
  waiting for transfers between devices: 410 us -> 194 us
  Pallas kernels: 175 us -> 295 us
  other arithmetic: 164 us -> 109 us
  starting transfers between devices: 72 us -> 112 us
  matrix products: 42.7 us -> 8.5 us
  blocking collectives: 0 us -> 13.7 us
    ppermute x54 -> x78, waiting for transfers between devices: 399 us -> 183 us  [exchange(): return lax.ppermute(v, 'batch', [(i, i ^ 1 << b) for i in range(n)])]
    pallas_call x8 -> x23, Pallas kernels: 175 us -> 295 us  [launch(): pl.pallas_call(kernel, grid_spec=pltpu.PrefetchScalarGridSpec(num_scalar_...]
    reduce_sum x17 -> x0, other arithmetic: 50.6 us -> none  [the longest x4 15.1 us: norm_parts(): centred = v - jnp.mean(v, axis=-1, keepdims=True)]
    dot_general x15 -> x4, matrix products: 42.7 us -> 8.5 us  [dot(): lax.dot_general(a, b, (((da,), (db,)), ((), ())), preferred_element_type=...]
    all_to_all x0 -> x4, starting transfers between devices: none -> 22.8 us  [pair_swap(): return lax.all_to_all(v, 'fsdp', 0, 0)]
    ppermute x54 -> x78, starting transfers between devices: 69.7 us -> 87.5 us  [exchange(): return lax.ppermute(v, 'batch', [(i, i ^ 1 << b) for i in range(n)])]
    all_to_all x0 -> x2, blocking collectives: none -> 13.7 us  [row_blocks_swap(): return lax.all_to_all(v.reshape(g, n, v.shape[1]), 'fsdp', 0, 0)]
    add x4, other arithmetic: 11.3 us -> 0.03 us  [step(): self.v = self.sequence.run(lambda a, b: a + b, self.v, self.got)]
  transfers between devices with their start and end apart: 66 -> 89, of which waited for: 34 -> 32; matrix products, arithmetic and copies ran while one was open for 20% -> 18% of each run, Pallas kernels for 9% -> 27%
where the time goes in v2:
time: 792 us; the launch traced here: 782 us
  Pallas kernels  295 us (37%)
  waiting for transfers between devices  194 us (24%)
  starting transfers between devices  112 us (14%)
  other arithmetic  109 us (14%)
  local copies, waits for them, and re-layouts  47.3 us (6%)
  blocking collectives  13.7 us (2%)
  matrix products  8.5 us (1%)
    pallas_call x23, Pallas kernels, launch(): pl.pallas_call(kernel, grid_spec=pltpu.PrefetchScalarGridSpec(num_scalar_...  295 us
    ppermute x78, waiting for transfers between devices, exchange(): return lax.ppermute(v, 'batch', [(i, i ^ 1 << b) for i in range(n)])  183 us
    ppermute x78, starting transfers between devices, exchange(): return lax.ppermute(v, 'batch', [(i, i ^ 1 << b) for i in range(n)])  87.5 us
    select_n x46, other arithmetic, joined(): return jnp.where(bit_of(b) == 1, high, low)  39.1 us
    convert_element_type x6, other arithmetic, final(): out.append(whole[at:at + size].astype(F32))  23.8 us
    all_to_all x4, starting transfers between devices, pair_swap(): return lax.all_to_all(v, 'fsdp', 0, 0)  22.8 us
    convert_element_type x30, other arithmetic, add16(): return (a.astype(F32) + b.astype(F32)).astype(BF)  21.3 us
  transfers between devices with their start and end apart: 89, of which 32 were waited for; matrix products, arithmetic and copies ran while one was open for 18% of the time, Pallas kernels for 27%

profile of v2, /device:TPU:0, one launch (start us, length us, event | category | flops | bytes accessed | tf_op | source)
XLA Modules:
  0.0 782.0 jit_solution(15848219549550084866)
XLA Ops:
  1.8 6.6 packed.1
  9.4 3.6 placed.2.refs_0_.base.x
  13.1 15.8 %ffn_forward.2 = (bf16[1024,1024]{1,0:T(8,128)(2,1)}, bf16[1024,2048]{1,0:T(8,128)(2,1)}, bf16[1024,1024]{1,0:T(8,128)(2,1)}) custom-call(s32[10]{0:T(128)} %stack.202.place, bf16[1024,1024]{1,0:T(8,128)(2,1)} %placed.2.refs_0_.base.x, f32[1,1024]{1,0:T(1,128)} %bitcast.246, bf16[2048,1024]{1,0:T(8,128)(2,1)} %up.1, bf16[2048,1024]{1,0:T(8,128)(2,1)} %down.1), custom_call_target="tpu_custom_call" | custom-call | flops 1 | bytes 1 | tf_op jit(solution)/shard_map/ffn_forward/pallas_call | solution.py:290
  37.2 10.4 %qkv.1 = (f32[1024,1024]{1,0:T(8,128)}, bf16[1024,1024]{1,0:T(8,128)(2,1)}, bf16[1024,512]{1,0:T(8,128)(2,1)}, bf16[1024,512]{1,0:T(8,128)(2,1)}, bf16[1024,512]{1,0:T(8,128)(2,1)}, /*index=5*/bf16[1024,512]{1,0:T(8,128)(2,1)}) custom-call(s32[10]{0:T(128)} %stack.202.place, bf16[1024,1024]{1,0:T(8,128)(2,1)} %placed.2.refs_0_.base.x, ...), custom_call_target="tpu_custom_call" | custom-call | flops 1 | bytes 1 | tf_op jit(solution)/shard_map/qkv/pallas_call | solution.py:290
  47.6 19.0 %attention_forward.1 = (bf16[1024,512]{1,0:T(8,128)(2,1)}, bf16[1024,1024]{1,0:T(8,128)(2,1)}) custom-call(s32[10]{0:T(128)} %stack.202.place, s32[1024,1]{1,0:T(8,128)} %copy.61.segq, s32[1,1024]{1,0:T(1,128)} %segk.5, bf16[1024,512]{1,0:T(8,128)(2,1)} %get-tuple-element.470.qc, bf16[1024,512]{1,0:T(8,128)(2,1)} %get-tuple-element.471.qp, ...), custom_call_target="tpu_custom_call" | custom-call | flops 1 | bytes 1 | tf_op jit(solution)/shard_map/attention_forward/pallas_call | solution.py:290
  72.4 14.1 %conv_forward.1 = (f32[1024,1024]{1,0:T(8,128)}, bf16[1024,1024]{1,0:T(8,128)(2,1)}, bf16[1024,1024]{1,0:T(8,128)(2,1)}, f32[1024,512]{1,0:T(8,128)}, f32[3,512]{1,0:T(4,128)}) custom-call(s32[10]{0:T(128)} %stack.202.place, f32[1024,1024]{1,0:T(8,128)} %get-tuple-element.528.base.x, bf16[1024,1024]{1,0:T(8,128)(2,1)} %get-tuple-element.360.p, ...), custom_call_target="tpu_custom_call" | custom-call | flops 1 | bytes 1 | tf_op jit(solution)/shard_map/conv_forward/pallas_call | solution.py:290
  86.4 2.7 collective-permute-start.4
  99.1 3.0 collective-permute-start.7
  104.4 5.7 batch_forward.1
  110.0 4.4 collective-permute-done.8.refs_2_
  115.7 17.0 %ffn_forward.3 = (f32[1024,1024]{1,0:T(8,128)}, bf16[1024,1024]{1,0:T(8,128)(2,1)}, bf16[1024,2048]{1,0:T(8,128)(2,1)}, bf16[1024,1024]{1,0:T(8,128)(2,1)}) custom-call(s32[10]{0:T(128)} %stack.202.place, f32[1024,1024]{1,0:T(8,128)} %get-tuple-element.437.refs_0_.x, bf16[1024,1024]{1,0:T(8,128)(2,1)} %get-tuple-element.364.refs_1_, ...), custom_call_target="tpu_custom_call" | custom-call | flops 1 | bytes 1 | tf_op jit(solution)/shard_map/ffn_forward/pallas_call | solution.py:290
  133.3 5.0 collective-permute-done.10.other
  139.3 3.6 placed.3.cot
  144.2 14.1 %final_down.1 = (bf16[1024,1024]{1,0:T(8,128)(2,1)}, f32[1024,1024]{1,0:T(8,128)}, bf16[1024,1024]{1,0:T(8,128)(2,1)}, f32[1,1024]{1,0:T(1,128)}, bf16[512,1024]{1,0:T(8,128)(2,1)}, /*index=5*/bf16[512,1024]{1,0:T(8,128)(2,1)}) custom-call(s32[10]{0:T(128)} %stack.202.place, f32[1024,1024]{1,0:T(8,128)} %get-tuple-element.393.x, ...), custom_call_target="tpu_custom_call" | custom-call | flops 1 | bytes 1 | tf_op jit(solution)/shard_map/final_down/pallas_call | solution.py:290
  161.7 6.6 down_keep.1
  168.4 16.6 %ffn_back.2 = (bf16[2,1024,1024]{2,1,0:T(8,128)(2,1)}, bf16[1024,2048]{1,0:T(8,128)(2,1)}) custom-call(s32[10]{0:T(128)} %stack.202.place, bf16[1024,1024]{1,0:T(8,128)(2,1)} %get-tuple-element.372.gf, bf16[1024,2048]{1,0:T(8,128)(2,1)} %get-tuple-element.373.pre, bf16[2048,1024]{1,0:T(8,128)(2,1)} %up, bf16[2048,1024]{1,0:T(8,128)(2,1)} %down), custom_call_target="tpu_custom_call" | custom-call | flops 1 | bytes 1 | tf_op jit(solution)/shard_map/ffn_back/pallas_call | solution.py:290
  188.5 5.6 all-to-all-start
  194.2 9.9 %up_grad.2 = (bf16[512,1024]{1,0:T(8,128)(2,1)}, bf16[512,1024]{1,0:T(8,128)(2,1)}, bf16[512,1024]{1,0:T(8,128)(2,1)}, bf16[512,1024]{1,0:T(8,128)(2,1)}) custom-call(s32[10]{0:T(128)} %stack.202.place, bf16[1024,2048]{1,0:T(8,128)(2,1)} %get-tuple-element.387.ga, bf16[1024,1024]{1,0:T(8,128)(2,1)} %get-tuple-element.388.u), custom_call_target="tpu_custom_call" | custom-call | flops 1 | bytes 1 | tf_op jit(solution)/shard_map/up_grad/pallas_call | solution.py:290
  204.1 13.2 %conv_back_one.1 = (f32[1024,1024]{1,0:T(8,128)}, f32[1,1024]{1,0:T(1,128)}, f32[1024,512]{1,0:T(8,128)}, f32[2,512]{1,0:T(2,128)}, bf16[512,1024]{1,0:T(8,128)(2,1)}) custom-call(s32[10]{0:T(128)} %stack.202.place, bf16[2,1024,1024]{2,1,0:T(8,128)(2,1)} %get-tuple-element.390.p, bf16[2,1024,1024]{2,1,0:T(8,128)(2,1)} %all-to-all-done.r, ...), custom_call_target="tpu_custom_call" | custom-call | flops 1 | bytes 1 | tf_op jit(solution)/shard_map/conv_back_one/pallas_call | solution.py:290
  221.2 5.3 collective-permute-done.14
  230.5 3.2 collective-permute-done.16
  233.7 2.6 collective-permute-start.17
  240.9 2.6 collective-permute-start.20
  243.5 17.2 %conv_back_two.1 = (bf16[2,1024,1024]{2,1,0:T(8,128)(2,1)}, bf16[1024,1024]{1,0:T(8,128)(2,1)}, f32[5,512]{1,0:T(8,128)}) custom-call(s32[10]{0:T(128)} %stack.202.place, f32[1024,512]{1,0:T(8,128)} %get-tuple-element.415.gbo, f32[1024,512]{1,0:T(8,128)} %get-tuple-element.395.dc, bf16[1024,1024]{1,0:T(8,128)(2,1)} %get-tuple-element.416.gp.gp_lag, ...), custom_call_target="tpu_custom_call" | custom-call | flops 1 | bytes 1 | tf_op jit(solution)/shard_map/conv_back_two/pallas_call | solution.py:290
  260.7 6.6 all_to_all.30
  267.3 5.9 all-to-all-start.1
  284.3 12.2 %context_back.1 = (f32[1024,1024]{1,0:T(8,128)}, f32[1,1024]{1,0:T(1,128)}, bf16[1024,512]{1,0:T(8,128)(2,1)}, bf16[512,1024]{1,0:T(8,128)(2,1)}) custom-call(s32[10]{0:T(128)} %stack.202.place, bf16[2,1024,1024]{2,1,0:T(8,128)(2,1)} %get-tuple-element.434.p, bf16[2,1024,1024]{2,1,0:T(8,128)(2,1)} %all-to-all-done.1.r, f32[1024,1024]{1,0:T(8,128)} %get-tuple-element.436.g, ...), custom_call_target="tpu_custom_call" | custom-call | flops 1 | bytes 1 | tf_op jit(solution)/shard_map/context_back/pallas_call | solution.py:290
  300.7 22.1 %attention_back.2 = (bf16[1024,256]{1,0:T(8,128)(2,1)}, bf16[1024,256]{1,0:T(8,128)(2,1)}, bf16[1024,256]{1,0:T(8,128)(2,1)}, f32[1024,256]{1,0:T(8,128)}, f32[1,256]{1,0:T(1,128)}, /*index=5*/f32[1,256]{1,0:T(1,128)}) custom-call(s32[10]{0:T(128)} %stack.202.place, s32[1024,1]{1,0:T(8,128)} %copy.61.segq, s32[1,1024]{1,0:T(1,128)} %segk.5, ...), custom_call_target="tpu_custom_call" | custom-call | flops 1 | bytes 1 | tf_op jit(solution)/shard_map/attention_back/pallas_call | solution.py:290
  329.2 4.5 fusion.11
  338.9 21.9 %attention_back.3 = (bf16[1024,256]{1,0:T(8,128)(2,1)}, bf16[1024,256]{1,0:T(8,128)(2,1)}, bf16[1024,256]{1,0:T(8,128)(2,1)}, f32[1024,256]{1,0:T(8,128)}, f32[1,256]{1,0:T(1,128)}, /*index=5*/f32[1,256]{1,0:T(1,128)}) custom-call(s32[10]{0:T(128)} %stack.202.place, s32[1024,1]{1,0:T(8,128)} %copy.61.segq, s32[1,1024]{1,0:T(1,128)} %segk.5, ...), custom_call_target="tpu_custom_call" | custom-call | flops 1 | bytes 1 | tf_op jit(solution)/shard_map/attention_back/pallas_call | solution.py:290
  363.3 3.0 fusion.2
  371.4 13.4 %projections_back.1 = (bf16[2,1024,1024]{2,1,0:T(8,128)(2,1)}, bf16[1024,1536]{1,0:T(8,128)(2,1)}) custom-call(s32[10]{0:T(128)} %stack.202.place, bf16[1024,256]{1,0:T(8,128)(2,1)} %get-tuple-element.485.refs_0_, bf16[1024,256]{1,0:T(8,128)(2,1)} %get-tuple-element.486.refs_1_, bf16[1024,256]{1,0:T(8,128)(2,1)} %get-tuple-element.487.refs_2_, ...), custom_call_target="tpu_custom_call" | custom-call | flops 1 | bytes 1 | tf_op jit(solution)/shard_map/projections_back/pallas_call | solution.py:290
  389.2 7.1 all_to_all.31
  402.3 5.7 all-to-all-start.3
  410.4 9.9 %collective-permute-done.32 = bf16[2,192,1024]{2,1,0:T(8,128)(2,1)} collective-permute-done((bf16[2,192,1024]{2,1,0:T(8,128)(2,1)}, bf16[2,192,1024]{2,1,0:T(8,128)(2,1)}, u32[]{:S(2)}, u32[]{:S(2)}) %collective-permute-start.32) | collective-permute-done | bytes 786464 | tf_op jit(solution)/shard_map/ppermute | solution.py:113
  433.9 2.6 maximum_select_fusion.2
  436.5 3.3 maximum_select_fusion.3
  439.8 4.5 maximum_convert_fusion
  448.7 2.6 collective-permute-start.39
  451.3 17.5 %back_down.1 = (f32[1024,1024]{1,0:T(8,128)}, bf16[1024,1024]{1,0:T(8,128)(2,1)}, f32[1,1024]{1,0:T(1,128)}, bf16[512,1024]{1,0:T(8,128)(2,1)}, bf16[512,1024]{1...) custom-call(s32[10]{0:T(128)} %stack.202.place, bf16[2,1024,1024]{2,1,0:T(8,128)(2,1)} %get-tuple-element.525.p, ...), custom_call_target="tpu_custom_call" | custom-call | flops 1 | bytes 1 | tf_op jit(solution)/shard_map/back_down/pallas_call | solution.py:290
  476.1 16.3 %ffn_back.3 = (bf16[2,1024,1024]{2,1,0:T(8,128)(2,1)}, bf16[1024,2048]{1,0:T(8,128)(2,1)}) custom-call(s32[10]{0:T(128)} %stack.202.place, bf16[1024,1024]{1,0:T(8,128)(2,1)} %get-tuple-element.539.gf, bf16[1024,2048]{1,0:T(8,128)(2,1)} %get-tuple-element.540.pre, bf16[2048,1024]{1,0:T(8,128)(2,1)} %up.1, bf16[2048,1024]{1,0:T(8,128)(2,1)} %down.1), custom_call_target="tpu_custom_call" | custom-call | flops 1 | bytes 1 | tf_op jit(solution)/shard_map/ffn_back/pallas_call | solution.py:290
  506.4 41.4 %collective-permute-done.52 = bf16[2,256,1024]{2,1,0:T(8,128)(2,1)S(1)} collective-permute-done((bf16[2,256,1024]{2,1,0:T(8,128)(2,1)S(1)}, bf16[2,256,1024]{2,1,0:T(8,128)(2,1)S(1)}, u32[]{:S(2)}, u32[]{:S(2)}) %collective-permute-start.52) | collective-permute-done | bytes 1048608 | tf_op jit(solution)/shard_map/ppermute | solution.py:113
  552.0 9.9 %up_grad.3 = (bf16[512,1024]{1,0:T(8,128)(2,1)}, bf16[512,1024]{1,0:T(8,128)(2,1)}, bf16[512,1024]{1,0:T(8,128)(2,1)}, bf16[512,1024]{1,0:T(8,128)(2,1)}) custom-call(s32[10]{0:T(128)} %stack.202.place, bf16[1024,2048]{1,0:T(8,128)(2,1)} %get-tuple-element.569.ga, bf16[1024,1024]{1,0:T(8,128)(2,1)} %get-tuple-element.570.u), custom_call_target="tpu_custom_call" | custom-call | flops 1 | bytes 1 | tf_op jit(solution)/shard_map/up_grad/pallas_call | solution.py:290
  567.2 5.6 all-to-all-start.5
  574.7 16.3 %collective-permute-done.54 = bf16[128,1024]{1,0:T(8,128)(2,1)} collective-permute-done((bf16[128,1024]{1,0:T(8,128)(2,1)}, bf16[128,1024]{1,0:T(8,128)(2,1)}, u32[]{:S(2)}, u32[]{:S(2)}) %collective-permute-start.54) | collective-permute-done | bytes 262176 | tf_op jit(solution)/shard_map/ppermute | solution.py:113
  594.9 3.2 collective-permute-done.51
  603.2 2.6 collective-permute-start.62
  605.8 2.6 maximum_select_fusion.4
  608.4 2.5 maximum_select_fusion.5
  610.9 4.5 maximum_convert_fusion.1
  615.5 7.9 %first_back.1 = (bf16[1024,1024]{1,0:T(8,128)(2,1)}, f32[1,1024]{1,0:T(1,128)}) custom-call(s32[10]{0:T(128)} %stack.202.place, bf16[2,1024,1024]{2,1,0:T(8,128)(2,1)} %get-tuple-element.588.p, bf16[2,1024,1024]{2,1,0:T(8,128)(2,1)} %all-to-all-done.5.r, f32[1024,1024]{1,0:T(8,128)} %get-tuple-element.590.g, bf16[1024,1024]{1,0:T(8,128)(2,1)} %placed.2.refs_0_.base.x, ...), custom_call_target="tpu_custom_call" | custom-call | flops 1 | bytes 1 | tf_op jit(solution)/shard_map/first_back/pallas_call | solution.py:290
  631.1 8.5 %collective-permute-done.56 = bf16[2,128,1024]{2,1,0:T(8,128)(2,1)} collective-permute-done((bf16[2,128,1024]{2,1,0:T(8,128)(2,1)S(1)}, bf16[2,128,1024]{2,1,0:T(8,128)(2,1)}, u32[]{:S(2)}, u32[]{:S(2)}) %collective-permute-start.56) | collective-permute-done | bytes 524320 | tf_op jit(solution)/shard_map/ppermute | solution.py:113
  651.3 20.1 %collective-permute-done.63 = bf16[2,256,1024]{2,1,0:T(8,128)(2,1)S(1)} collective-permute-done((bf16[2,256,1024]{2,1,0:T(8,128)(2,1)S(1)}, bf16[2,256,1024]{2,1,0:T(8,128)(2,1)S(1)}, u32[]{:S(2)}, u32[]{:S(2)}) %collective-permute-start.63) | collective-permute-done | bytes 1048608 | tf_op jit(solution)/shard_map/ppermute | solution.py:113
  674.8 16.9 %collective-permute-done.69 = bf16[384,1024]{1,0:T(8,128)(2,1)S(1)} collective-permute-done((bf16[384,1024]{1,0:T(8,128)(2,1)S(1)}, bf16[384,1024]{1,0:T(8,128)(2,1)S(1)}, u32[]{:S(2)}, u32[]{:S(2)}) %collective-permute-start.69) | collective-permute-done | bytes 786464 | tf_op jit(solution)/shard_map/ppermute | solution.py:113
  697.5 5.3 collective-permute-done.68
  707.0 3.0 collective-permute-start.71
  711.1 8.2 %collective-permute-done.74 = bf16[2,128,1024]{2,1,0:T(8,128)(2,1)S(1)} collective-permute-done((bf16[2,128,1024]{2,1,0:T(8,128)(2,1)S(1)}, bf16[2,128,1024]{2,1,0:T(8,128)(2,1)S(1)}, u32[]{:S(2)}, u32[]{:S(2)}) %collective-permute-start.74) | collective-permute-done | bytes 524320 | tf_op jit(solution)/shard_map/ppermute | solution.py:113
  720.3 12.0 %collective-permute-done.73 = bf16[512,1024]{1,0:T(8,128)(2,1)S(1)} collective-permute-done((bf16[512,1024]{1,0:T(8,128)(2,1)S(1)}, bf16[512,1024]{1,0:T(8,128)(2,1)S(1)}, u32[]{:S(2)}, u32[]{:S(2)}) %collective-permute-start.73) | collective-permute-done | bytes 1048608 | tf_op jit(solution)/shard_map/ppermute | solution.py:113
  735.0 4.5 maximum_convert_fusion.2
  745.3 2.5 fusion.1
  749.3 7.0 collective-permute-done.79
  758.4 3.6 collective-permute-done.84
  766.9 4.2 slice_convert_fusion
  777.3 4.5 maximum_convert_fusion.3
  (501 shorter events, 215.0 us)
Async XLA Ops:
  13.0 22.1 %collective-permute-start.2 = (bf16[512,3072]{1,0:T(8,128)(2,1)}, bf16[512,3072]{1,0:T(8,128)(2,1)S(1)}, u32[]{:S(2)}, u32[]{:S(2)}) collective-permute-start(bf16[512,3072]{1,0:T(8,128)(2,1)} %get-tuple-element.354), channel_id=1, source_target_pairs={{0,1},{1,0},{2,3},{3,2},{4,5},{5,4},{6,7},{7,6},{8,9},{9,8},{10,11... | collective-permute-start | bytes 9437192 | tf_op jit(solution)/shard_map/ppermute | solution.py:47
  158.4 26.6 %collective-permute-start.11 = (bf16[512,1024]{1,0:T(8,128)(2,1)}, bf16[512,1024]{1,0:T(8,128)(2,1)S(1)}, u32[]{:S(2)}, u32[]{:S(2)}) collective-permute-start(bf16[512,1024]{1,0:T(8,128)(2,1)} %get-tuple-element.378), channel_id=1, source_target_pairs={{0,2},{2,0},{4,6},{6,4},{8,10},{10,8},{12,14},{14,12},{16,18},{18,... | collective-permute-start | bytes 3145736 | tf_op jit(solution)/shard_map/ppermute | solution.py:113
  160.2 25.2 %collective-permute-start.12 = (bf16[512,1024]{1,0:T(8,128)(2,1)}, bf16[512,1024]{1,0:T(8,128)(2,1)S(1)}, u32[]{:S(2)}, u32[]{:S(2)}) collective-permute-start(bf16[512,1024]{1,0:T(8,128)(2,1)} %get-tuple-element.379), channel_id=1, source_target_pairs={{0,4},{2,6},{4,0},{6,2},{8,12},{10,14},{12,8},{14,10},{16,20},{18,... | collective-permute-start | bytes 3145736 | tf_op jit(solution)/shard_map/ppermute | solution.py:113
  186.9 30.4 %collective-permute-start.13 = (bf16[2,256,1024]{2,1,0:T(8,128)(2,1)S(1)}, bf16[2,256,1024]{2,1,0:T(8,128)(2,1)S(1)}, u32[]{:S(2)}, u32[]{:S(2)}) collective-permute-start(bf16[2,256,1024]{2,1,0:T(8,128)(2,1)S(1)} %pad_maximum_fusion.12), channel_id=1, source_target_pairs={{0,8},{2,10},{4,12},{6,14},{8,0},{10,2},{12,4},{14,6},{16,24},{18,... | collective-permute-start | bytes 3145736 | tf_op jit(solution)/shard_map/ppermute | solution.py:113
  188.5 15.5 %all-to-all-start = ((bf16[2,1024,1024]{2,1,0:T(8,128)(2,1)}), bf16[2,1024,1024]{2,1,0:T(8,128)(2,1)}, u32[]{:S(2)}, u32[]{:S(2)}) async-start(bf16[2,1024,1024]{2,1,0:T(8,128)(2,1)} %get-tuple-element.390.p), calls=%async_computation | async-start | bytes 8388608 | tf_op jit(solution)/shard_map/all_to_all | solution.py:73
  217.6 21.2 %collective-permute-start.19 = (bf16[128,1024]{1,0:T(8,128)(2,1)S(1)}, bf16[128,1024]{1,0:T(8,128)(2,1)S(1)}, u32[]{:S(2)}, u32[]{:S(2)}) collective-permute-start(bf16[128,1024]{1,0:T(8,128)(2,1)S(1)} %get-tuple-element.784), channel_id=1, source_target_pairs={{0,2},{2,0},{4,6},{6,4},{8,10},{10,8},{12,14},{14,12},{16,18},{18,... | collective-permute-start | bytes 786440 | tf_op jit(solution)/shard_map/ppermute | solution.py:113
  218.5 20.3 %collective-permute-start.18 = (bf16[128,1024]{1,0:T(8,128)(2,1)S(1)}, bf16[128,1024]{1,0:T(8,128)(2,1)S(1)}, u32[]{:S(2)}, u32[]{:S(2)}) collective-permute-start(bf16[128,1024]{1,0:T(8,128)(2,1)S(1)} %get-tuple-element.786), channel_id=1, source_target_pairs={{0,4},{2,6},{4,0},{6,2},{8,12},{10,14},{12,8},{14,10},{16,20},{18,... | collective-permute-start | bytes 786440 | tf_op jit(solution)/shard_map/ppermute | solution.py:113
  239.0 34.6 %collective-permute-start.21 = (bf16[512,1024]{1,0:T(8,128)(2,1)}, bf16[512,1024]{1,0:T(8,128)(2,1)}, u32[]{:S(2)}, u32[]{:S(2)}) collective-permute-start(bf16[512,1024]{1,0:T(8,128)(2,1)} %get-tuple-element.428), channel_id=1, source_target_pairs={{0,2},{2,0},{4,6},{6,4},{8,10},{10,8},{12,14},{14,12},{16,18},{18,... | collective-permute-start | bytes 3145736 | tf_op jit(solution)/shard_map/ppermute | solution.py:113
  239.7 33.9 %collective-permute-start.22 = (bf16[512,1024]{1,0:T(8,128)(2,1)}, bf16[512,1024]{1,0:T(8,128)(2,1)}, u32[]{:S(2)}, u32[]{:S(2)}) collective-permute-start(bf16[512,1024]{1,0:T(8,128)(2,1)} %get-tuple-element.429), channel_id=1, source_target_pairs={{0,4},{2,6},{4,0},{6,2},{8,12},{10,14},{12,8},{14,10},{16,20},{18,... | collective-permute-start | bytes 3145736 | tf_op jit(solution)/shard_map/ppermute | solution.py:113
  240.9 39.5 %collective-permute-start.20 = (bf16[2,128,1024]{2,1,0:T(8,128)(2,1)S(1)}, bf16[2,128,1024]{2,1,0:T(8,128)(2,1)}, u32[]{:S(2)}, u32[]{:S(2)}) collective-permute-start(bf16[2,128,1024]{2,1,0:T(8,128)(2,1)S(1)} %pad_maximum_fusion.29), channel_id=1, source_target_pairs={{0,16},{2,18},{4,20},{6,22},{8,24},{10,26},{12,28},{14,30},{16,0},... | collective-permute-start | bytes 1572872 | tf_op jit(solution)/shard_map/ppermute | solution.py:113
  267.3 17.0 %all-to-all-start.1 = ((bf16[2,1024,1024]{2,1,0:T(8,128)(2,1)}), bf16[2,1024,1024]{2,1,0:T(8,128)(2,1)}, u32[]{:S(2)}, u32[]{:S(2)}) async-start(bf16[2,1024,1024]{2,1,0:T(8,128)(2,1)} %get-tuple-element.434.p), calls=%async_computation.1 | async-start | bytes 8388608 | tf_op jit(solution)/shard_map/all_to_all | solution.py:73
  279.9 45.7 %collective-permute-start.25 = (bf16[2,256,1024]{2,1,0:T(8,128)(2,1)}, bf16[2,256,1024]{2,1,0:T(8,128)(2,1)}, u32[]{:S(2)}, u32[]{:S(2)}) collective-permute-start(bf16[2,256,1024]{2,1,0:T(8,128)(2,1)} %pad_maximum_fusion.14), channel_id=1, source_target_pairs={{0,8},{2,10},{4,12},{6,14},{8,0},{10,2},{12,4},{14,6},{16,24},{18,... | collective-permute-start | bytes 3145736 | tf_op jit(solution)/shard_map/ppermute | solution.py:113
  281.6 14.8 %collective-permute-start.23 = (bf16[128,1024]{1,0:T(8,128)(2,1)S(1)}, bf16[128,1024]{1,0:T(8,128)(2,1)S(1)}, u32[]{:S(2)}, u32[]{:S(2)}) collective-permute-start(bf16[128,1024]{1,0:T(8,128)(2,1)S(1)} %get-tuple-element.444), channel_id=1, source_target_pairs={{0,4},{2,6},{4,0},{6,2},{8,12},{10,14},{12,8},{14,10},{16,20},{18,... | collective-permute-start | bytes 786440 | tf_op jit(solution)/shard_map/ppermute | solution.py:113
  299.2 36.8 %collective-permute-start.28 = (bf16[2,256,1024]{2,1,0:T(8,128)(2,1)}, bf16[2,256,1024]{2,1,0:T(8,128)(2,1)}, u32[]{:S(2)}, u32[]{:S(2)}) collective-permute-start(bf16[2,256,1024]{2,1,0:T(8,128)(2,1)} %pad_maximum_fusion.13), channel_id=1, source_target_pairs={{0,8},{2,10},{4,12},{6,14},{8,0},{10,2},{12,4},{14,6},{16,24},{18,... | collective-permute-start | bytes 3145736 | tf_op jit(solution)/shard_map/ppermute | solution.py:113
  333.7 36.6 %collective-permute-start.29 = (bf16[384,1024]{1,0:T(8,128)(2,1)}, bf16[384,1024]{1,0:T(8,128)(2,1)S(1)}, u32[]{:S(2)}, u32[]{:S(2)}) collective-permute-start(bf16[384,1024]{1,0:T(8,128)(2,1)} %get-tuple-element.731), channel_id=1, source_target_pairs={{0,2},{2,0},{4,6},{6,4},{8,10},{10,8},{12,14},{14,12},{16,18},{18,... | collective-permute-start | bytes 2359304 | tf_op jit(solution)/shard_map/ppermute | solution.py:113
  335.1 35.2 %collective-permute-start.30 = (bf16[384,1024]{1,0:T(8,128)(2,1)}, bf16[384,1024]{1,0:T(8,128)(2,1)S(1)}, u32[]{:S(2)}, u32[]{:S(2)}) collective-permute-start(bf16[384,1024]{1,0:T(8,128)(2,1)} %get-tuple-element.696), channel_id=1, source_target_pairs={{0,4},{2,6},{4,0},{6,2},{8,12},{10,14},{12,8},{14,10},{16,20},{18,... | collective-permute-start | bytes 2359304 | tf_op jit(solution)/shard_map/ppermute | solution.py:113
  338.0 46.9 %collective-permute-start.31 = (bf16[2,128,1024]{2,1,0:T(8,128)(2,1)S(1)}, bf16[2,128,1024]{2,1,0:T(8,128)(2,1)S(1)}, u32[]{:S(2)}, u32[]{:S(2)}) collective-permute-start(bf16[2,128,1024]{2,1,0:T(8,128)(2,1)S(1)} %pad_maximum_fusion.30), channel_id=1, source_target_pairs={{0,16},{2,18},{4,20},{6,22},{8,24},{10,26},{12,28},{14,30},{16,0},... | collective-permute-start | bytes 1572872 | tf_op jit(solution)/shard_map/ppermute | solution.py:113
  338.4 89.9 %collective-permute-start.35 = (bf16[512,1024]{1,0:T(8,128)(2,1)S(1)}, bf16[512,1024]{1,0:T(8,128)(2,1)}, u32[]{:S(2)}, u32[]{:S(2)}) collective-permute-start(bf16[512,1024]{1,0:T(8,128)(2,1)S(1)} %maximum_select_fusion.14), channel_id=1, source_target_pairs={{0,2},{2,0},{4,6},{6,4},{8,10},{10,8},{12,14},{14,12},{16,18},{18,... | collective-permute-start | bytes 3145736 | tf_op jit(solution)/shard_map/ppermute | solution.py:113
  369.1 59.2 %collective-permute-start.36 = (bf16[512,1024]{1,0:T(8,128)(2,1)}, bf16[512,1024]{1,0:T(8,128)(2,1)}, u32[]{:S(2)}, u32[]{:S(2)}) collective-permute-start(bf16[512,1024]{1,0:T(8,128)(2,1)} %maximum_select_fusion.15), channel_id=1, source_target_pairs={{0,4},{2,6},{4,0},{6,2},{8,12},{10,14},{12,8},{14,10},{16,20},{18,... | collective-permute-start | bytes 3145736 | tf_op jit(solution)/shard_map/ppermute | solution.py:113
  385.8 38.2 %collective-permute-start.37 = (bf16[128,1024]{1,0:T(8,128)(2,1)S(1)}, bf16[128,1024]{1,0:T(8,128)(2,1)}, u32[]{:S(2)}, u32[]{:S(2)}) collective-permute-start(bf16[128,1024]{1,0:T(8,128)(2,1)S(1)} %get-tuple-element.514), channel_id=1, source_target_pairs={{0,4},{2,6},{4,0},{6,2},{8,12},{10,14},{12,8},{14,10},{16,20},{18,... | collective-permute-start | bytes 786440 | tf_op jit(solution)/shard_map/ppermute | solution.py:113
  400.4 19.9 %collective-permute-start.32 = (bf16[2,192,1024]{2,1,0:T(8,128)(2,1)}, bf16[2,192,1024]{2,1,0:T(8,128)(2,1)}, u32[]{:S(2)}, u32[]{:S(2)}) collective-permute-start(bf16[2,192,1024]{2,1,0:T(8,128)(2,1)} %pad_maximum_fusion.26), channel_id=1, source_target_pairs={{0,8},{2,10},{4,12},{6,14},{8,0},{10,2},{12,4},{14,6},{16,24},{18,... | collective-permute-start | bytes 2359304 | tf_op jit(solution)/shard_map/ppermute | solution.py:113
  400.8 23.2 %collective-permute-start.38 = (bf16[128,1024]{1,0:T(8,128)(2,1)}, bf16[128,1024]{1,0:T(8,128)(2,1)}, u32[]{:S(2)}, u32[]{:S(2)}) collective-permute-start(bf16[128,1024]{1,0:T(8,128)(2,1)} %get-tuple-element.516), channel_id=1, source_target_pairs={{0,2},{2,0},{4,6},{6,4},{8,10},{10,8},{12,14},{14,12},{16,18},{18,... | collective-permute-start | bytes 786440 | tf_op jit(solution)/shard_map/ppermute | solution.py:113
  402.3 49.0 %all-to-all-start.3 = ((bf16[2,1024,1024]{2,1,0:T(8,128)(2,1)}), bf16[2,1024,1024]{2,1,0:T(8,128)(2,1)}, u32[]{:S(2)}, u32[]{:S(2)}) async-start(bf16[2,1024,1024]{2,1,0:T(8,128)(2,1)} %get-tuple-element.525.p), calls=%async_computation.3 | async-start | bytes 8388608 | tf_op jit(solution)/shard_map/all_to_all | solution.py:73
  427.8 42.5 %collective-permute-start.47 = (bf16[2,256,1024]{2,1,0:T(8,128)(2,1)}, bf16[2,256,1024]{2,1,0:T(8,128)(2,1)}, u32[]{:S(2)}, u32[]{:S(2)}) collective-permute-start(bf16[2,256,1024]{2,1,0:T(8,128)(2,1)} %pad_maximum_fusion.21), channel_id=1, source_target_pairs={{0,8},{2,10},{4,12},{6,14},{8,0},{10,2},{12,4},{14,6},{16,24},{18,... | collective-permute-start | bytes 3145736 | tf_op jit(solution)/shard_map/ppermute | solution.py:113
  428.5 19.3 %collective-permute-start.34 = (bf16[96,1024]{1,0:T(8,128)(2,1)S(1)}, bf16[96,1024]{1,0:T(8,128)(2,1)S(1)}, u32[]{:S(2)}, u32[]{:S(2)}) collective-permute-start(bf16[96,1024]{1,0:T(8,128)(2,1)S(1)} %get-tuple-element.790), channel_id=1, source_target_pairs={{0,2},{2,0},{4,6},{6,4},{8,10},{10,8},{12,14},{14,12},{16,18},{18,... | collective-permute-start | bytes 589832 | tf_op jit(solution)/shard_map/ppermute | solution.py:113
  430.0 17.8 %collective-permute-start.33 = (bf16[96,1024]{1,0:T(8,128)(2,1)S(1)}, bf16[96,1024]{1,0:T(8,128)(2,1)S(1)}, u32[]{:S(2)}, u32[]{:S(2)}) collective-permute-start(bf16[96,1024]{1,0:T(8,128)(2,1)S(1)} %get-tuple-element.792), channel_id=1, source_target_pairs={{0,4},{2,6},{4,0},{6,2},{8,12},{10,14},{12,8},{14,10},{16,20},{18,... | collective-permute-start | bytes 589832 | tf_op jit(solution)/shard_map/ppermute | solution.py:113
  432.5 40.4 %collective-permute-start.41 = (bf16[640,1024]{1,0:T(8,128)(2,1)}, bf16[640,1024]{1,0:T(8,128)(2,1)}, u32[]{:S(2)}, u32[]{:S(2)}) collective-permute-start(bf16[640,1024]{1,0:T(8,128)(2,1)} %get-tuple-element.684), channel_id=1, source_target_pairs={{0,4},{2,6},{4,0},{6,2},{8,12},{10,14},{12,8},{14,10},{16,20},{18,... | collective-permute-start | bytes 3932168 | tf_op jit(solution)/shard_map/ppermute | solution.py:113
  433.3 39.5 %collective-permute-start.40 = (bf16[640,1024]{1,0:T(8,128)(2,1)}, bf16[640,1024]{1,0:T(8,128)(2,1)}, u32[]{:S(2)}, u32[]{:S(2)}) collective-permute-start(bf16[640,1024]{1,0:T(8,128)(2,1)} %get-tuple-element.686), channel_id=1, source_target_pairs={{0,2},{2,0},{4,6},{6,4},{8,10},{10,8},{12,14},{14,12},{16,18},{18,... | collective-permute-start | bytes 3932168 | tf_op jit(solution)/shard_map/ppermute | solution.py:113
  448.7 26.1 %collective-permute-start.39 = (bf16[2,96,1024]{2,1,0:T(8,128)(2,1)}, bf16[2,96,1024]{2,1,0:T(8,128)(2,1)}, u32[]{:S(2)}, u32[]{:S(2)}) collective-permute-start(bf16[2,96,1024]{2,1,0:T(8,128)(2,1)} %pad_maximum_fusion.33), channel_id=1, source_target_pairs={{0,16},{2,18},{4,20},{6,22},{8,24},{10,26},{12,28},{14,30},{16,0},... | collective-permute-start | bytes 1179656 | tf_op jit(solution)/shard_map/ppermute | solution.py:113
  468.8 24.1 %collective-permute-start.45 = (bf16[512,1024]{1,0:T(8,128)(2,1)}, bf16[512,1024]{1,0:T(8,128)(2,1)}, u32[]{:S(2)}, u32[]{:S(2)}) collective-permute-start(bf16[512,1024]{1,0:T(8,128)(2,1)} %get-tuple-element.548), channel_id=1, source_target_pairs={{0,2},{2,0},{4,6},{6,4},{8,10},{10,8},{12,14},{14,12},{16,18},{18,... | collective-permute-start | bytes 3145736 | tf_op jit(solution)/shard_map/ppermute | solution.py:113
  470.4 22.7 %collective-permute-start.46 = (bf16[512,1024]{1,0:T(8,128)(2,1)}, bf16[512,1024]{1,0:T(8,128)(2,1)S(1)}, u32[]{:S(2)}, u32[]{:S(2)}) collective-permute-start(bf16[512,1024]{1,0:T(8,128)(2,1)} %get-tuple-element.549), channel_id=1, source_target_pairs={{0,4},{2,6},{4,0},{6,2},{8,12},{10,14},{12,8},{14,10},{16,20},{18,... | collective-permute-start | bytes 3145736 | tf_op jit(solution)/shard_map/ppermute | solution.py:113
  497.5 51.2 %collective-permute-start.44 = (bf16[2,320,1024]{2,1,0:T(8,128)(2,1)S(1)}, bf16[2,320,1024]{2,1,0:T(8,128)(2,1)S(1)}, u32[]{:S(2)}, u32[]{:S(2)}) collective-permute-start(bf16[2,320,1024]{2,1,0:T(8,128)(2,1)S(1)} %pad_maximum_fusion.9), channel_id=1, source_target_pairs={{0,8},{2,10},{4,12},{6,14},{8,0},{10,2},{12,4},{14,6},{16,24},{18,... | collective-permute-start | bytes 3932168 | tf_op jit(solution)/shard_map/ppermute | solution.py:113
  499.9 48.0 %collective-permute-start.52 = (bf16[2,256,1024]{2,1,0:T(8,128)(2,1)S(1)}, bf16[2,256,1024]{2,1,0:T(8,128)(2,1)S(1)}, u32[]{:S(2)}, u32[]{:S(2)}) collective-permute-start(bf16[2,256,1024]{2,1,0:T(8,128)(2,1)S(1)} %pad_maximum_fusion.22), channel_id=1, source_target_pairs={{0,8},{2,10},{4,12},{6,14},{8,0},{10,2},{12,4},{14,6},{16,24},{18,... | collective-permute-start | bytes 3145736 | tf_op jit(solution)/shard_map/ppermute | solution.py:113
  502.9 47.1 %collective-permute-start.42 = (bf16[96,1024]{1,0:T(8,128)(2,1)S(1)}, bf16[96,1024]{1,0:T(8,128)(2,1)S(1)}, u32[]{:S(2)}, u32[]{:S(2)}) collective-permute-start(bf16[96,1024]{1,0:T(8,128)(2,1)S(1)} %get-tuple-element.557), channel_id=1, source_target_pairs={{0,4},{2,6},{4,0},{6,2},{8,12},{10,14},{12,8},{14,10},{16,20},{18,... | collective-permute-start | bytes 589832 | tf_op jit(solution)/shard_map/ppermute | solution.py:113
  503.9 99.3 %collective-permute-start.48 = (bf16[512,1024]{1,0:T(8,128)(2,1)S(1)}, bf16[512,1024]{1,0:T(8,128)(2,1)}, u32[]{:S(2)}, u32[]{:S(2)}) collective-permute-start(bf16[512,1024]{1,0:T(8,128)(2,1)S(1)} %maximum_select_fusion.16), channel_id=1, source_target_pairs={{0,2},{2,0},{4,6},{6,4},{8,10},{10,8},{12,14},{14,12},{16,18},{18,... | collective-permute-start | bytes 3145736 | tf_op jit(solution)/shard_map/ppermute | solution.py:113
  504.5 45.5 %collective-permute-start.43 = (bf16[96,1024]{1,0:T(8,128)(2,1)S(1)}, bf16[96,1024]{1,0:T(8,128)(2,1)S(1)}, u32[]{:S(2)}, u32[]{:S(2)}) collective-permute-start(bf16[96,1024]{1,0:T(8,128)(2,1)S(1)} %get-tuple-element.559), channel_id=1, source_target_pairs={{0,2},{2,0},{4,6},{6,4},{8,10},{10,8},{12,14},{14,12},{16,18},{18,... | collective-permute-start | bytes 589832 | tf_op jit(solution)/shard_map/ppermute | solution.py:113
  547.9 54.9 %collective-permute-start.49 = (bf16[512,1024]{1,0:T(8,128)(2,1)S(1)}, bf16[512,1024]{1,0:T(8,128)(2,1)}, u32[]{:S(2)}, u32[]{:S(2)}) collective-permute-start(bf16[512,1024]{1,0:T(8,128)(2,1)S(1)} %maximum_select_fusion.17), channel_id=1, source_target_pairs={{0,4},{2,6},{4,0},{6,2},{8,12},{10,14},{12,8},{14,10},{16,20},{18,... | collective-permute-start | bytes 3145736 | tf_op jit(solution)/shard_map/ppermute | solution.py:113
  561.9 65.1 %collective-permute-start.57 = (bf16[512,1024]{1,0:T(8,128)(2,1)}, bf16[512,1024]{1,0:T(8,128)(2,1)}, u32[]{:S(2)}, u32[]{:S(2)}) collective-permute-start(bf16[512,1024]{1,0:T(8,128)(2,1)} %get-tuple-element.571), channel_id=1, source_target_pairs={{0,2},{2,0},{4,6},{6,4},{8,10},{10,8},{12,14},{14,12},{16,18},{18,... | collective-permute-start | bytes 3145736 | tf_op jit(solution)/shard_map/ppermute | solution.py:113
  563.5 27.6 %collective-permute-start.54 = (bf16[128,1024]{1,0:T(8,128)(2,1)}, bf16[128,1024]{1,0:T(8,128)(2,1)}, u32[]{:S(2)}, u32[]{:S(2)}) collective-permute-start(bf16[128,1024]{1,0:T(8,128)(2,1)} %get-tuple-element.772), channel_id=1, source_target_pairs={{0,2},{2,0},{4,6},{6,4},{8,10},{10,8},{12,14},{14,12},{16,18},{18,... | collective-permute-start | bytes 786440 | tf_op jit(solution)/shard_map/ppermute | solution.py:113
  566.0 25.6 %collective-permute-start.53 = (bf16[128,1024]{1,0:T(8,128)(2,1)}, bf16[128,1024]{1,0:T(8,128)(2,1)}, u32[]{:S(2)}, u32[]{:S(2)}) collective-permute-start(bf16[128,1024]{1,0:T(8,128)(2,1)} %get-tuple-element.774), channel_id=1, source_target_pairs={{0,4},{2,6},{4,0},{6,2},{8,12},{10,14},{12,8},{14,10},{16,20},{18,... | collective-permute-start | bytes 786440 | tf_op jit(solution)/shard_map/ppermute | solution.py:113
  567.2 48.3 %all-to-all-start.5 = ((bf16[2,1024,1024]{2,1,0:T(8,128)(2,1)}), bf16[2,1024,1024]{2,1,0:T(8,128)(2,1)}, u32[]{:S(2)}, u32[]{:S(2)}) async-start(bf16[2,1024,1024]{2,1,0:T(8,128)(2,1)} %get-tuple-element.588.p), calls=%async_computation.5 | async-start | bytes 8388608 | tf_op jit(solution)/shard_map/all_to_all | solution.py:73
  598.1 45.4 %collective-permute-start.64 = (bf16[2,192,1024]{2,1,0:T(8,128)(2,1)}, bf16[2,192,1024]{2,1,0:T(8,128)(2,1)}, u32[]{:S(2)}, u32[]{:S(2)}) collective-permute-start(bf16[2,192,1024]{2,1,0:T(8,128)(2,1)} %pad_maximum_fusion.27), channel_id=1, source_target_pairs={{0,8},{2,10},{4,12},{6,14},{8,0},{10,2},{12,4},{14,6},{16,24},{18,... | collective-permute-start | bytes 2359304 | tf_op jit(solution)/shard_map/ppermute | solution.py:113
  601.4 28.0 %collective-permute-start.58 = (bf16[512,1024]{1,0:T(8,128)(2,1)}, bf16[512,1024]{1,0:T(8,128)(2,1)}, u32[]{:S(2)}, u32[]{:S(2)}) collective-permute-start(bf16[512,1024]{1,0:T(8,128)(2,1)} %get-tuple-element.606), channel_id=1, source_target_pairs={{0,4},{2,6},{4,0},{6,2},{8,12},{10,14},{12,8},{14,10},{16,20},{18,... | collective-permute-start | bytes 3145736 | tf_op jit(solution)/shard_map/ppermute | solution.py:113
  602.8 36.8 %collective-permute-start.56 = (bf16[2,128,1024]{2,1,0:T(8,128)(2,1)S(1)}, bf16[2,128,1024]{2,1,0:T(8,128)(2,1)}, u32[]{:S(2)}, u32[]{:S(2)}) collective-permute-start(bf16[2,128,1024]{2,1,0:T(8,128)(2,1)S(1)} %pad_maximum_fusion.31), channel_id=1, source_target_pairs={{0,16},{2,18},{4,20},{6,22},{8,24},{10,26},{12,28},{14,30},{16,0},... | collective-permute-start | bytes 1572872 | tf_op jit(solution)/shard_map/ppermute | solution.py:113
  603.2 69.1 %collective-permute-start.62 = (bf16[2,160,1024]{2,1,0:T(8,128)(2,1)S(1)}, bf16[2,160,1024]{2,1,0:T(8,128)(2,1)}, u32[]{:S(2)}, u32[]{:S(2)}) collective-permute-start(bf16[2,160,1024]{2,1,0:T(8,128)(2,1)S(1)} %pad_maximum_fusion.28), channel_id=1, source_target_pairs={{0,16},{2,18},{4,20},{6,22},{8,24},{10,26},{12,28},{14,30},{16,0},... | collective-permute-start | bytes 1966088 | tf_op jit(solution)/shard_map/ppermute | solution.py:113
  627.0 21.1 %collective-permute-start.55 = (f32[12,512]{1,0:T(8,128)S(1)}, f32[12,512]{1,0:T(8,128)S(1)}, u32[]{:S(2)}, u32[]{:S(2)}) collective-permute-start(f32[12,512]{1,0:T(8,128)S(1)} %concatenate.621), channel_id=1, source_target_pairs={{0,2},{2,0},{4,6},{6,4},{8,10},{10,8},{12,14},{14,12},{16,18},{18,... | collective-permute-start | bytes 73736 | tf_op jit(solution)/shard_map/ppermute | solution.py:113
  643.5 27.8 %collective-permute-start.63 = (bf16[2,256,1024]{2,1,0:T(8,128)(2,1)S(1)}, bf16[2,256,1024]{2,1,0:T(8,128)(2,1)S(1)}, u32[]{:S(2)}, u32[]{:S(2)}) collective-permute-start(bf16[2,256,1024]{2,1,0:T(8,128)(2,1)S(1)} %pad_maximum_fusion.24), channel_id=1, source_target_pairs={{0,8},{2,10},{4,12},{6,14},{8,0},{10,2},{12,4},{14,6},{16,24},{18,... | collective-permute-start | bytes 3145736 | tf_op jit(solution)/shard_map/ppermute | solution.py:113
  648.0 55.7 %collective-permute-start.66 = (bf16[2,256,1024]{2,1,0:T(8,128)(2,1)S(1)}, bf16[2,256,1024]{2,1,0:T(8,128)(2,1)S(1)}, u32[]{:S(2)}, u32[]{:S(2)}) collective-permute-start(bf16[2,256,1024]{2,1,0:T(8,128)(2,1)S(1)} %pad_maximum_fusion.23), channel_id=1, source_target_pairs={{0,8},{2,10},{4,12},{6,14},{8,0},{10,2},{12,4},{14,6},{16,24},{18,... | collective-permute-start | bytes 3145736 | tf_op jit(solution)/shard_map/ppermute | solution.py:113
  648.1 26.7 %collective-permute-start.61 = (f32[12,512]{1,0:T(8,128)S(1)}, f32[12,512]{1,0:T(8,128)S(1)}, u32[]{:S(2)}, u32[]{:S(2)}) collective-permute-start(f32[12,512]{1,0:T(8,128)S(1)} %add.402), channel_id=1, source_target_pairs={{0,4},{2,6},{4,0},{6,2},{8,12},{10,14},{12,8},{14,10},{16,20},{18,... | collective-permute-start | bytes 73736 | tf_op jit(solution)/shard_map/ppermute | solution.py:113
  650.2 24.7 %collective-permute-start.70 = (bf16[384,1024]{1,0:T(8,128)(2,1)S(1)}, bf16[384,1024]{1,0:T(8,128)(2,1)S(1)}, u32[]{:S(2)}, u32[]{:S(2)}) collective-permute-start(bf16[384,1024]{1,0:T(8,128)(2,1)S(1)} %maximum_select_fusion.23), channel_id=1, source_target_pairs={{0,4},{2,6},{4,0},{6,2},{8,12},{10,14},{12,8},{14,10},{16,20},{18,... | collective-permute-start | bytes 2359304 | tf_op jit(solution)/shard_map/ppermute | solution.py:113
  671.3 20.4 %collective-permute-start.69 = (bf16[384,1024]{1,0:T(8,128)(2,1)S(1)}, bf16[384,1024]{1,0:T(8,128)(2,1)S(1)}, u32[]{:S(2)}, u32[]{:S(2)}) collective-permute-start(bf16[384,1024]{1,0:T(8,128)(2,1)S(1)} %maximum_select_fusion.22), channel_id=1, source_target_pairs={{0,2},{2,0},{4,6},{6,4},{8,10},{10,8},{12,14},{14,12},{16,18},{18,... | collective-permute-start | bytes 2359304 | tf_op jit(solution)/shard_map/ppermute | solution.py:113
  673.7 33.4 %collective-permute-start.75 = (bf16[160,1024]{1,0:T(8,128)(2,1)S(1)}, bf16[160,1024]{1,0:T(8,128)(2,1)S(1)}, u32[]{:S(2)}, u32[]{:S(2)}) collective-permute-start(bf16[160,1024]{1,0:T(8,128)(2,1)S(1)} %get-tuple-element.644), channel_id=1, source_target_pairs={{0,4},{2,6},{4,0},{6,2},{8,12},{10,14},{12,8},{14,10},{16,20},{18,... | collective-permute-start | bytes 983048 | tf_op jit(solution)/shard_map/ppermute | solution.py:113
  674.8 31.0 %collective-permute-start.65 = (f32[12,512]{1,0:T(8,128)S(1)}, f32[12,512]{1,0:T(8,128)S(1)}, u32[]{:S(2)}, u32[]{:S(2)}) collective-permute-start(f32[12,512]{1,0:T(8,128)S(1)} %add.406), channel_id=1, source_target_pairs={{0,8},{2,10},{4,12},{6,14},{8,0},{10,2},{12,4},{14,6},{16,24},{18,... | collective-permute-start | bytes 73736 | tf_op jit(solution)/shard_map/ppermute | solution.py:113
  703.6 15.7 %collective-permute-start.74 = (bf16[2,128,1024]{2,1,0:T(8,128)(2,1)S(1)}, bf16[2,128,1024]{2,1,0:T(8,128)(2,1)S(1)}, u32[]{:S(2)}, u32[]{:S(2)}) collective-permute-start(bf16[2,128,1024]{2,1,0:T(8,128)(2,1)S(1)} %pad_maximum_fusion.32), channel_id=1, source_target_pairs={{0,16},{2,18},{4,20},{6,22},{8,24},{10,26},{12,28},{14,30},{16,0},... | collective-permute-start | bytes 1572872 | tf_op jit(solution)/shard_map/ppermute | solution.py:113
  704.2 28.7 %collective-permute-start.72 = (bf16[512,1024]{1,0:T(8,128)(2,1)S(1)}, bf16[512,1024]{1,0:T(8,128)(2,1)S(1)}, u32[]{:S(2)}, u32[]{:S(2)}) collective-permute-start(bf16[512,1024]{1,0:T(8,128)(2,1)S(1)} %maximum_select_fusion.18), channel_id=1, source_target_pairs={{0,2},{2,0},{4,6},{6,4},{8,10},{10,8},{12,14},{14,12},{16,18},{18,... | collective-permute-start | bytes 3145736 | tf_op jit(solution)/shard_map/ppermute | solution.py:113
  706.2 26.1 %collective-permute-start.73 = (bf16[512,1024]{1,0:T(8,128)(2,1)S(1)}, bf16[512,1024]{1,0:T(8,128)(2,1)S(1)}, u32[]{:S(2)}, u32[]{:S(2)}) collective-permute-start(bf16[512,1024]{1,0:T(8,128)(2,1)S(1)} %maximum_select_fusion.19), channel_id=1, source_target_pairs={{0,4},{2,6},{4,0},{6,2},{8,12},{10,14},{12,8},{14,10},{16,20},{18,... | collective-permute-start | bytes 3145736 | tf_op jit(solution)/shard_map/ppermute | solution.py:113
  707.0 32.4 %collective-permute-start.71 = (f32[12,512]{1,0:T(8,128)S(1)}, f32[12,512]{1,0:T(8,128)S(1)}, u32[]{:S(2)}, u32[]{:S(2)}) collective-permute-start(f32[12,512]{1,0:T(8,128)S(1)} %add.410), channel_id=1, source_target_pairs={{0,16},{2,18},{4,20},{6,22},{8,24},{10,26},{12,28},{14,30},{16,0},... | collective-permute-start | bytes 73736 | tf_op jit(solution)/shard_map/ppermute | solution.py:113
  710.6 31.0 %collective-permute-start.80 = (bf16[2,320,1024]{2,1,0:T(8,128)(2,1)S(1)}, bf16[2,320,1024]{2,1,0:T(8,128)(2,1)S(1)}, u32[]{:S(2)}, u32[]{:S(2)}) collective-permute-start(bf16[2,320,1024]{2,1,0:T(8,128)(2,1)S(1)} %pad_maximum_fusion.10), channel_id=1, source_target_pairs={{0,8},{2,10},{4,12},{6,14},{8,0},{10,2},{12,4},{14,6},{16,24},{18,... | collective-permute-start | bytes 3932168 | tf_op jit(solution)/shard_map/ppermute | solution.py:113
  719.6 19.9 %collective-permute-start.77 = (bf16[128,1024]{1,0:T(8,128)(2,1)S(1)}, bf16[128,1024]{1,0:T(8,128)(2,1)S(1)}, u32[]{:S(2)}, u32[]{:S(2)}) collective-permute-start(bf16[128,1024]{1,0:T(8,128)(2,1)S(1)} %get-tuple-element.656), channel_id=1, source_target_pairs={{0,4},{2,6},{4,0},{6,2},{8,12},{10,14},{12,8},{14,10},{16,20},{18,... | collective-permute-start | bytes 786440 | tf_op jit(solution)/shard_map/ppermute | solution.py:113
  741.5 14.9 %collective-permute-start.79 = (bf16[2,256,1024]{2,1,0:T(8,128)(2,1)S(1)}, bf16[2,256,1024]{2,1,0:T(8,128)(2,1)S(1)}, u32[]{:S(2)}, u32[]{:S(2)}) collective-permute-start(bf16[2,256,1024]{2,1,0:T(8,128)(2,1)S(1)} %pad_maximum_fusion.25), channel_id=1, source_target_pairs={{0,8},{2,10},{4,12},{6,14},{8,0},{10,2},{12,4},{14,6},{16,24},{18,... | collective-permute-start | bytes 3145736 | tf_op jit(solution)/shard_map/ppermute | solution.py:113
  742.3 19.7 %collective-permute-start.84 = (bf16[640,1024]{1,0:T(8,128)(2,1)S(1)}, bf16[640,1024]{1,0:T(8,128)(2,1)S(1)}, u32[]{:S(2)}, u32[]{:S(2)}) collective-permute-start(bf16[640,1024]{1,0:T(8,128)(2,1)S(1)} %maximum_select_fusion.13), channel_id=1, source_target_pairs={{0,4},{2,6},{4,0},{6,2},{8,12},{10,14},{12,8},{14,10},{16,20},{18,... | collective-permute-start | bytes 3932168 | tf_op jit(solution)/shard_map/ppermute | solution.py:113
  743.2 20.8 %collective-permute-start.83 = (bf16[640,1024]{1,0:T(8,128)(2,1)S(1)}, bf16[640,1024]{1,0:T(8,128)(2,1)S(1)}, u32[]{:S(2)}, u32[]{:S(2)}) collective-permute-start(bf16[640,1024]{1,0:T(8,128)(2,1)S(1)} %maximum_select_fusion.12), channel_id=1, source_target_pairs={{0,2},{2,0},{4,6},{6,4},{8,10},{10,8},{12,14},{14,12},{16,18},{18,... | collective-permute-start | bytes 3932168 | tf_op jit(solution)/shard_map/ppermute | solution.py:113
  756.9 16.3 %collective-permute-start.82 = (bf16[512,1024]{1,0:T(8,128)(2,1)S(1)}, bf16[512,1024]{1,0:T(8,128)(2,1)S(1)}, u32[]{:S(2)}, u32[]{:S(2)}) collective-permute-start(bf16[512,1024]{1,0:T(8,128)(2,1)S(1)} %maximum_select_fusion.21), channel_id=1, source_target_pairs={{0,4},{2,6},{4,0},{6,2},{8,12},{10,14},{12,8},{14,10},{16,20},{18,... | collective-permute-start | bytes 3145736 | tf_op jit(solution)/shard_map/ppermute | solution.py:113
  757.5 17.8 %collective-permute-start.81 = (bf16[512,1024]{1,0:T(8,128)(2,1)S(1)}, bf16[512,1024]{1,0:T(8,128)(2,1)S(1)}, u32[]{:S(2)}, u32[]{:S(2)}) collective-permute-start(bf16[512,1024]{1,0:T(8,128)(2,1)S(1)} %maximum_select_fusion.20), channel_id=1, source_target_pairs={{0,2},{2,0},{4,6},{6,4},{8,10},{10,8},{12,14},{14,12},{16,18},{18,... | collective-permute-start | bytes 3145736 | tf_op jit(solution)/shard_map/ppermute | solution.py:113
  (96 other events, 783.9 us)

commit v3 on v2

--- a/solution.py
+++ b/solution.py
@@ -17,7 +17,7 @@
 BF = jnp.bfloat16
 F32 = jnp.float32
 VMEM = 56 * 1024 * 1024
-PLAN = ("", "a", "", "a", "a", "", "ba", "a", "bcab", "c", "b", "cdbac", "dc", "bedc", "eedb", "feescfdscfesdfesfdfsdf")
+PLAN = ("", "a", "", "a", "a", "", "ba", "a", "bcab", "c", "b", "cdbac", "dc", "e", "bdceedb", "feescfdscfesdfesfdfsdf")
 
 
 def dot(a, b, da=1, db=0):

time: 792 us -> 782 us (0.987)
  waiting for transfers between devices: 194 us -> 170 us
  Pallas kernels: 295 us -> 305 us
    ppermute x78, waiting for transfers between devices: 183 us -> 159 us  [exchange(): return lax.ppermute(v, 'batch', [(i, i ^ 1 << b) for i in range(n)])]
    pallas_call x23, Pallas kernels: 295 us -> 305 us  [launch(): pl.pallas_call(kernel, grid_spec=pltpu.PrefetchScalarGridSpec(num_scalar_...]
    select_n x46 -> x47, other arithmetic: 39.1 us -> 39.5 us  [joined(): return jnp.where(bit_of(b) == 1, high, low)]
  transfers between devices with their start and end apart: 89 -> 89, of which waited for: 32 -> 32; matrix products, arithmetic and copies ran while one was open for 18% -> 18% of each run, Pallas kernels for 27% -> 29%
where the time goes in v3:
time: 782 us; the launch traced here: 771 us
  Pallas kernels  305 us (39%)
  waiting for transfers between devices  170 us (22%)
  starting transfers between devices  116 us (15%)
  other arithmetic  107 us (14%)
  local copies, waits for them, and re-layouts  47.6 us (6%)
  blocking collectives  13.7 us (2%)
  matrix products  8.49 us (1%)
    pallas_call x23, Pallas kernels, launch(): pl.pallas_call(kernel, grid_spec=pltpu.PrefetchScalarGridSpec(num_scalar_...  305 us
    ppermute x78, waiting for transfers between devices, exchange(): return lax.ppermute(v, 'batch', [(i, i ^ 1 << b) for i in range(n)])  159 us
    ppermute x78, starting transfers between devices, exchange(): return lax.ppermute(v, 'batch', [(i, i ^ 1 << b) for i in range(n)])  91.3 us
    select_n x47, other arithmetic, joined(): return jnp.where(bit_of(b) == 1, high, low)  39.5 us
    convert_element_type x6, other arithmetic, final(): out.append(whole[at:at + size].astype(F32))  23.8 us
    all_to_all x4, starting transfers between devices, pair_swap(): return lax.all_to_all(v, 'fsdp', 0, 0)  22.9 us
    convert_element_type x30, other arithmetic, add16(): return (a.astype(F32) + b.astype(F32)).astype(BF)  20.2 us
  transfers between devices with their start and end apart: 89, of which 32 were waited for; matrix products, arithmetic and copies ran while one was open for 18% of the time, Pallas kernels for 29%

profile of v3, /device:TPU:0, one launch (start us, length us, event | category | flops | bytes accessed | tf_op | source)
XLA Modules:
  0.0 771.2 jit_solution(10039410486641456616)
XLA Ops:
  1.8 6.6 packed.1
  9.4 3.6 placed.2.refs_0_.base.x
  13.1 15.8 %ffn_forward.2 = (bf16[1024,1024]{1,0:T(8,128)(2,1)}, bf16[1024,2048]{1,0:T(8,128)(2,1)}, bf16[1024,1024]{1,0:T(8,128)(2,1)}) custom-call(s32[10]{0:T(128)} %stack.202.place, bf16[1024,1024]{1,0:T(8,128)(2,1)} %placed.2.refs_0_.base.x, f32[1,1024]{1,0:T(1,128)} %bitcast.242, bf16[2048,1024]{1,0:T(8,128)(2,1)} %up.1, bf16[2048,1024]{1,0:T(8,128)(2,1)} %down.1), custom_call_target="tpu_custom_call" | custom-call | flops 1 | bytes 1 | tf_op jit(solution)/shard_map/ffn_forward/pallas_call | solution.py:290
  37.2 10.4 %qkv.1 = (f32[1024,1024]{1,0:T(8,128)}, bf16[1024,1024]{1,0:T(8,128)(2,1)}, bf16[1024,512]{1,0:T(8,128)(2,1)}, bf16[1024,512]{1,0:T(8,128)(2,1)}, bf16[1024,512]{1,0:T(8,128)(2,1)}, /*index=5*/bf16[1024,512]{1,0:T(8,128)(2,1)}) custom-call(s32[10]{0:T(128)} %stack.202.place, bf16[1024,1024]{1,0:T(8,128)(2,1)} %placed.2.refs_0_.base.x, ...), custom_call_target="tpu_custom_call" | custom-call | flops 1 | bytes 1 | tf_op jit(solution)/shard_map/qkv/pallas_call | solution.py:290
  47.7 19.0 %attention_forward.1 = (bf16[1024,512]{1,0:T(8,128)(2,1)}, bf16[1024,1024]{1,0:T(8,128)(2,1)}) custom-call(s32[10]{0:T(128)} %stack.202.place, s32[1024,1]{1,0:T(8,128)} %copy.61.segq, s32[1,1024]{1,0:T(1,128)} %segk.5, bf16[1024,512]{1,0:T(8,128)(2,1)} %get-tuple-element.470.qc, bf16[1024,512]{1,0:T(8,128)(2,1)} %get-tuple-element.471.qp, ...), custom_call_target="tpu_custom_call" | custom-call | flops 1 | bytes 1 | tf_op jit(solution)/shard_map/attention_forward/pallas_call | solution.py:290
  72.4 13.9 %conv_forward.1 = (f32[1024,1024]{1,0:T(8,128)}, bf16[1024,1024]{1,0:T(8,128)(2,1)}, bf16[1024,1024]{1,0:T(8,128)(2,1)}, f32[1024,512]{1,0:T(8,128)}, f32[3,512]{1,0:T(4,128)}) custom-call(s32[10]{0:T(128)} %stack.202.place, f32[1024,1024]{1,0:T(8,128)} %get-tuple-element.528.base.x, bf16[1024,1024]{1,0:T(8,128)(2,1)} %get-tuple-element.360.p, ...), custom_call_target="tpu_custom_call" | custom-call | flops 1 | bytes 1 | tf_op jit(solution)/shard_map/conv_forward/pallas_call | solution.py:290
  86.3 2.7 collective-permute-start.4
  98.9 3.0 collective-permute-start.7
  104.2 5.7 batch_forward.1
  109.9 4.4 collective-permute-done.8.refs_2_
  115.6 17.0 %ffn_forward.3 = (f32[1024,1024]{1,0:T(8,128)}, bf16[1024,1024]{1,0:T(8,128)(2,1)}, bf16[1024,2048]{1,0:T(8,128)(2,1)}, bf16[1024,1024]{1,0:T(8,128)(2,1)}) custom-call(s32[10]{0:T(128)} %stack.202.place, f32[1024,1024]{1,0:T(8,128)} %get-tuple-element.437.refs_0_.x, bf16[1024,1024]{1,0:T(8,128)(2,1)} %get-tuple-element.364.refs_1_, ...), custom_call_target="tpu_custom_call" | custom-call | flops 1 | bytes 1 | tf_op jit(solution)/shard_map/ffn_forward/pallas_call | solution.py:290
  133.1 5.1 collective-permute-done.10.other
  139.2 3.6 placed.3.cot
  144.1 14.1 %final_down.1 = (bf16[1024,1024]{1,0:T(8,128)(2,1)}, f32[1024,1024]{1,0:T(8,128)}, bf16[1024,1024]{1,0:T(8,128)(2,1)}, f32[1,1024]{1,0:T(1,128)}, bf16[512,1024]{1,0:T(8,128)(2,1)}, /*index=5*/bf16[512,1024]{1,0:T(8,128)(2,1)}) custom-call(s32[10]{0:T(128)} %stack.202.place, f32[1024,1024]{1,0:T(8,128)} %get-tuple-element.393.x, ...), custom_call_target="tpu_custom_call" | custom-call | flops 1 | bytes 1 | tf_op jit(solution)/shard_map/final_down/pallas_call | solution.py:290
  161.6 6.6 down_keep.1
  168.2 26.7 %ffn_back.2 = (bf16[2,1024,1024]{2,1,0:T(8,128)(2,1)}, bf16[1024,2048]{1,0:T(8,128)(2,1)}) custom-call(s32[10]{0:T(128)} %stack.202.place, bf16[1024,1024]{1,0:T(8,128)(2,1)} %get-tuple-element.372.gf, bf16[1024,2048]{1,0:T(8,128)(2,1)} %get-tuple-element.373.pre, bf16[2048,1024]{1,0:T(8,128)(2,1)} %up, bf16[2048,1024]{1,0:T(8,128)(2,1)} %down), custom_call_target="tpu_custom_call" | custom-call | flops 1 | bytes 1 | tf_op jit(solution)/shard_map/ffn_back/pallas_call | solution.py:290
  198.4 5.6 all-to-all-start
  204.1 9.9 %up_grad.2 = (bf16[512,1024]{1,0:T(8,128)(2,1)}, bf16[512,1024]{1,0:T(8,128)(2,1)}, bf16[512,1024]{1,0:T(8,128)(2,1)}, bf16[512,1024]{1,0:T(8,128)(2,1)}) custom-call(s32[10]{0:T(128)} %stack.202.place, bf16[1024,2048]{1,0:T(8,128)(2,1)} %get-tuple-element.387.ga, bf16[1024,1024]{1,0:T(8,128)(2,1)} %get-tuple-element.388.u), custom_call_target="tpu_custom_call" | custom-call | flops 1 | bytes 1 | tf_op jit(solution)/shard_map/up_grad/pallas_call | solution.py:290
  213.9 13.2 %conv_back_one.1 = (f32[1024,1024]{1,0:T(8,128)}, f32[1,1024]{1,0:T(1,128)}, f32[1024,512]{1,0:T(8,128)}, f32[2,512]{1,0:T(2,128)}, bf16[512,1024]{1,0:T(8,128)(2,1)}) custom-call(s32[10]{0:T(128)} %stack.202.place, bf16[2,1024,1024]{2,1,0:T(8,128)(2,1)} %get-tuple-element.390.p, bf16[2,1024,1024]{2,1,0:T(8,128)(2,1)} %all-to-all-done.r, ...), custom_call_target="tpu_custom_call" | custom-call | flops 1 | bytes 1 | tf_op jit(solution)/shard_map/conv_back_one/pallas_call | solution.py:290
  230.5 5.9 collective-permute-done.14
  236.9 3.1 collective-permute-done.15
  240.5 3.2 collective-permute-done.16
  252.4 2.6 collective-permute-start.20
  254.9 17.2 %conv_back_two.1 = (bf16[2,1024,1024]{2,1,0:T(8,128)(2,1)}, bf16[1024,1024]{1,0:T(8,128)(2,1)}, f32[5,512]{1,0:T(8,128)}) custom-call(s32[10]{0:T(128)} %stack.202.place, f32[1024,512]{1,0:T(8,128)} %get-tuple-element.415.gbo, f32[1024,512]{1,0:T(8,128)} %get-tuple-element.395.dc, bf16[1024,1024]{1,0:T(8,128)(2,1)} %get-tuple-element.416.gp.gp_lag, ...), custom_call_target="tpu_custom_call" | custom-call | flops 1 | bytes 1 | tf_op jit(solution)/shard_map/conv_back_two/pallas_call | solution.py:290
  272.2 6.6 all_to_all.30
  278.8 5.9 all-to-all-start.1
  296.4 12.2 %context_back.1 = (f32[1024,1024]{1,0:T(8,128)}, f32[1,1024]{1,0:T(1,128)}, bf16[1024,512]{1,0:T(8,128)(2,1)}, bf16[512,1024]{1,0:T(8,128)(2,1)}) custom-call(s32[10]{0:T(128)} %stack.202.place, bf16[2,1024,1024]{2,1,0:T(8,128)(2,1)} %get-tuple-element.434.p, bf16[2,1024,1024]{2,1,0:T(8,128)(2,1)} %all-to-all-done.1.r, f32[1024,1024]{1,0:T(8,128)} %get-tuple-element.436.g, ...), custom_call_target="tpu_custom_call" | custom-call | flops 1 | bytes 1 | tf_op jit(solution)/shard_map/context_back/pallas_call | solution.py:290
  312.6 22.1 %attention_back.2 = (bf16[1024,256]{1,0:T(8,128)(2,1)}, bf16[1024,256]{1,0:T(8,128)(2,1)}, bf16[1024,256]{1,0:T(8,128)(2,1)}, f32[1024,256]{1,0:T(8,128)}, f32[1,256]{1,0:T(1,128)}, /*index=5*/f32[1,256]{1,0:T(1,128)}) custom-call(s32[10]{0:T(128)} %stack.202.place, s32[1024,1]{1,0:T(8,128)} %copy.61.segq, s32[1,1024]{1,0:T(1,128)} %segk.5, ...), custom_call_target="tpu_custom_call" | custom-call | flops 1 | bytes 1 | tf_op jit(solution)/shard_map/attention_back/pallas_call | solution.py:290
  340.2 4.4 fusion.11
  350.6 21.9 %attention_back.3 = (bf16[1024,256]{1,0:T(8,128)(2,1)}, bf16[1024,256]{1,0:T(8,128)(2,1)}, bf16[1024,256]{1,0:T(8,128)(2,1)}, f32[1024,256]{1,0:T(8,128)}, f32[1,256]{1,0:T(1,128)}, /*index=5*/f32[1,256]{1,0:T(1,128)}) custom-call(s32[10]{0:T(128)} %stack.202.place, s32[1024,1]{1,0:T(8,128)} %copy.61.segq, s32[1,1024]{1,0:T(1,128)} %segk.5, ...), custom_call_target="tpu_custom_call" | custom-call | flops 1 | bytes 1 | tf_op jit(solution)/shard_map/attention_back/pallas_call | solution.py:290
  375.0 3.0 fusion.2
  382.4 13.4 %projections_back.1 = (bf16[2,1024,1024]{2,1,0:T(8,128)(2,1)}, bf16[1024,1536]{1,0:T(8,128)(2,1)}) custom-call(s32[10]{0:T(128)} %stack.202.place, bf16[1024,256]{1,0:T(8,128)(2,1)} %get-tuple-element.485.refs_0_, bf16[1024,256]{1,0:T(8,128)(2,1)} %get-tuple-element.486.refs_1_, bf16[1024,256]{1,0:T(8,128)(2,1)} %get-tuple-element.487.refs_2_, ...), custom_call_target="tpu_custom_call" | custom-call | flops 1 | bytes 1 | tf_op jit(solution)/shard_map/projections_back/pallas_call | solution.py:290
  400.9 7.1 all_to_all.31
  413.9 5.6 all-to-all-start.3
  422.1 9.9 %collective-permute-done.32 = bf16[2,192,1024]{2,1,0:T(8,128)(2,1)} collective-permute-done((bf16[2,192,1024]{2,1,0:T(8,128)(2,1)}, bf16[2,192,1024]{2,1,0:T(8,128)(2,1)}, u32[]{:S(2)}, u32[]{:S(2)}) %collective-permute-start.32) | collective-permute-done | bytes 786464 | tf_op jit(solution)/shard_map/ppermute | solution.py:113
  447.9 3.4 maximum_select_fusion.3
  451.2 4.5 maximum_convert_fusion
  455.9 2.6 collective-permute-start.39
  458.6 17.8 %back_down.1 = (f32[1024,1024]{1,0:T(8,128)}, bf16[1024,1024]{1,0:T(8,128)(2,1)}, f32[1,1024]{1,0:T(1,128)}, bf16[512,1024]{1,0:T(8,128)(2,1)}, bf16[512,1024]{1...) custom-call(s32[10]{0:T(128)} %stack.202.place, bf16[2,1024,1024]{2,1,0:T(8,128)(2,1)} %get-tuple-element.525.p, ...), custom_call_target="tpu_custom_call" | custom-call | flops 1 | bytes 1 | tf_op jit(solution)/shard_map/back_down/pallas_call | solution.py:290
  487.0 16.4 %ffn_back.3 = (bf16[2,1024,1024]{2,1,0:T(8,128)(2,1)}, bf16[1024,2048]{1,0:T(8,128)(2,1)}) custom-call(s32[10]{0:T(128)} %stack.202.place, bf16[1024,1024]{1,0:T(8,128)(2,1)} %get-tuple-element.539.gf, bf16[1024,2048]{1,0:T(8,128)(2,1)} %get-tuple-element.540.pre, bf16[2048,1024]{1,0:T(8,128)(2,1)} %up.1, bf16[2048,1024]{1,0:T(8,128)(2,1)} %down.1), custom_call_target="tpu_custom_call" | custom-call | flops 1 | bytes 1 | tf_op jit(solution)/shard_map/ffn_back/pallas_call | solution.py:290
  507.6 2.6 maximum_select_fusion.34
  514.0 9.9 %up_grad.3 = (bf16[512,1024]{1,0:T(8,128)(2,1)}, bf16[512,1024]{1,0:T(8,128)(2,1)}, bf16[512,1024]{1,0:T(8,128)(2,1)}, bf16[512,1024]{1,0:T(8,128)(2,1)}) custom-call(s32[10]{0:T(128)} %stack.202.place, bf16[1024,2048]{1,0:T(8,128)(2,1)} %get-tuple-element.553.ga, bf16[1024,1024]{1,0:T(8,128)(2,1)} %get-tuple-element.554.u), custom_call_target="tpu_custom_call" | custom-call | flops 1 | bytes 1 | tf_op jit(solution)/shard_map/up_grad/pallas_call | solution.py:290
  525.9 5.8 all-to-all-start.5
  539.2 15.2 %collective-permute-done.52 = bf16[96,1024]{1,0:T(8,128)(2,1)} collective-permute-done((bf16[96,1024]{1,0:T(8,128)(2,1)}, bf16[96,1024]{1,0:T(8,128)(2,1)}, u32[]{:S(2)}, u32[]{:S(2)}) %collective-permute-start.52) | collective-permute-done | bytes 196640 | tf_op jit(solution)/shard_map/ppermute | solution.py:113
  562.8 16.9 %collective-permute-done.54 = bf16[128,1024]{1,0:T(8,128)(2,1)S(1)} collective-permute-done((bf16[128,1024]{1,0:T(8,128)(2,1)S(1)}, bf16[128,1024]{1,0:T(8,128)(2,1)S(1)}, u32[]{:S(2)}, u32[]{:S(2)}) %collective-permute-start.54) | collective-permute-done | bytes 262176 | tf_op jit(solution)/shard_map/ppermute | solution.py:113
  580.9 5.9 collective-permute-done.49
  587.3 3.4 collective-permute-done.48
  592.9 2.6 collective-permute-start.62
  597.6 4.5 maximum_convert_fusion.1
  602.1 7.9 %first_back.1 = (bf16[1024,1024]{1,0:T(8,128)(2,1)}, f32[1,1024]{1,0:T(1,128)}) custom-call(s32[10]{0:T(128)} %stack.202.place, bf16[2,1024,1024]{2,1,0:T(8,128)(2,1)} %get-tuple-element.588.p, bf16[2,1024,1024]{2,1,0:T(8,128)(2,1)} %all-to-all-done.5.r, f32[1024,1024]{1,0:T(8,128)} %get-tuple-element.590.g, bf16[1024,1024]{1,0:T(8,128)(2,1)} %placed.2.refs_0_.base.x, ...), custom_call_target="tpu_custom_call" | custom-call | flops 1 | bytes 1 | tf_op jit(solution)/shard_map/first_back/pallas_call | solution.py:290
  616.9 9.5 %collective-permute-done.56 = bf16[2,128,1024]{2,1,0:T(8,128)(2,1)} collective-permute-done((bf16[2,128,1024]{2,1,0:T(8,128)(2,1)S(1)}, bf16[2,128,1024]{2,1,0:T(8,128)(2,1)}, u32[]{:S(2)}, u32[]{:S(2)}) %collective-permute-start.56) | collective-permute-done | bytes 524320 | tf_op jit(solution)/shard_map/ppermute | solution.py:113
  627.7 3.0 collective-permute-start.59
  632.5 3.9 collective-permute-done.59
  640.6 19.0 %collective-permute-done.63 = bf16[2,256,1024]{2,1,0:T(8,128)(2,1)S(1)} collective-permute-done((bf16[2,256,1024]{2,1,0:T(8,128)(2,1)S(1)}, bf16[2,256,1024]{2,1,0:T(8,128)(2,1)S(1)}, u32[]{:S(2)}, u32[]{:S(2)}) %collective-permute-start.63) | collective-permute-done | bytes 1048608 | tf_op jit(solution)/shard_map/ppermute | solution.py:113
  665.9 5.8 collective-permute-done.69
  682.6 4.7 collective-permute-done.76
  693.5 9.1 %collective-permute-done.73 = bf16[512,1024]{1,0:T(8,128)(2,1)S(1)} collective-permute-done((bf16[512,1024]{1,0:T(8,128)(2,1)S(1)}, bf16[512,1024]{1,0:T(8,128)(2,1)S(1)}, u32[]{:S(2)}, u32[]{:S(2)}) %collective-permute-start.73) | collective-permute-done | bytes 1048608 | tf_op jit(solution)/shard_map/ppermute | solution.py:113
  705.4 4.5 maximum_convert_fusion.2
  712.2 10.0 %collective-permute-done.80 = bf16[2,320,1024]{2,1,0:T(8,128)(2,1)S(1)} collective-permute-done((bf16[2,320,1024]{2,1,0:T(8,128)(2,1)S(1)}, bf16[2,320,1024]{2,1,0:T(8,128)(2,1)S(1)}, u32[]{:S(2)}, u32[]{:S(2)}) %collective-permute-start.80) | collective-permute-done | bytes 1310752 | tf_op jit(solution)/shard_map/ppermute | solution.py:113
  729.2 6.9 collective-permute-done.79
  739.9 8.1 %collective-permute-done.84 = bf16[640,1024]{1,0:T(8,128)(2,1)S(1)} collective-permute-done((bf16[640,1024]{1,0:T(8,128)(2,1)S(1)}, bf16[640,1024]{1,0:T(8,128)(2,1)S(1)}, u32[]{:S(2)}, u32[]{:S(2)}) %collective-permute-start.84) | collective-permute-done | bytes 1310752 | tf_op jit(solution)/shard_map/ppermute | solution.py:113
  750.9 4.2 slice_convert_fusion
  755.1 8.2 %collective-permute-done.82 = bf16[512,1024]{1,0:T(8,128)(2,1)S(1)} collective-permute-done((bf16[512,1024]{1,0:T(8,128)(2,1)S(1)}, bf16[512,1024]{1,0:T(8,128)(2,1)S(1)}, u32[]{:S(2)}, u32[]{:S(2)}) %collective-permute-start.82) | collective-permute-done | bytes 1048608 | tf_op jit(solution)/shard_map/ppermute | solution.py:113
  766.2 4.5 maximum_convert_fusion.3
  (479 shorter events, 215.9 us)
Async XLA Ops:
  13.0 22.1 %collective-permute-start.2 = (bf16[512,3072]{1,0:T(8,128)(2,1)}, bf16[512,3072]{1,0:T(8,128)(2,1)S(1)}, u32[]{:S(2)}, u32[]{:S(2)}) collective-permute-start(bf16[512,3072]{1,0:T(8,128)(2,1)} %get-tuple-element.354), channel_id=1, source_target_pairs={{0,1},{1,0},{2,3},{3,2},{4,5},{5,4},{6,7},{7,6},{8,9},{9,8},{10,11... | collective-permute-start | bytes 9437192 | tf_op jit(solution)/shard_map/ppermute | solution.py:47
  158.2 36.7 %collective-permute-start.11 = (bf16[512,1024]{1,0:T(8,128)(2,1)}, bf16[512,1024]{1,0:T(8,128)(2,1)S(1)}, u32[]{:S(2)}, u32[]{:S(2)}) collective-permute-start(bf16[512,1024]{1,0:T(8,128)(2,1)} %get-tuple-element.378), channel_id=1, source_target_pairs={{0,2},{2,0},{4,6},{6,4},{8,10},{10,8},{12,14},{14,12},{16,18},{18,... | collective-permute-start | bytes 3145736 | tf_op jit(solution)/shard_map/ppermute | solution.py:113
  160.0 34.8 %collective-permute-start.12 = (bf16[512,1024]{1,0:T(8,128)(2,1)}, bf16[512,1024]{1,0:T(8,128)(2,1)S(1)}, u32[]{:S(2)}, u32[]{:S(2)}) collective-permute-start(bf16[512,1024]{1,0:T(8,128)(2,1)} %get-tuple-element.379), channel_id=1, source_target_pairs={{0,4},{2,6},{4,0},{6,2},{8,12},{10,14},{12,8},{14,10},{16,20},{18,... | collective-permute-start | bytes 3145736 | tf_op jit(solution)/shard_map/ppermute | solution.py:113
  196.8 30.4 %collective-permute-start.13 = (bf16[2,256,1024]{2,1,0:T(8,128)(2,1)S(1)}, bf16[2,256,1024]{2,1,0:T(8,128)(2,1)S(1)}, u32[]{:S(2)}, u32[]{:S(2)}) collective-permute-start(bf16[2,256,1024]{2,1,0:T(8,128)(2,1)S(1)} %pad_maximum_fusion.12), channel_id=1, source_target_pairs={{0,8},{2,10},{4,12},{6,14},{8,0},{10,2},{12,4},{14,6},{16,24},{18,... | collective-permute-start | bytes 3145736 | tf_op jit(solution)/shard_map/ppermute | solution.py:113
  198.4 15.5 %all-to-all-start = ((bf16[2,1024,1024]{2,1,0:T(8,128)(2,1)}), bf16[2,1024,1024]{2,1,0:T(8,128)(2,1)}, u32[]{:S(2)}, u32[]{:S(2)}) async-start(bf16[2,1024,1024]{2,1,0:T(8,128)(2,1)} %get-tuple-element.390.p), calls=%async_computation | async-start | bytes 8388608 | tf_op jit(solution)/shard_map/all_to_all | solution.py:73
  227.5 21.2 %collective-permute-start.19 = (bf16[128,1024]{1,0:T(8,128)(2,1)S(1)}, bf16[128,1024]{1,0:T(8,128)(2,1)S(1)}, u32[]{:S(2)}, u32[]{:S(2)}) collective-permute-start(bf16[128,1024]{1,0:T(8,128)(2,1)S(1)} %get-tuple-element.784), channel_id=1, source_target_pairs={{0,2},{2,0},{4,6},{6,4},{8,10},{10,8},{12,14},{14,12},{16,18},{18,... | collective-permute-start | bytes 786440 | tf_op jit(solution)/shard_map/ppermute | solution.py:113
  228.4 20.3 %collective-permute-start.18 = (bf16[128,1024]{1,0:T(8,128)(2,1)S(1)}, bf16[128,1024]{1,0:T(8,128)(2,1)S(1)}, u32[]{:S(2)}, u32[]{:S(2)}) collective-permute-start(bf16[128,1024]{1,0:T(8,128)(2,1)S(1)} %get-tuple-element.786), channel_id=1, source_target_pairs={{0,4},{2,6},{4,0},{6,2},{8,12},{10,14},{12,8},{14,10},{16,20},{18,... | collective-permute-start | bytes 786440 | tf_op jit(solution)/shard_map/ppermute | solution.py:113
  248.9 36.1 %collective-permute-start.21 = (bf16[512,1024]{1,0:T(8,128)(2,1)}, bf16[512,1024]{1,0:T(8,128)(2,1)}, u32[]{:S(2)}, u32[]{:S(2)}) collective-permute-start(bf16[512,1024]{1,0:T(8,128)(2,1)} %get-tuple-element.428), channel_id=1, source_target_pairs={{0,2},{2,0},{4,6},{6,4},{8,10},{10,8},{12,14},{14,12},{16,18},{18,... | collective-permute-start | bytes 3145736 | tf_op jit(solution)/shard_map/ppermute | solution.py:113
  249.6 35.4 %collective-permute-start.22 = (bf16[512,1024]{1,0:T(8,128)(2,1)}, bf16[512,1024]{1,0:T(8,128)(2,1)}, u32[]{:S(2)}, u32[]{:S(2)}) collective-permute-start(bf16[512,1024]{1,0:T(8,128)(2,1)} %get-tuple-element.429), channel_id=1, source_target_pairs={{0,4},{2,6},{4,0},{6,2},{8,12},{10,14},{12,8},{14,10},{16,20},{18,... | collective-permute-start | bytes 3145736 | tf_op jit(solution)/shard_map/ppermute | solution.py:113
  252.4 39.5 %collective-permute-start.20 = (bf16[2,128,1024]{2,1,0:T(8,128)(2,1)S(1)}, bf16[2,128,1024]{2,1,0:T(8,128)(2,1)}, u32[]{:S(2)}, u32[]{:S(2)}) collective-permute-start(bf16[2,128,1024]{2,1,0:T(8,128)(2,1)S(1)} %pad_maximum_fusion.29), channel_id=1, source_target_pairs={{0,16},{2,18},{4,20},{6,22},{8,24},{10,26},{12,28},{14,30},{16,0},... | collective-permute-start | bytes 1572872 | tf_op jit(solution)/shard_map/ppermute | solution.py:113
  278.8 17.7 %all-to-all-start.1 = ((bf16[2,1024,1024]{2,1,0:T(8,128)(2,1)}), bf16[2,1024,1024]{2,1,0:T(8,128)(2,1)}, u32[]{:S(2)}, u32[]{:S(2)}) async-start(bf16[2,1024,1024]{2,1,0:T(8,128)(2,1)} %get-tuple-element.434.p), calls=%async_computation.1 | async-start | bytes 8388608 | tf_op jit(solution)/shard_map/all_to_all | solution.py:73
  291.4 45.9 %collective-permute-start.25 = (bf16[2,256,1024]{2,1,0:T(8,128)(2,1)}, bf16[2,256,1024]{2,1,0:T(8,128)(2,1)}, u32[]{:S(2)}, u32[]{:S(2)}) collective-permute-start(bf16[2,256,1024]{2,1,0:T(8,128)(2,1)} %pad_maximum_fusion.14), channel_id=1, source_target_pairs={{0,8},{2,10},{4,12},{6,14},{8,0},{10,2},{12,4},{14,6},{16,24},{18,... | collective-permute-start | bytes 3145736 | tf_op jit(solution)/shard_map/ppermute | solution.py:113
  293.1 15.5 %collective-permute-start.23 = (bf16[128,1024]{1,0:T(8,128)(2,1)S(1)}, bf16[128,1024]{1,0:T(8,128)(2,1)S(1)}, u32[]{:S(2)}, u32[]{:S(2)}) collective-permute-start(bf16[128,1024]{1,0:T(8,128)(2,1)S(1)} %get-tuple-element.444), channel_id=1, source_target_pairs={{0,4},{2,6},{4,0},{6,2},{8,12},{10,14},{12,8},{14,10},{16,20},{18,... | collective-permute-start | bytes 786440 | tf_op jit(solution)/shard_map/ppermute | solution.py:113
  294.7 13.9 %collective-permute-start.24 = (bf16[128,1024]{1,0:T(8,128)(2,1)S(1)}, bf16[128,1024]{1,0:T(8,128)(2,1)}, u32[]{:S(2)}, u32[]{:S(2)}) collective-permute-start(bf16[128,1024]{1,0:T(8,128)(2,1)S(1)} %get-tuple-element.446), channel_id=1, source_target_pairs={{0,2},{2,0},{4,6},{6,4},{8,10},{10,8},{12,14},{14,12},{16,18},{18,... | collective-permute-start | bytes 786440 | tf_op jit(solution)/shard_map/ppermute | solution.py:113
  311.1 36.6 %collective-permute-start.28 = (bf16[2,256,1024]{2,1,0:T(8,128)(2,1)}, bf16[2,256,1024]{2,1,0:T(8,128)(2,1)}, u32[]{:S(2)}, u32[]{:S(2)}) collective-permute-start(bf16[2,256,1024]{2,1,0:T(8,128)(2,1)} %pad_maximum_fusion.13), channel_id=1, source_target_pairs={{0,8},{2,10},{4,12},{6,14},{8,0},{10,2},{12,4},{14,6},{16,24},{18,... | collective-permute-start | bytes 3145736 | tf_op jit(solution)/shard_map/ppermute | solution.py:113
  344.7 36.6 %collective-permute-start.29 = (bf16[384,1024]{1,0:T(8,128)(2,1)}, bf16[384,1024]{1,0:T(8,128)(2,1)S(1)}, u32[]{:S(2)}, u32[]{:S(2)}) collective-permute-start(bf16[384,1024]{1,0:T(8,128)(2,1)} %get-tuple-element.731), channel_id=1, source_target_pairs={{0,2},{2,0},{4,6},{6,4},{8,10},{10,8},{12,14},{14,12},{16,18},{18,... | collective-permute-start | bytes 2359304 | tf_op jit(solution)/shard_map/ppermute | solution.py:113
  346.1 35.2 %collective-permute-start.30 = (bf16[384,1024]{1,0:T(8,128)(2,1)}, bf16[384,1024]{1,0:T(8,128)(2,1)S(1)}, u32[]{:S(2)}, u32[]{:S(2)}) collective-permute-start(bf16[384,1024]{1,0:T(8,128)(2,1)} %get-tuple-element.696), channel_id=1, source_target_pairs={{0,4},{2,6},{4,0},{6,2},{8,12},{10,14},{12,8},{14,10},{16,20},{18,... | collective-permute-start | bytes 2359304 | tf_op jit(solution)/shard_map/ppermute | solution.py:113
  349.6 46.2 %collective-permute-start.31 = (bf16[2,128,1024]{2,1,0:T(8,128)(2,1)S(1)}, bf16[2,128,1024]{2,1,0:T(8,128)(2,1)S(1)}, u32[]{:S(2)}, u32[]{:S(2)}) collective-permute-start(bf16[2,128,1024]{2,1,0:T(8,128)(2,1)S(1)} %pad_maximum_fusion.30), channel_id=1, source_target_pairs={{0,16},{2,18},{4,20},{6,22},{8,24},{10,26},{12,28},{14,30},{16,0},... | collective-permute-start | bytes 1572872 | tf_op jit(solution)/shard_map/ppermute | solution.py:113
  350.1 89.7 %collective-permute-start.35 = (bf16[512,1024]{1,0:T(8,128)(2,1)S(1)}, bf16[512,1024]{1,0:T(8,128)(2,1)}, u32[]{:S(2)}, u32[]{:S(2)}) collective-permute-start(bf16[512,1024]{1,0:T(8,128)(2,1)S(1)} %maximum_select_fusion.14), channel_id=1, source_target_pairs={{0,2},{2,0},{4,6},{6,4},{8,10},{10,8},{12,14},{14,12},{16,18},{18,... | collective-permute-start | bytes 3145736 | tf_op jit(solution)/shard_map/ppermute | solution.py:113
  380.8 58.9 %collective-permute-start.36 = (bf16[512,1024]{1,0:T(8,128)(2,1)}, bf16[512,1024]{1,0:T(8,128)(2,1)}, u32[]{:S(2)}, u32[]{:S(2)}) collective-permute-start(bf16[512,1024]{1,0:T(8,128)(2,1)} %maximum_select_fusion.15), channel_id=1, source_target_pairs={{0,4},{2,6},{4,0},{6,2},{8,12},{10,14},{12,8},{14,10},{16,20},{18,... | collective-permute-start | bytes 3145736 | tf_op jit(solution)/shard_map/ppermute | solution.py:113
  396.8 38.7 %collective-permute-start.37 = (bf16[128,1024]{1,0:T(8,128)(2,1)}, bf16[128,1024]{1,0:T(8,128)(2,1)}, u32[]{:S(2)}, u32[]{:S(2)}) collective-permute-start(bf16[128,1024]{1,0:T(8,128)(2,1)} %get-tuple-element.514), channel_id=1, source_target_pairs={{0,4},{2,6},{4,0},{6,2},{8,12},{10,14},{12,8},{14,10},{16,20},{18,... | collective-permute-start | bytes 786440 | tf_op jit(solution)/shard_map/ppermute | solution.py:113
  412.0 19.9 %collective-permute-start.32 = (bf16[2,192,1024]{2,1,0:T(8,128)(2,1)}, bf16[2,192,1024]{2,1,0:T(8,128)(2,1)}, u32[]{:S(2)}, u32[]{:S(2)}) collective-permute-start(bf16[2,192,1024]{2,1,0:T(8,128)(2,1)} %pad_maximum_fusion.26), channel_id=1, source_target_pairs={{0,8},{2,10},{4,12},{6,14},{8,0},{10,2},{12,4},{14,6},{16,24},{18,... | collective-permute-start | bytes 2359304 | tf_op jit(solution)/shard_map/ppermute | solution.py:113
  412.5 23.0 %collective-permute-start.38 = (bf16[128,1024]{1,0:T(8,128)(2,1)S(1)}, bf16[128,1024]{1,0:T(8,128)(2,1)}, u32[]{:S(2)}, u32[]{:S(2)}) collective-permute-start(bf16[128,1024]{1,0:T(8,128)(2,1)S(1)} %get-tuple-element.516), channel_id=1, source_target_pairs={{0,2},{2,0},{4,6},{6,4},{8,10},{10,8},{12,14},{14,12},{16,18},{18,... | collective-permute-start | bytes 786440 | tf_op jit(solution)/shard_map/ppermute | solution.py:113
  413.9 44.6 %all-to-all-start.3 = ((bf16[2,1024,1024]{2,1,0:T(8,128)(2,1)}), bf16[2,1024,1024]{2,1,0:T(8,128)(2,1)}, u32[]{:S(2)}, u32[]{:S(2)}) async-start(bf16[2,1024,1024]{2,1,0:T(8,128)(2,1)} %get-tuple-element.525.p), calls=%async_computation.3 | async-start | bytes 8388608 | tf_op jit(solution)/shard_map/all_to_all | solution.py:73
  439.3 70.9 %collective-permute-start.44 = (bf16[2,256,1024]{2,1,0:T(8,128)(2,1)}, bf16[2,256,1024]{2,1,0:T(8,128)(2,1)}, u32[]{:S(2)}, u32[]{:S(2)}) collective-permute-start(bf16[2,256,1024]{2,1,0:T(8,128)(2,1)} %pad_maximum_fusion.21), channel_id=1, source_target_pairs={{0,8},{2,10},{4,12},{6,14},{8,0},{10,2},{12,4},{14,6},{16,24},{18,... | collective-permute-start | bytes 3145736 | tf_op jit(solution)/shard_map/ppermute | solution.py:113
  439.9 15.9 %collective-permute-start.34 = (bf16[96,1024]{1,0:T(8,128)(2,1)S(1)}, bf16[96,1024]{1,0:T(8,128)(2,1)S(1)}, u32[]{:S(2)}, u32[]{:S(2)}) collective-permute-start(bf16[96,1024]{1,0:T(8,128)(2,1)S(1)} %get-tuple-element.790), channel_id=1, source_target_pairs={{0,2},{2,0},{4,6},{6,4},{8,10},{10,8},{12,14},{14,12},{16,18},{18,... | collective-permute-start | bytes 589832 | tf_op jit(solution)/shard_map/ppermute | solution.py:113
  441.4 14.3 %collective-permute-start.33 = (bf16[96,1024]{1,0:T(8,128)(2,1)S(1)}, bf16[96,1024]{1,0:T(8,128)(2,1)S(1)}, u32[]{:S(2)}, u32[]{:S(2)}) collective-permute-start(bf16[96,1024]{1,0:T(8,128)(2,1)S(1)} %get-tuple-element.792), channel_id=1, source_target_pairs={{0,4},{2,6},{4,0},{6,2},{8,12},{10,14},{12,8},{14,10},{16,20},{18,... | collective-permute-start | bytes 589832 | tf_op jit(solution)/shard_map/ppermute | solution.py:113
  443.2 34.7 %collective-permute-start.41 = (bf16[640,1024]{1,0:T(8,128)(2,1)}, bf16[640,1024]{1,0:T(8,128)(2,1)}, u32[]{:S(2)}, u32[]{:S(2)}) collective-permute-start(bf16[640,1024]{1,0:T(8,128)(2,1)} %get-tuple-element.684), channel_id=1, source_target_pairs={{0,4},{2,6},{4,0},{6,2},{8,12},{10,14},{12,8},{14,10},{16,20},{18,... | collective-permute-start | bytes 3932168 | tf_op jit(solution)/shard_map/ppermute | solution.py:113
  444.8 33.7 %collective-permute-start.40 = (bf16[640,1024]{1,0:T(8,128)(2,1)}, bf16[640,1024]{1,0:T(8,128)(2,1)}, u32[]{:S(2)}, u32[]{:S(2)}) collective-permute-start(bf16[640,1024]{1,0:T(8,128)(2,1)} %get-tuple-element.686), channel_id=1, source_target_pairs={{0,2},{2,0},{4,6},{6,4},{8,10},{10,8},{12,14},{14,12},{16,18},{18,... | collective-permute-start | bytes 3932168 | tf_op jit(solution)/shard_map/ppermute | solution.py:113
  455.9 29.2 %collective-permute-start.39 = (bf16[2,96,1024]{2,1,0:T(8,128)(2,1)S(1)}, bf16[2,96,1024]{2,1,0:T(8,128)(2,1)}, u32[]{:S(2)}, u32[]{:S(2)}) collective-permute-start(bf16[2,96,1024]{2,1,0:T(8,128)(2,1)S(1)} %pad_maximum_fusion.33), channel_id=1, source_target_pairs={{0,16},{2,18},{4,20},{6,22},{8,24},{10,26},{12,28},{14,30},{16,0},... | collective-permute-start | bytes 1179656 | tf_op jit(solution)/shard_map/ppermute | solution.py:113
  476.3 27.1 %collective-permute-start.42 = (bf16[512,1024]{1,0:T(8,128)(2,1)}, bf16[512,1024]{1,0:T(8,128)(2,1)S(1)}, u32[]{:S(2)}, u32[]{:S(2)}) collective-permute-start(bf16[512,1024]{1,0:T(8,128)(2,1)} %get-tuple-element.546), channel_id=1, source_target_pairs={{0,2},{2,0},{4,6},{6,4},{8,10},{10,8},{12,14},{14,12},{16,18},{18,... | collective-permute-start | bytes 3145736 | tf_op jit(solution)/shard_map/ppermute | solution.py:113
  477.9 25.5 %collective-permute-start.43 = (bf16[512,1024]{1,0:T(8,128)(2,1)}, bf16[512,1024]{1,0:T(8,128)(2,1)S(1)}, u32[]{:S(2)}, u32[]{:S(2)}) collective-permute-start(bf16[512,1024]{1,0:T(8,128)(2,1)} %get-tuple-element.547), channel_id=1, source_target_pairs={{0,4},{2,6},{4,0},{6,2},{8,12},{10,14},{12,8},{14,10},{16,20},{18,... | collective-permute-start | bytes 3145736 | tf_op jit(solution)/shard_map/ppermute | solution.py:113
  483.5 53.4 %collective-permute-start.47 = (bf16[2,320,1024]{2,1,0:T(8,128)(2,1)}, bf16[2,320,1024]{2,1,0:T(8,128)(2,1)}, u32[]{:S(2)}, u32[]{:S(2)}) collective-permute-start(bf16[2,320,1024]{2,1,0:T(8,128)(2,1)} %pad_maximum_fusion.9), channel_id=1, source_target_pairs={{0,8},{2,10},{4,12},{6,14},{8,0},{10,2},{12,4},{14,6},{16,24},{18,... | collective-permute-start | bytes 3932168 | tf_op jit(solution)/shard_map/ppermute | solution.py:113
  506.5 27.6 %collective-permute-start.50 = (bf16[2,256,1024]{2,1,0:T(8,128)(2,1)}, bf16[2,256,1024]{2,1,0:T(8,128)(2,1)}, u32[]{:S(2)}, u32[]{:S(2)}) collective-permute-start(bf16[2,256,1024]{2,1,0:T(8,128)(2,1)} %pad_maximum_fusion.22), channel_id=1, source_target_pairs={{0,8},{2,10},{4,12},{6,14},{8,0},{10,2},{12,4},{14,6},{16,24},{18,... | collective-permute-start | bytes 3145736 | tf_op jit(solution)/shard_map/ppermute | solution.py:113
  512.4 26.8 %collective-permute-start.51 = (bf16[96,1024]{1,0:T(8,128)(2,1)}, bf16[96,1024]{1,0:T(8,128)(2,1)}, u32[]{:S(2)}, u32[]{:S(2)}) collective-permute-start(bf16[96,1024]{1,0:T(8,128)(2,1)} %get-tuple-element.569), channel_id=1, source_target_pairs={{0,4},{2,6},{4,0},{6,2},{8,12},{10,14},{12,8},{14,10},{16,20},{18,... | collective-permute-start | bytes 589832 | tf_op jit(solution)/shard_map/ppermute | solution.py:113
  523.8 86.2 %collective-permute-start.57 = (bf16[512,1024]{1,0:T(8,128)(2,1)}, bf16[512,1024]{1,0:T(8,128)(2,1)}, u32[]{:S(2)}, u32[]{:S(2)}) collective-permute-start(bf16[512,1024]{1,0:T(8,128)(2,1)} %get-tuple-element.555), channel_id=1, source_target_pairs={{0,2},{2,0},{4,6},{6,4},{8,10},{10,8},{12,14},{14,12},{16,18},{18,... | collective-permute-start | bytes 3145736 | tf_op jit(solution)/shard_map/ppermute | solution.py:113
  524.3 30.1 %collective-permute-start.52 = (bf16[96,1024]{1,0:T(8,128)(2,1)}, bf16[96,1024]{1,0:T(8,128)(2,1)}, u32[]{:S(2)}, u32[]{:S(2)}) collective-permute-start(bf16[96,1024]{1,0:T(8,128)(2,1)} %get-tuple-element.571), channel_id=1, source_target_pairs={{0,2},{2,0},{4,6},{6,4},{8,10},{10,8},{12,14},{14,12},{16,18},{18,... | collective-permute-start | bytes 589832 | tf_op jit(solution)/shard_map/ppermute | solution.py:113
  525.9 76.2 %all-to-all-start.5 = ((bf16[2,1024,1024]{2,1,0:T(8,128)(2,1)}), bf16[2,1024,1024]{2,1,0:T(8,128)(2,1)}, u32[]{:S(2)}, u32[]{:S(2)}) async-start(bf16[2,1024,1024]{2,1,0:T(8,128)(2,1)} %get-tuple-element.588.p), calls=%async_computation.5 | async-start | bytes 8388608 | tf_op jit(solution)/shard_map/all_to_all | solution.py:73
  534.1 58.4 %collective-permute-start.46 = (bf16[512,1024]{1,0:T(8,128)(2,1)S(1)}, bf16[512,1024]{1,0:T(8,128)(2,1)S(1)}, u32[]{:S(2)}, u32[]{:S(2)}) collective-permute-start(bf16[512,1024]{1,0:T(8,128)(2,1)S(1)} %maximum_select_fusion.17), channel_id=1, source_target_pairs={{0,4},{2,6},{4,0},{6,2},{8,12},{10,14},{12,8},{14,10},{16,20},{18,... | collective-permute-start | bytes 3145736 | tf_op jit(solution)/shard_map/ppermute | solution.py:113
  536.9 56.0 %collective-permute-start.45 = (bf16[512,1024]{1,0:T(8,128)(2,1)S(1)}, bf16[512,1024]{1,0:T(8,128)(2,1)S(1)}, u32[]{:S(2)}, u32[]{:S(2)}) collective-permute-start(bf16[512,1024]{1,0:T(8,128)(2,1)S(1)} %maximum_select_fusion.16), channel_id=1, source_target_pairs={{0,2},{2,0},{4,6},{6,4},{8,10},{10,8},{12,14},{14,12},{16,18},{18,... | collective-permute-start | bytes 3145736 | tf_op jit(solution)/shard_map/ppermute | solution.py:113
  558.4 21.3 %collective-permute-start.54 = (bf16[128,1024]{1,0:T(8,128)(2,1)S(1)}, bf16[128,1024]{1,0:T(8,128)(2,1)S(1)}, u32[]{:S(2)}, u32[]{:S(2)}) collective-permute-start(bf16[128,1024]{1,0:T(8,128)(2,1)S(1)} %get-tuple-element.772), channel_id=1, source_target_pairs={{0,2},{2,0},{4,6},{6,4},{8,10},{10,8},{12,14},{14,12},{16,18},{18,... | collective-permute-start | bytes 786440 | tf_op jit(solution)/shard_map/ppermute | solution.py:113
  559.2 21.0 %collective-permute-start.53 = (bf16[128,1024]{1,0:T(8,128)(2,1)S(1)}, bf16[128,1024]{1,0:T(8,128)(2,1)S(1)}, u32[]{:S(2)}, u32[]{:S(2)}) collective-permute-start(bf16[128,1024]{1,0:T(8,128)(2,1)S(1)} %get-tuple-element.774), channel_id=1, source_target_pairs={{0,4},{2,6},{4,0},{6,2},{8,12},{10,14},{12,8},{14,10},{16,20},{18,... | collective-permute-start | bytes 786440 | tf_op jit(solution)/shard_map/ppermute | solution.py:113
  586.7 23.3 %collective-permute-start.58 = (bf16[512,1024]{1,0:T(8,128)(2,1)}, bf16[512,1024]{1,0:T(8,128)(2,1)}, u32[]{:S(2)}, u32[]{:S(2)}) collective-permute-start(bf16[512,1024]{1,0:T(8,128)(2,1)} %get-tuple-element.606), channel_id=1, source_target_pairs={{0,4},{2,6},{4,0},{6,2},{8,12},{10,14},{12,8},{14,10},{16,20},{18,... | collective-permute-start | bytes 3145736 | tf_op jit(solution)/shard_map/ppermute | solution.py:113
  590.7 40.6 %collective-permute-start.64 = (bf16[2,192,1024]{2,1,0:T(8,128)(2,1)}, bf16[2,192,1024]{2,1,0:T(8,128)(2,1)}, u32[]{:S(2)}, u32[]{:S(2)}) collective-permute-start(bf16[2,192,1024]{2,1,0:T(8,128)(2,1)} %pad_maximum_fusion.27), channel_id=1, source_target_pairs={{0,8},{2,10},{4,12},{6,14},{8,0},{10,2},{12,4},{14,6},{16,24},{18,... | collective-permute-start | bytes 2359304 | tf_op jit(solution)/shard_map/ppermute | solution.py:113
  592.5 33.9 %collective-permute-start.56 = (bf16[2,128,1024]{2,1,0:T(8,128)(2,1)S(1)}, bf16[2,128,1024]{2,1,0:T(8,128)(2,1)}, u32[]{:S(2)}, u32[]{:S(2)}) collective-permute-start(bf16[2,128,1024]{2,1,0:T(8,128)(2,1)S(1)} %pad_maximum_fusion.31), channel_id=1, source_target_pairs={{0,16},{2,18},{4,20},{6,22},{8,24},{10,26},{12,28},{14,30},{16,0},... | collective-permute-start | bytes 1572872 | tf_op jit(solution)/shard_map/ppermute | solution.py:113
  592.9 67.6 %collective-permute-start.62 = (bf16[2,160,1024]{2,1,0:T(8,128)(2,1)S(1)}, bf16[2,160,1024]{2,1,0:T(8,128)(2,1)}, u32[]{:S(2)}, u32[]{:S(2)}) collective-permute-start(bf16[2,160,1024]{2,1,0:T(8,128)(2,1)S(1)} %pad_maximum_fusion.28), channel_id=1, source_target_pairs={{0,16},{2,18},{4,20},{6,22},{8,24},{10,26},{12,28},{14,30},{16,0},... | collective-permute-start | bytes 1966088 | tf_op jit(solution)/shard_map/ppermute | solution.py:113
  612.2 25.4 %collective-permute-start.55 = (f32[12,512]{1,0:T(8,128)S(1)}, f32[12,512]{1,0:T(8,128)S(1)}, u32[]{:S(2)}, u32[]{:S(2)}) collective-permute-start(f32[12,512]{1,0:T(8,128)S(1)} %concatenate.621), channel_id=1, source_target_pairs={{0,2},{2,0},{4,6},{6,4},{8,10},{10,8},{12,14},{14,12},{16,18},{18,... | collective-permute-start | bytes 73736 | tf_op jit(solution)/shard_map/ppermute | solution.py:113
  631.2 28.4 %collective-permute-start.63 = (bf16[2,256,1024]{2,1,0:T(8,128)(2,1)S(1)}, bf16[2,256,1024]{2,1,0:T(8,128)(2,1)S(1)}, u32[]{:S(2)}, u32[]{:S(2)}) collective-permute-start(bf16[2,256,1024]{2,1,0:T(8,128)(2,1)S(1)} %pad_maximum_fusion.24), channel_id=1, source_target_pairs={{0,8},{2,10},{4,12},{6,14},{8,0},{10,2},{12,4},{14,6},{16,24},{18,... | collective-permute-start | bytes 3145736 | tf_op jit(solution)/shard_map/ppermute | solution.py:113
  637.5 42.5 %collective-permute-start.66 = (bf16[2,256,1024]{2,1,0:T(8,128)(2,1)S(1)}, bf16[2,256,1024]{2,1,0:T(8,128)(2,1)S(1)}, u32[]{:S(2)}, u32[]{:S(2)}) collective-permute-start(bf16[2,256,1024]{2,1,0:T(8,128)(2,1)S(1)} %pad_maximum_fusion.23), channel_id=1, source_target_pairs={{0,8},{2,10},{4,12},{6,14},{8,0},{10,2},{12,4},{14,6},{16,24},{18,... | collective-permute-start | bytes 3145736 | tf_op jit(solution)/shard_map/ppermute | solution.py:113
  637.6 25.9 %collective-permute-start.61 = (f32[12,512]{1,0:T(8,128)S(1)}, f32[12,512]{1,0:T(8,128)S(1)}, u32[]{:S(2)}, u32[]{:S(2)}) collective-permute-start(f32[12,512]{1,0:T(8,128)S(1)} %add.402), channel_id=1, source_target_pairs={{0,4},{2,6},{4,0},{6,2},{8,12},{10,14},{12,8},{14,10},{16,20},{18,... | collective-permute-start | bytes 73736 | tf_op jit(solution)/shard_map/ppermute | solution.py:113
  638.0 27.3 %collective-permute-start.70 = (bf16[384,1024]{1,0:T(8,128)(2,1)S(1)}, bf16[384,1024]{1,0:T(8,128)(2,1)S(1)}, u32[]{:S(2)}, u32[]{:S(2)}) collective-permute-start(bf16[384,1024]{1,0:T(8,128)(2,1)S(1)} %maximum_select_fusion.23), channel_id=1, source_target_pairs={{0,4},{2,6},{4,0},{6,2},{8,12},{10,14},{12,8},{14,10},{16,20},{18,... | collective-permute-start | bytes 2359304 | tf_op jit(solution)/shard_map/ppermute | solution.py:113
  661.9 20.7 %collective-permute-start.75 = (bf16[160,1024]{1,0:T(8,128)(2,1)S(1)}, bf16[160,1024]{1,0:T(8,128)(2,1)S(1)}, u32[]{:S(2)}, u32[]{:S(2)}) collective-permute-start(bf16[160,1024]{1,0:T(8,128)(2,1)S(1)} %get-tuple-element.644), channel_id=1, source_target_pairs={{0,4},{2,6},{4,0},{6,2},{8,12},{10,14},{12,8},{14,10},{16,20},{18,... | collective-permute-start | bytes 983048 | tf_op jit(solution)/shard_map/ppermute | solution.py:113
  663.7 12.9 %collective-permute-start.68 = (bf16[128,1024]{1,0:T(8,128)(2,1)S(1)}, bf16[128,1024]{1,0:T(8,128)(2,1)S(1)}, u32[]{:S(2)}, u32[]{:S(2)}) collective-permute-start(bf16[128,1024]{1,0:T(8,128)(2,1)S(1)} %get-tuple-element.766), channel_id=1, source_target_pairs={{0,2},{2,0},{4,6},{6,4},{8,10},{10,8},{12,14},{14,12},{16,18},{18,... | collective-permute-start | bytes 786440 | tf_op jit(solution)/shard_map/ppermute | solution.py:113
  677.6 15.3 %collective-permute-start.74 = (bf16[2,128,1024]{2,1,0:T(8,128)(2,1)S(1)}, bf16[2,128,1024]{2,1,0:T(8,128)(2,1)S(1)}, u32[]{:S(2)}, u32[]{:S(2)}) collective-permute-start(bf16[2,128,1024]{2,1,0:T(8,128)(2,1)S(1)} %pad_maximum_fusion.32), channel_id=1, source_target_pairs={{0,16},{2,18},{4,20},{6,22},{8,24},{10,26},{12,28},{14,30},{16,0},... | collective-permute-start | bytes 1572872 | tf_op jit(solution)/shard_map/ppermute | solution.py:113
  680.5 22.9 %collective-permute-start.72 = (bf16[512,1024]{1,0:T(8,128)(2,1)S(1)}, bf16[512,1024]{1,0:T(8,128)(2,1)S(1)}, u32[]{:S(2)}, u32[]{:S(2)}) collective-permute-start(bf16[512,1024]{1,0:T(8,128)(2,1)S(1)} %maximum_select_fusion.18), channel_id=1, source_target_pairs={{0,2},{2,0},{4,6},{6,4},{8,10},{10,8},{12,14},{14,12},{16,18},{18,... | collective-permute-start | bytes 3145736 | tf_op jit(solution)/shard_map/ppermute | solution.py:113
  680.7 29.2 %collective-permute-start.71 = (f32[12,512]{1,0:T(8,128)S(1)}, f32[12,512]{1,0:T(8,128)S(1)}, u32[]{:S(2)}, u32[]{:S(2)}) collective-permute-start(f32[12,512]{1,0:T(8,128)S(1)} %add.410), channel_id=1, source_target_pairs={{0,16},{2,18},{4,20},{6,22},{8,24},{10,26},{12,28},{14,30},{16,0},... | collective-permute-start | bytes 73736 | tf_op jit(solution)/shard_map/ppermute | solution.py:113
  687.8 14.9 %collective-permute-start.73 = (bf16[512,1024]{1,0:T(8,128)(2,1)S(1)}, bf16[512,1024]{1,0:T(8,128)(2,1)S(1)}, u32[]{:S(2)}, u32[]{:S(2)}) collective-permute-start(bf16[512,1024]{1,0:T(8,128)(2,1)S(1)} %maximum_select_fusion.19), channel_id=1, source_target_pairs={{0,4},{2,6},{4,0},{6,2},{8,12},{10,14},{12,8},{14,10},{16,20},{18,... | collective-permute-start | bytes 3145736 | tf_op jit(solution)/shard_map/ppermute | solution.py:113
  690.2 31.9 %collective-permute-start.80 = (bf16[2,320,1024]{2,1,0:T(8,128)(2,1)S(1)}, bf16[2,320,1024]{2,1,0:T(8,128)(2,1)S(1)}, u32[]{:S(2)}, u32[]{:S(2)}) collective-permute-start(bf16[2,320,1024]{2,1,0:T(8,128)(2,1)S(1)} %pad_maximum_fusion.10), channel_id=1, source_target_pairs={{0,8},{2,10},{4,12},{6,14},{8,0},{10,2},{12,4},{14,6},{16,24},{18,... | collective-permute-start | bytes 3932168 | tf_op jit(solution)/shard_map/ppermute | solution.py:113
  693.1 16.8 %collective-permute-start.77 = (bf16[128,1024]{1,0:T(8,128)(2,1)S(1)}, bf16[128,1024]{1,0:T(8,128)(2,1)S(1)}, u32[]{:S(2)}, u32[]{:S(2)}) collective-permute-start(bf16[128,1024]{1,0:T(8,128)(2,1)S(1)} %get-tuple-element.656), channel_id=1, source_target_pairs={{0,4},{2,6},{4,0},{6,2},{8,12},{10,14},{12,8},{14,10},{16,20},{18,... | collective-permute-start | bytes 786440 | tf_op jit(solution)/shard_map/ppermute | solution.py:113
  710.3 25.8 %collective-permute-start.79 = (bf16[2,256,1024]{2,1,0:T(8,128)(2,1)S(1)}, bf16[2,256,1024]{2,1,0:T(8,128)(2,1)S(1)}, u32[]{:S(2)}, u32[]{:S(2)}) collective-permute-start(bf16[2,256,1024]{2,1,0:T(8,128)(2,1)S(1)} %pad_maximum_fusion.25), channel_id=1, source_target_pairs={{0,8},{2,10},{4,12},{6,14},{8,0},{10,2},{12,4},{14,6},{16,24},{18,... | collective-permute-start | bytes 3145736 | tf_op jit(solution)/shard_map/ppermute | solution.py:113
  723.1 24.9 %collective-permute-start.84 = (bf16[640,1024]{1,0:T(8,128)(2,1)S(1)}, bf16[640,1024]{1,0:T(8,128)(2,1)S(1)}, u32[]{:S(2)}, u32[]{:S(2)}) collective-permute-start(bf16[640,1024]{1,0:T(8,128)(2,1)S(1)} %maximum_select_fusion.13), channel_id=1, source_target_pairs={{0,4},{2,6},{4,0},{6,2},{8,12},{10,14},{12,8},{14,10},{16,20},{18,... | collective-permute-start | bytes 3932168 | tf_op jit(solution)/shard_map/ppermute | solution.py:113
  723.9 24.1 %collective-permute-start.83 = (bf16[640,1024]{1,0:T(8,128)(2,1)S(1)}, bf16[640,1024]{1,0:T(8,128)(2,1)S(1)}, u32[]{:S(2)}, u32[]{:S(2)}) collective-permute-start(bf16[640,1024]{1,0:T(8,128)(2,1)S(1)} %maximum_select_fusion.12), channel_id=1, source_target_pairs={{0,2},{2,0},{4,6},{6,4},{8,10},{10,8},{12,14},{14,12},{16,18},{18,... | collective-permute-start | bytes 3932168 | tf_op jit(solution)/shard_map/ppermute | solution.py:113
  736.7 26.6 %collective-permute-start.82 = (bf16[512,1024]{1,0:T(8,128)(2,1)S(1)}, bf16[512,1024]{1,0:T(8,128)(2,1)S(1)}, u32[]{:S(2)}, u32[]{:S(2)}) collective-permute-start(bf16[512,1024]{1,0:T(8,128)(2,1)S(1)} %maximum_select_fusion.21), channel_id=1, source_target_pairs={{0,4},{2,6},{4,0},{6,2},{8,12},{10,14},{12,8},{14,10},{16,20},{18,... | collective-permute-start | bytes 3145736 | tf_op jit(solution)/shard_map/ppermute | solution.py:113
  739.4 24.8 %collective-permute-start.81 = (bf16[512,1024]{1,0:T(8,128)(2,1)S(1)}, bf16[512,1024]{1,0:T(8,128)(2,1)S(1)}, u32[]{:S(2)}, u32[]{:S(2)}) collective-permute-start(bf16[512,1024]{1,0:T(8,128)(2,1)S(1)} %maximum_select_fusion.20), channel_id=1, source_target_pairs={{0,2},{2,0},{4,6},{6,4},{8,10},{10,8},{12,14},{14,12},{16,18},{18,... | collective-permute-start | bytes 3145736 | tf_op jit(solution)/shard_map/ppermute | solution.py:113
  (85 other events, 642.5 us)
